TPU v7x, 32 devices: a whole 2x2x4 slice. The times are simulated.
32 devices in a mesh: group: 2 (over x), dp: 16 (over z, y, core).
Axes of the slice: x: 2, y: 2, z: 4, core: 2. Of those that a mesh axis runs over, the one named last changes fastest.
Arguments:
- states: bfloat16 [8192, 8192], P(('group', 'dp')), parts along dimension 0, may hold values from -6 to 6
- queries: bfloat16 [8192, 4096], P(('group', 'dp')), parts along dimension 0, may hold values from -160 to 160
- kv_weight: bfloat16 [8192, 1024], P('dp'), may hold values from -0.0625 to 0.0625
- kv_bias: float32 [1024], replicated, may hold values from -3 to 3
- lengths: int32 [32], P(('group', 'dp')), parts along dimension 0, may hold values from 2 to 32, as said below
- bounds: int32 [32, 2], P(('group', 'dp')), parts along dimension 0, may hold values from 1 to 255, as said below
- balance: int32 [32, 32], P(('group', 'dp')), parts along dimension 0, may hold values from 0 to 15, as said below
Outputs:
- context: bfloat16 [8192, 4096], P(('group', 'dp')), parts along dimension 0
- work_rows: bfloat16 [6144, 1024], P(('group', 'dp')), parts along dimension 0
There are 2 independent parts, one for each index of `group`. A program takes and returns all parts, laid end to end along the dimension named above; an argument that names none is the same for every part. Nothing has to cross between parts.
Inputs may be any that keep to these rules, and one draw needn't show every extreme that they name: `lengths`: half of the replicas, drawn from the seed, hold 24 or more spans, the others at most 16; one replica holds 32. balance[r, j] = r for j < 24 and for slots past the pair; the slots from 24 up to the pair's end go to other replicas with fewer than 24 spans; a replica sends at most one span to any other, and no replica computes more than 24 spans, one exactly 24. 1 <= bounds[r, 0] < bounds[r, 1] < lengths[r] * 8.
All inputs are finite; a program needn't handle non-finite values.
Results may differ from a plain program's by a relative error of at most 0.012.
The roundings to bfloat16 on the way count: a program that leaves them out, or rounds other values in their place, can miss the bound.
Values may be sent and summed in bfloat16 or wider, within the bound.
No kernel may reach another device: no remote copies, remote signals or barrier semaphores. Data moves between devices by JAX's collectives and lax.ppermute only.
A program may use at most 128 MiB of HBM per device.

v0:
```python
import math

import jax
import jax.numpy as jnp
from jax import lax
from jax.sharding import PartitionSpec as P

HEAD = 128
SPAN = 8
HOME = 32
WORK = 24


def pair_layout(all_lengths, all_plans):
    replicas = all_lengths.shape[0]
    slot_ids = jnp.arange(HOME, dtype=jnp.int32)
    replica_ids = jnp.arange(replicas, dtype=jnp.int32)
    live_slot = slot_ids[None, :] < all_lengths[:, None]
    moved_slot = live_slot & (all_plans != replica_ids[:, None])
    kept_count = jnp.sum((live_slot & jnp.logical_not(moved_slot)).astype(jnp.int32), axis=1)
    onehot = (
        (all_plans[:, :, None] == replica_ids[None, None, :]) & moved_slot[:, :, None]
    ).astype(jnp.int32)
    send_count = jnp.sum(onehot, axis=1)
    before = jnp.cumsum(send_count, axis=0) - send_count
    rank_moved = jnp.sum(onehot * (kept_count[None, None, :] + before[:, None, :]), axis=2)
    work_rank = jnp.where(moved_slot, rank_moved, slot_ids[None, :])
    return (live_slot, moved_slot, work_rank)


def rotate(key_rows, position):
    half_head = key_rows.shape[-1] // 2
    frequency = jnp.exp(
        jnp.arange(half_head, dtype=jnp.float32) * (-2.0 * math.log(1000000.0) / key_rows.shape[-1])
    )
    angles = position.astype(jnp.float32)[:, None] * frequency[None, :]
    cosines = jnp.cos(angles)[:, None, :]
    sines = jnp.sin(angles)[:, None, :]
    first = key_rows[..., :half_head]
    second = key_rows[..., half_head:]
    return jnp.concatenate(
        [first * cosines - second * sines, second * cosines + first * sines], axis=-1
    )


def attend(query_rows, kv_rows, length, chosen_start, rejected_start):
    row_count = query_rows.shape[0]
    kv_heads = kv_rows.shape[1] // (2 * HEAD)
    group_size = query_rows.shape[1] // (kv_heads * HEAD)
    token_ids = jnp.arange(row_count, dtype=jnp.int32)
    segment = (token_ids >= chosen_start).astype(jnp.int32) + (token_ids >= rejected_start).astype(
        jnp.int32
    )
    position = jnp.where(
        token_ids >= rejected_start, token_ids - (rejected_start - chosen_start), token_ids
    )
    is_live = token_ids < length * SPAN
    key_rows = kv_rows[:, : kv_heads * HEAD].astype(jnp.float32).reshape(row_count, kv_heads, HEAD)
    key_rows = rotate(key_rows, position).astype(jnp.bfloat16)
    value_rows = kv_rows[:, kv_heads * HEAD :].reshape(row_count, kv_heads, HEAD)
    query_heads = query_rows.reshape(row_count, kv_heads, group_size, HEAD)
    scores = jnp.einsum(
        "tkgh,skh->kgts", query_heads, key_rows, preferred_element_type=jnp.float32
    ) * HEAD ** (-0.5)
    allowed = (
        (token_ids[None, :] <= token_ids[:, None])
        & is_live[None, :]
        & ((segment[None, :] == segment[:, None]) | (segment[None, :] == 0))
    )
    allowed = allowed | (token_ids[None, :] == token_ids[:, None])
    scores = jnp.where(allowed[None, None], scores, -1e30)
    row_max = jnp.max(scores, axis=-1, keepdims=True)
    weights = jnp.exp(scores - row_max)
    weights = (weights / jnp.sum(weights, axis=-1, keepdims=True)).astype(jnp.bfloat16)
    mixed = jnp.einsum("kgts,skh->tkgh", weights, value_rows, preferred_element_type=jnp.float32)
    mixed = mixed.reshape(row_count, -1)
    return jnp.where(is_live[:, None], mixed, 0.0).astype(jnp.bfloat16)


def select_spans(span_pool, source, valid):
    picked = jnp.take(span_pool, source, axis=0)
    return jnp.where(valid[:, None, None], picked, jnp.zeros((), span_pool.dtype))


def project(row_block, kv_weight, kv_bias):
    total = jnp.dot(
        row_block,
        lax.all_gather(kv_weight, "dp", axis=0, tiled=True),
        preferred_element_type=jnp.float32,
    )
    return (total + kv_bias[None, :]).astype(jnp.bfloat16)


def per_device(states, queries, kv_weight, kv_bias, lengths, bounds, balance):
    replicas = lax.axis_size("dp")
    own_index = lax.axis_index("dp")
    all_lengths, all_plans = (
        lax.all_gather(lengths, "dp", axis=0, tiled=True),
        lax.all_gather(balance, "dp", axis=0, tiled=True),
    )
    live_slot, moved_slot, work_rank = pair_layout(all_lengths, all_plans)
    replica_ids = jnp.arange(replicas, dtype=jnp.int32)
    slot_ids = jnp.arange(HOME, dtype=jnp.int32)
    own_live = live_slot[own_index]
    own_moved = moved_slot[own_index]
    own_dest = balance[0]
    out_match = (own_dest[None, :] == replica_ids[:, None]) & own_moved[None, :]
    out_slot = jnp.sum(jnp.where(out_match, slot_ids[None, :], 0), axis=1)
    out_any = jnp.any(out_match, axis=1)
    from_sender = moved_slot & (all_plans == own_index)
    sender_any = jnp.any(from_sender, axis=1)
    sender_rank = jnp.sum(jnp.where(from_sender, work_rank, 0), axis=1)
    kept_count = jnp.sum((own_live & jnp.logical_not(own_moved)).astype(jnp.int32))
    work_ids = jnp.arange(WORK, dtype=jnp.int32)
    from_peer = sender_any[None, :] & (sender_rank[None, :] == work_ids[:, None])
    work_source = jnp.where(
        work_ids < kept_count,
        work_ids,
        HOME + jnp.sum(jnp.where(from_peer, replica_ids[None, :], 0), axis=1),
    )
    work_valid = (work_ids < kept_count) | jnp.any(from_peer, axis=1)
    home_kv = project(states, kv_weight, kv_bias).reshape(HOME, SPAN, kv_weight.shape[1])
    home_kv = jnp.where(own_live[:, None, None], home_kv, jnp.zeros((), jnp.bfloat16))
    outgoing = select_spans(home_kv, out_slot, out_any)
    arrived = lax.all_to_all(outgoing, "dp", split_axis=0, concat_axis=0, tiled=True)
    span_pool = jnp.concatenate([home_kv, arrived], axis=0)
    work_kv = select_spans(span_pool, work_source, work_valid)
    context = attend(
        queries,
        home_kv.reshape(HOME * SPAN, kv_weight.shape[1]),
        lengths[0],
        bounds[0, 0],
        bounds[0, 1],
    )
    return (context, work_kv.reshape(WORK * SPAN, kv_weight.shape[1]))


def solution(mesh):
    in_specs = (
        P(("group", "dp"), None),
        P(("group", "dp"), None),
        P("dp", None),
        P(),
        P(("group", "dp")),
        P(("group", "dp"), None),
        P(("group", "dp"), None),
    )
    out_specs = (P(("group", "dp"), None), P(("group", "dp"), None))
    return jax.shard_map(
        per_device, mesh=mesh, in_specs=in_specs, out_specs=out_specs, check_vma=False
    )
```

profile of v0, /device:TPU:0, one launch (start us, length us, event | category | flops | bytes accessed | tf_op | source)
XLA Modules:
  0.0 187.2 jit_solution(12925545002933809958)
XLA Ops:
  8.6 1.2 dynamic-slice
  10.6 13.7 %all-reduce = s32[16]{0:T(128)S(1)} all-reduce(s32[16]{0:T(128)S(1)} %dynamic-update-slice), channel_id=1, replica_groups=mesh['group'=2,'dp'=16] {'dp'}, use_global_device_ids=true, to_apply=%add | all-reduce | flops 16 | bytes 128
  24.3 18.4 %all-gather = s32[16,1,32]{2,1,0:T(1,128)S(1)} all-gather(s32[1,1,32]{2,1,0:T(1,128)} %bitcast.66), channel_id=1, replica_groups=mesh['group'=2,'dp'=16] {'dp'}, dimensions={0}, use_global_device_ids=true | all-gather | bytes 2176 | tf_op jit(solution)/shard_map/all_gather | solution.py:99
  43.7 2.1 %copy.39 = bf16[32,8,32,128]{3,2,1,0:T(8,128)(2,1)S(1)} copy(bf16[32,8,32,128]{3,1,2,0:T(8,128)(2,1)} %bitcast.60) | data formatting | bytes 4194304
  48.8 1.4 fusion.31
  51.6 1.3 broadcast_compare_fusion
  52.9 1.3 fusion.21
  54.3 0.8 select_reduce_fusion.1
  55.8 1.4 fusion.20
  57.6 0.8 fusion.14
  58.4 1.2 multiply_cosine_fusion
  59.6 80.3 %all-gather.3.cloned.1.call-done = bf16[8192,1024]{1,0:T(8,128)(2,1)} async-done(((bf16[512,1024]{1,0:T(8,128)(2,1)}), bf16[8192,1024]{1,0:T(8,128)(2,1)}) %all-gather.3.cloned.1.call-update) | async-done | bytes 16777232 | tf_op jit(solution)/shard_map/all_gather | solution.py:88
  139.9 12.2 %broadcast_select_fusion = (bf16[256,1024]{1,0:T(8,128)(2,1)S(1)}, bf16[256,1024]{1,0:T(8,128)(2,1)}) fusion(pred[256]{0:T(512)(128)(4,1)S(1)} %broadcast_in_dim.165, f32[1024]{0:T(1024)} %param.10, bf16[256,8192]{1,0:T(8,128)(2,1)} %param.7, bf16[8192,1024]{1,0:T(8,128)(2,1)} %all-gather.3.cloned.1.call-done), kind=kOutput, calls=%fused_computation.20 | convolution fusion | flops 4295753728 | bytes 22024448 | tf_op jit(solution)/shard_map/dot_general | solution.py:86
  152.4 1.1 fusion.30
  153.6 1.2 subtract_convert_fusion
  154.8 1.4 fusion.6
  156.2 2.4 %fusion.32 = (f32[4,8,256]{2,1,0:T(8,128)S(1)}, f32[4,8,256,256]{2,3,1,0:T(8,128)S(1)}) fusion(f32[4,256,256,8]{2,1,3,0:T(8,128)S(1)} %fusion.6, pred[256,256]{0,1:T(8,128)(4,1)S(1)} %copy-done.1), kind=kOutput, calls=%fused_computation.84 | output fusion | flops 12583167 | bytes 16875520 | tf_op jit(solution)/shard_map/sub | solution.py:73
  158.6 2.1 %fusion.4 = bf16[4,128,8,256]{3,1,2,0:T(8,128)(2,1)} fusion(bf16[256,4,128,1]{0,2,3,1:T(8,128)(2,1)S(1)} %bitcast.62, f32[4,8,256,256]{2,3,1,0:T(8,128)S(1)} %get-tuple-element.22, f32[4,8,256]{2,1,0:T(8,128)S(1)} %get-tuple-element.21), kind=kOutput, calls=%fused_computation.10 | convolution fusion | flops 541065216 | bytes 10780672 | tf_op jit(solution)/shard_map/kgts,skh->tkgh/dot_general | solution.py:75
  160.8 2.9 %copy.32 = bf16[256,4096]{1,0:T(8,128)(2,1)S(1)} copy(bf16[256,4096]{0,1:T(8,128)(2,1)} %bitcast.61) | data formatting | bytes 4194304 | tf_op jit(solution)/shard_map/reshape | solution.py:76
  164.4 0.8 select_select_fusion
  165.2 3.5 %all-to-all-start = ((bf16[16,8,1024]{2,1,0:T(8,128)(2,1)}), bf16[16,8,1024]{2,1,0:T(8,128)(2,1)S(1)}, u32[]{:S(2)}, u32[]{:S(2)}) async-start(bf16[16,8,1024]{2,1,0:T(8,128)(2,1)} %select_select_fusion), calls=%async_computation | async-start | bytes 524288 | tf_op jit(solution)/shard_map/all_to_all | solution.py:125
  168.8 1.9 %select_convert_fusion = bf16[256,4096]{1,0:T(8,128)(2,1)} fusion(bf16[256,4096]{1,0:T(8,128)(2,1)S(1)} %copy.32, pred[256]{0:T(512)(128)(4,1)S(1)} %iota_compare_fusion.8), kind=kLoop, calls=%fused_computation.7 | loop fusion | flops 1048576 | bytes 4194560 | tf_op jit(solution)/shard_map/convert_element_type | solution.py:77
  170.7 8.1 %all-to-all-done = bf16[16,8,1024]{2,1,0:T(8,128)(2,1)S(1)} async-done(((bf16[16,8,1024]{2,1,0:T(8,128)(2,1)}), bf16[16,8,1024]{2,1,0:T(8,128)(2,1)S(1)}, u32[]{:S(2)}, u32[]{:S(2)}) %all-to-all-start) | async-done | bytes 262176 | tf_op jit(solution)/shard_map/all_to_all | solution.py:125
  179.4 0.9 fusion.9
  (47 shorter events, 8.4 us)
Async XLA Ops:
  7.2 132.7 %all-gather.3.cloned.1.call-start = ((), (), s32[]{:S(2)}) async-start(), calls=%async_computation.1 | async-start | bytes 17825792 | tf_op jit(solution)/shard_map/all_gather | solution.py:88
  153.5 2.7 %copy-start.1 = (pred[256,256]{0,1:T(8,128)(4,1)S(1)}, pred[256,256]{0,1:T(8,128)(4,1)}, u32[]{:S(2)}) copy-start(pred[256,256]{0,1:T(8,128)(4,1)} %fusion.14) | copy-start | bytes 196612
  158.6 5.1 %copy-start = (bf16[256,1024]{1,0:T(8,128)(2,1)S(1)}, bf16[256,1024]{1,0:T(8,128)(2,1)}, u32[]{:S(2)}) copy-start(bf16[256,1024]{1,0:T(8,128)(2,1)} %get-tuple-element.20) | copy-start | bytes 1572868
  158.6 5.8 %copy-start.4 = (pred[16]{0:T(512)(128)(4,1)S(1)}, pred[16]{0:T(512)(128)(4,1)}, u32[]{:S(2)}) copy-start(pred[16]{0:T(512)(128)(4,1)} %fusion.20) | copy-start | bytes 52
  158.6 5.8 %copy-start.5 = (pred[16]{0:T(512)(128)(4,1)S(1)}, pred[16]{0:T(512)(128)(4,1)}, u32[]{:S(2)}) copy-start(pred[16]{0:T(512)(128)(4,1)} %compare_and_fusion.1) | copy-start | bytes 52
  160.8 18.7 %copy-start.2 = (pred[192]{0:T(512)(128)(4,1)S(1)}, pred[192]{0:T(512)(128)(4,1)}, u32[]{:S(2)}) copy-start(pred[192]{0:T(512)(128)(4,1)} %broadcast_in_dim.173) | copy-start | bytes 580
  160.8 18.7 %copy-start.3 = (pred[192]{0:T(512)(128)(4,1)S(1)}, pred[192]{0:T(512)(128)(4,1)}, u32[]{:S(2)}) copy-start(pred[192]{0:T(512)(128)(4,1)} %broadcast_in_dim.178) | copy-start | bytes 580
  165.2 13.5 %all-to-all-start = ((bf16[16,8,1024]{2,1,0:T(8,128)(2,1)}), bf16[16,8,1024]{2,1,0:T(8,128)(2,1)S(1)}, u32[]{:S(2)}, u32[]{:S(2)}) async-start(bf16[16,8,1024]{2,1,0:T(8,128)(2,1)} %select_select_fusion), calls=%async_computation | async-start | bytes 524288 | tf_op jit(solution)/shard_map/all_to_all | solution.py:125
Sparse Core Ops, SparseCore 0:
  10.2 129.6 all-gather.2
where the time goes:
time: 188 us; the launch traced here: 187 us
  waiting for transfers between devices  89 us (47%)
  blocking collectives  32.1 us (17%)
  other arithmetic  17.8 us (9%)
  between operations  16.3 us (9%)
  matrix products  15.7 us (8%)
  local copies, waits for them, and re-layouts  12.6 us (7%)
  starting transfers between devices  3.57 us (2%)
    all_gather x1, waiting for transfers between devices, project(): lax.all_gather(kv_weight, 'dp', axis=0, tiled=True)  80.3 us
    all_gather x1, blocking collectives, per_device(): lax.all_gather(balance, 'dp', axis=0, tiled=True)  18.4 us
    unnamed x1, blocking collectives  13.7 us
    dot_general x1, matrix products, project(): jnp.dot(row_block, lax.all_gather(kv_weight, 'dp', axis=0, tiled=True), p...  12.2 us
    all_to_all x1, waiting for transfers between devices, per_device(): lax.all_to_all(outgoing, 'dp', split_axis=0, concat_axis=0, tiled=True)  8.11 us
    unnamed x16, local copies, waits for them, and re-layouts  4.12 us
  transfers between devices with their start and end apart: 2, of which 2 were waited for; matrix products, arithmetic and copies ran while one was open for 10% of the time, Pallas kernels for 0%

commit v1 on v0

v1 whole, which is shorter than its diff:
```python
import math

import jax
import jax.numpy as jnp
from jax import lax
from jax.experimental import pallas as pl
from jax.experimental.pallas import tpu as pltpu
from jax.sharding import PartitionSpec as P

HEAD = 128
SPAN = 8
HOME = 32
WORK = 24
ABSENT = 1e30
MASKED = -1e30
MIB = 1 << 20


def ring_place(ring, position):
    return jnp.where(2 * position < ring, 2 * position, 2 * (ring - 1 - position) + 1)


class Links:
    def __init__(self, replicas, groups):
        ring = replicas // 4
        places = [p for p in range(0, ring, 2)] + [p for p in range(1, ring, 2)][::-1]
        ahead = {places[i]: places[(i + 1) % ring] for i in range(ring)}
        steps = [
            ((z * 2 + y) * 2 + c, (ahead[z] * 2 + y) * 2 + c)
            for z in range(ring)
            for y in range(2)
            for c in range(2)
        ]
        self.routes = {
            "fore": ("z", "dp", steps),
            "back": ("z", "dp", [(d, s) for s, d in steps]),
            "y": ("y", "dp", [(i, i ^ 2) for i in range(replicas)]),
            "x": ("x", "group", [(i, i ^ 1) for i in range(groups)]),
        }
        self.last = {}

    def send(self, value, route):
        link, axis, pairs = self.routes[route]
        if link in self.last:
            value = lax.optimization_barrier((value, self.last[link]))[0]
        self.last[link] = lax.ppermute(value, axis, pairs)
        return self.last[link]


def core_swap(value, replicas):
    return lax.ppermute(value, "dp", [(i, i ^ 1) for i in range(replicas)])


def multiply(own_states, peer_states, pieces, blocks, start=None):
    count = len(pieces)
    depth, columns = pieces[0].shape
    tokens = own_states.shape[0]

    def kernel(block_ref, own_ref, peer_ref, *refs):
        piece_refs = refs[:count]
        refs = refs[count:]
        if start is not None:
            start_refs, refs = refs[:2], refs[2:]
        own_out, peer_out, left, right, sems = refs
        copies = []
        for i in range(count):
            span = pl.ds(pl.multiple_of(block_ref[i] * depth, 128), depth)
            group = (
                pltpu.make_async_copy(piece_refs[i], right.at[i], sems.at[3 * i]),
                pltpu.make_async_copy(
                    own_ref.at[:, span], left.at[i, pl.ds(0, tokens)], sems.at[3 * i + 1]
                ),
                pltpu.make_async_copy(
                    peer_ref.at[:, span], left.at[i, pl.ds(tokens, tokens)], sems.at[3 * i + 2]
                ),
            )
            for copy in group:
                copy.start()
            copies.append(group)
        for i in range(count):
            for copy in copies[i]:
                copy.wait()
            product = jnp.dot(left[i], right[i], preferred_element_type=jnp.float32)
            for out, part, first in (
                (own_out, product[:tokens], 0),
                (peer_out, product[tokens:], 1),
            ):
                if i == 0:
                    out[...] = part if start is None else start_refs[first][...] + part
                else:
                    out[...] += part

    anywhere = pl.BlockSpec(memory_space=pl.ANY)
    inside = pl.BlockSpec(memory_space=pltpu.VMEM)
    total = jax.ShapeDtypeStruct((tokens, columns), jnp.float32)
    return pl.pallas_call(
        kernel,
        out_shape=(total, total),
        in_specs=[pl.BlockSpec(memory_space=pltpu.SMEM)]
        + [anywhere] * (2 + count)
        + [inside] * (0 if start is None else 2),
        out_specs=(inside, inside),
        scratch_shapes=[
            pltpu.VMEM((count, 2 * tokens, depth), jnp.bfloat16),
            pltpu.VMEM((count, depth, columns), jnp.bfloat16),
            pltpu.SemaphoreType.DMA((3 * count,)),
        ],
        compiler_params=pltpu.CompilerParams(vmem_limit_bytes=32 * MIB),
        cost_estimate=pl.CostEstimate(
            flops=4 * count * tokens * depth * columns,
            bytes_accessed=count * (4 * tokens * depth + 2 * depth * columns),
            transcendentals=0,
        ),
    )(blocks, own_states, peer_states, *pieces, *(() if start is None else start))


def finish(own_part, peer_part, bias, cosines, sines, destination, live_rows, replicas):
    tokens, columns = own_part.shape
    keys = columns // 2
    rows = replicas * SPAN

    def kernel(own_ref, peer_ref, bias_ref, cos_ref, sin_ref, dest_ref, live_ref, kv_ref, key_ref, out_ref):
        kv = (own_ref[...] + peer_ref[...] + bias_ref[...]).astype(jnp.bfloat16)
        kv = jnp.where(live_ref[...] > 0.5, kv.astype(jnp.float32), 0.0)
        kept = kv.astype(jnp.bfloat16)
        kv_ref[...] = kept
        row = lax.broadcasted_iota(jnp.int32, (rows, tokens), 0)
        token = lax.broadcasted_iota(jnp.int32, (rows, tokens), 1)
        match = (dest_ref[...] == row // SPAN) & (token % SPAN == row % SPAN)
        pick = jnp.where(match, 1.0, 0.0)
        found = jnp.sum(pick, axis=1, keepdims=True)
        spans = jnp.dot(pick.astype(jnp.bfloat16), kept, preferred_element_type=jnp.float32)
        out_ref[...] = jnp.where(found > 0.5, spans, ABSENT).astype(jnp.bfloat16)
        for head in range(keys // HEAD):
            part = kv[:, head * HEAD : (head + 1) * HEAD]
            turned = part * cos_ref[...] + pltpu.roll(part, HEAD // 2, 1) * sin_ref[...]
            key_ref[:, head * HEAD : (head + 1) * HEAD] = turned.astype(jnp.bfloat16)

    return pl.pallas_call(
        kernel,
        out_shape=(
            jax.ShapeDtypeStruct((tokens, columns), jnp.bfloat16),
            jax.ShapeDtypeStruct((tokens, keys), jnp.bfloat16),
            jax.ShapeDtypeStruct((rows, columns), jnp.bfloat16),
        ),
        compiler_params=pltpu.CompilerParams(vmem_limit_bytes=16 * MIB),
        cost_estimate=pl.CostEstimate(
            flops=2 * rows * tokens * columns,
            bytes_accessed=10 * tokens * columns,
            transcendentals=0,
        ),
    )(own_part, peer_part, bias, cosines, sines, destination, live_rows)


def attend(scalars, queries, keys, kv, context=None):
    tokens = queries.shape[0]
    heads = keys.shape[1] // HEAD
    width = queries.shape[1] // (2 * heads)
    half_tokens = tokens // 2

    def kernel(scalar_ref, query_ref, key_ref, value_ref, *refs):
        context_ref, mask_ref = refs[-2:]
        live = scalar_ref[1]

        @pl.when(pl.program_id(0) == 0)
        def _():
            target = lax.broadcasted_iota(jnp.int32, (tokens, tokens), 0)
            source = lax.broadcasted_iota(jnp.int32, (tokens, tokens), 1)

            def segment(token):
                return jnp.where(token >= scalar_ref[2], 1, 0) + jnp.where(
                    token >= scalar_ref[3], 1, 0
                )

            near = (segment(source) == segment(target)) | (segment(source) == 0)
            allowed = ((source <= target) & (source < live) & near) | (source == target)
            mask_ref[...] = jnp.where(allowed, 0.0, MASKED)

        scale = HEAD**-0.5 * math.log2(math.e)
        key = key_ref[...]
        value = value_ref[...]
        for start, reach in ((0, half_tokens), (half_tokens, tokens)):
            rows = slice(start, start + half_tokens)
            mask = mask_ref[rows, :reach]
            is_live = (
                lax.broadcasted_iota(jnp.int32, (half_tokens, HEAD), 0) + start < live
            )
            for head in range(width // HEAD):
                lanes = slice(head * HEAD, (head + 1) * HEAD)
                scores = lax.dot_general(
                    query_ref[rows, lanes],
                    key[:reach],
                    (((1,), (1,)), ((), ())),
                    preferred_element_type=jnp.float32,
                )
                scores = scores * scale + mask
                weights = jnp.exp2(scores - jnp.max(scores, axis=1, keepdims=True))
                inverse = 1.0 / jnp.sum(weights, axis=1, keepdims=True)
                weights = (weights * inverse).astype(jnp.bfloat16)
                mixed = jnp.dot(weights, value[:reach], preferred_element_type=jnp.float32)
                context_ref[rows, lanes] = jnp.where(is_live, mixed, 0.0).astype(jnp.bfloat16)

    wide = pl.BlockSpec((tokens, width), lambda i, s: (0, s[0] * heads + i))
    in_specs = [
        wide,
        pl.BlockSpec((tokens, HEAD), lambda i, s: (0, i)),
        pl.BlockSpec((tokens, HEAD), lambda i, s: (0, heads + i)),
    ]
    arguments = [scalars, queries, keys, kv]
    if context is not None:
        in_specs.append(pl.BlockSpec(memory_space=pl.ANY))
        arguments.append(context)
    return pl.pallas_call(
        kernel,
        out_shape=jax.ShapeDtypeStruct(queries.shape, jnp.bfloat16),
        grid_spec=pltpu.PrefetchScalarGridSpec(
            num_scalar_prefetch=1,
            grid=(heads,),
            in_specs=in_specs,
            out_specs=wide,
            scratch_shapes=[pltpu.VMEM((tokens, tokens), jnp.float32)],
        ),
        input_output_aliases={} if context is None else {4: 0},
        compiler_params=pltpu.CompilerParams(vmem_limit_bytes=16 * MIB),
        cost_estimate=pl.CostEstimate(
            flops=4 * tokens * tokens * heads * width,
            bytes_accessed=4 * tokens * heads * width,
            transcendentals=tokens * tokens * heads * width // HEAD,
        ),
    )(*arguments)


def place(half, kept_count, keep_rows, mine, other, mine_spans, other_spans):
    rows = WORK * SPAN
    slots, columns = mine_spans.shape
    part = columns // 2

    def kernel(half_ref, kept_ref, keep_ref, mine_ref, other_ref, mine_in, other_in, out_ref):
        present = jnp.where(other_in[:, :HEAD].astype(jnp.float32) > 0.5 * ABSENT, 0.0, 1.0)
        row = lax.broadcasted_iota(jnp.int32, (slots, slots), 0)
        column = lax.broadcasted_iota(jnp.int32, (slots, slots), 1)
        before = (column // SPAN < row // SPAN) & (column % SPAN == 0)
        before = jnp.where(before, 1.0, 0.0).astype(jnp.bfloat16)
        earlier = jnp.dot(
            before, present.astype(jnp.bfloat16), preferred_element_type=jnp.float32
        )
        rank = earlier[:, :1].astype(jnp.int32) + kept_ref[0]
        work = lax.broadcasted_iota(jnp.int32, (slots, rows), 1)
        sender = lax.broadcasted_iota(jnp.int32, (slots, rows), 0)
        hit = (work // SPAN == rank) & (work % SPAN == sender % SPAN) & (present[:, :1] > 0.5)
        hit = jnp.where(hit, 1.0, 0.0).astype(jnp.bfloat16)
        keep = keep_ref[...] > 0.5
        own = half_ref[0]
        for home, spans, which in ((mine_ref, mine_in, own), (other_ref, other_in, 1 - own)):
            moved = lax.dot_general(
                hit, spans[...], (((0,), (0,)), ((), ())), preferred_element_type=jnp.float32
            )
            total = jnp.where(keep, home[...].astype(jnp.float32), moved).astype(jnp.bfloat16)
            out_ref[:, pl.ds(pl.multiple_of(which * part, HEAD), part)] = total[:, :part]
            out_ref[:, pl.ds(pl.multiple_of((2 + which) * part, HEAD), part)] = total[:, part:]

    inside = pl.BlockSpec(memory_space=pltpu.VMEM)
    scalar = pl.BlockSpec(memory_space=pltpu.SMEM)
    home_rows = pl.BlockSpec((rows, columns), lambda i: (0, 0))
    whole = pl.BlockSpec((slots, columns), lambda i: (0, 0))
    return pl.pallas_call(
        kernel,
        grid=(1,),
        out_shape=jax.ShapeDtypeStruct((rows, 2 * columns), jnp.bfloat16),
        in_specs=[
            scalar,
            scalar,
            pl.BlockSpec((rows, 1), lambda i: (0, 0)),
            home_rows,
            home_rows,
            whole,
            whole,
        ],
        out_specs=pl.BlockSpec((rows, 2 * columns), lambda i: (0, 0)),
        compiler_params=pltpu.CompilerParams(vmem_limit_bytes=16 * MIB),
        cost_estimate=pl.CostEstimate(
            flops=4 * rows * slots * columns,
            bytes_accessed=8 * rows * columns,
            transcendentals=0,
        ),
    )(half, kept_count, keep_rows, mine, other, mine_spans, other_spans)


def per_device(states, queries, kv_weight, kv_bias, lengths, bounds, balance):
    replicas = lax.axis_size("dp")
    own_index = lax.axis_index("dp")
    half = lax.axis_index("group") % 2
    core = own_index % 2
    own_y = own_index // 2 % 2
    own_z = own_index // 4
    ring = replicas // 4
    position = jnp.where(own_z % 2 == 0, own_z // 2, ring - 1 - own_z // 2)
    tokens = states.shape[0]
    width = kv_weight.shape[1]
    quarter = width // 4

    def columns_of(array, which):
        parts = [
            lax.dynamic_slice_in_dim(array, (2 * j + which) * quarter, quarter, array.ndim - 1)
            for j in range(2)
        ]
        return jnp.concatenate(parts, axis=-1)

    def block(offset, across):
        z = ring_place(ring, (position - offset + ring) % ring)
        y = own_y if not across else 1 - own_y
        return ((z * 2 + y) * 2 + core).astype(jnp.int32)

    links = Links(replicas, lax.axis_size("group"))
    mine_weight = columns_of(kv_weight, half)
    other_weight = columns_of(kv_weight, 1 - half)
    peer_states = core_swap(states, replicas)
    fore = ring // 2
    order = [k for j in range(1, ring) for k in (j, -j)][: ring - 1]
    held = {0: mine_weight}
    mine = [(mine_weight, block(0, False))]
    other = [(other_weight, block(0, False))]
    late = []
    across = links.send(mine_weight, "y")
    mine.append((across, block(0, True)))
    for k in order:
        held[k] = links.send(held[k - 1], "fore") if k > 0 else links.send(held[k + 1], "back")
        mine.append((held[k], block(k, False)))
        across = links.send(held[k], "y")
        mine.append((across, block(k, True)))
        if 1 <= k < fore:
            other.append((links.send(held[k], "x"), block(k, False)))
        piece = (links.send(across, "x"), block(k, True))
        (late if k == order[-1] else other).append(piece)
    moving = other_weight
    for j in range(1, ring - fore + 1):
        moving = links.send(moving, "back")
        (late if j == ring - fore else other).append((moving, block(-j, False)))
    late.append((links.send(other_weight, "y"), block(0, True)))

    def project(pieces, start=None):
        blocks = jnp.stack([b for _, b in pieces])
        return multiply(states, peer_states, [p for p, _ in pieces], blocks, start)

    mine_own, mine_peer = project(mine[-1:], project(mine[:-1]))
    other_own, other_peer = project(late, project(other))

    token_ids = jnp.arange(tokens, dtype=jnp.int32)
    live_tokens = lengths[0] * SPAN
    is_live = token_ids < live_tokens
    owner = jnp.repeat(balance[0], SPAN)
    is_moved = is_live & (owner != own_index)
    destination = jnp.where(is_moved, owner, -1)[None, :]
    live_rows = is_live.astype(jnp.float32)[:, None]
    keep = is_live & jnp.logical_not(is_moved)
    keep_rows = keep.astype(jnp.float32)[:, None]
    kept_count = (jnp.sum(keep.astype(jnp.int32)) // SPAN)[None]
    chosen, rejected = bounds[0, 0], bounds[0, 1]
    place_ids = jnp.where(token_ids >= rejected, token_ids - (rejected - chosen), token_ids)
    frequency = jnp.exp(
        jnp.arange(HEAD // 2, dtype=jnp.float32) * (-2.0 * math.log(1000000.0) / HEAD)
    )
    angles = place_ids.astype(jnp.float32)[:, None] * frequency[None, :]
    cosines, sines = jnp.cos(angles), jnp.sin(angles)
    cosines = jnp.concatenate([cosines, cosines], axis=1)
    sines = jnp.concatenate([-sines, sines], axis=1)

    def complete(own_part, peer_part, which):
        return finish(
            own_part,
            core_swap(peer_part, replicas),
            columns_of(kv_bias, which)[None, :],
            cosines,
            sines,
            destination,
            live_rows,
            replicas,
        )

    def exchange(spans):
        spans = spans.reshape(replicas, SPAN, width // 2)
        spans = lax.all_to_all(spans, "dp", split_axis=0, concat_axis=0, tiled=True)
        return spans.reshape(replicas * SPAN, width // 2)

    def scalars(which):
        return jnp.stack([which, live_tokens, chosen, rejected]).astype(jnp.int32)

    mine_kv, mine_keys, mine_spans = complete(mine_own, mine_peer, half)
    other_kv, other_keys, other_spans = complete(other_own, other_peer, 1 - half)
    mine_spans = exchange(mine_spans)
    other_spans = exchange(other_spans)
    context = attend(scalars(half), queries, mine_keys, mine_kv)
    context = attend(scalars(1 - half), queries, other_keys, other_kv, context)
    work_rows = place(
        half[None].astype(jnp.int32),
        kept_count,
        keep_rows,
        mine_kv,
        other_kv,
        mine_spans,
        other_spans,
    )
    return (context, work_rows)


def solution(mesh):
    in_specs = (
        P(("group", "dp"), None),
        P(("group", "dp"), None),
        P("dp", None),
        P(),
        P(("group", "dp")),
        P(("group", "dp"), None),
        P(("group", "dp"), None),
    )
    out_specs = (P(("group", "dp"), None), P(("group", "dp"), None))
    return jax.shard_map(
        per_device, mesh=mesh, in_specs=in_specs, out_specs=out_specs, check_vma=False
    )
```

time: 188 us -> 126 us (0.67)
  waiting for transfers between devices: 89 us -> 39.3 us
  Pallas kernels: 0 us -> 35.2 us
  blocking collectives: 32.1 us -> 0 us
  starting transfers between devices: 3.57 us -> 27 us
  matrix products: 15.7 us -> 0 us
  between operations: 16.3 us -> 5.06 us
  other arithmetic: 17.8 us -> 7.62 us
    all_gather x1 -> x0, waiting for transfers between devices: 80.3 us -> none  [project(): lax.all_gather(kv_weight, 'dp', axis=0, tiled=True)]
    ppermute x0 -> x17, waiting for transfers between devices: none -> 36.2 us  [the longest x14 36.2 us: send(): self.last[link] = lax.ppermute(value, axis, pairs)]
    pallas_call x0 -> x9, Pallas kernels: none -> 35.2 us  [the longest x2 18 us: attend(): pl.pallas_call(kernel, out_shape=jax.ShapeDtypeStruct(queries.shape, jnp....]
    ppermute x0 -> x17, starting transfers between devices: none -> 19.4 us  [the longest x14 18.7 us: send(): self.last[link] = lax.ppermute(value, axis, pairs)]
    all_gather x1 -> x0, blocking collectives: 18.4 us -> none  [per_device(): lax.all_gather(balance, 'dp', axis=0, tiled=True)]
    dot_general x3 -> x0, matrix products: 15.7 us -> none  [the longest x1 12.2 us: project(): jnp.dot(row_block, lax.all_gather(kv_weight, 'dp', axis=0, tiled=True), p...]
    unnamed x1 -> x0, blocking collectives: 13.7 us -> none
    all_to_all x1 -> x2, waiting for transfers between devices: 8.11 us -> 3.13 us  [exchange(): spans = lax.all_to_all(spans, 'dp', split_axis=0, concat_axis=0, tiled=True)]
  transfers between devices with their start and end apart: 2 -> 19, of which waited for: 2 -> 8; matrix products, arithmetic and copies ran while one was open for 10% -> 10% of each run, Pallas kernels for 0% -> 26%
where the time goes in v1:
time: 126 us; the launch traced here: 125 us
  waiting for transfers between devices  39.3 us (31%)
  Pallas kernels  35.2 us (28%)
  starting transfers between devices  27 us (21%)
  local copies, waits for them, and re-layouts  10.9 us (9%)
  other arithmetic  7.62 us (6%)
  between operations  5.06 us (4%)
    ppermute x14, waiting for transfers between devices, send(): self.last[link] = lax.ppermute(value, axis, pairs)  36.2 us
    ppermute x14, starting transfers between devices, send(): self.last[link] = lax.ppermute(value, axis, pairs)  18.7 us
    pallas_call x2, Pallas kernels, attend(): pl.pallas_call(kernel, out_shape=jax.ShapeDtypeStruct(queries.shape, jnp....  18 us
    pallas_call x4, Pallas kernels, multiply(): pl.pallas_call(kernel, out_shape=(total, total), in_specs=[pl.BlockSpec(m...  12.9 us
    all_to_all x2, starting transfers between devices, exchange(): spans = lax.all_to_all(spans, 'dp', split_axis=0, concat_axis=0, tiled=True)  7.67 us
    unnamed x30, local copies, waits for them, and re-layouts  6.5 us
    all_to_all x2, waiting for transfers between devices, exchange(): spans = lax.all_to_all(spans, 'dp', split_axis=0, concat_axis=0, tiled=True)  3.13 us
    dynamic_slice x2, local copies, waits for them, and re-layouts, columns_of(): lax.dynamic_slice_in_dim(array, (2 * j + which) * quarter, quarter, array...  2.64 us
  transfers between devices with their start and end apart: 19, of which 8 were waited for; matrix products, arithmetic and copies ran while one was open for 10% of the time, Pallas kernels for 26%

profile of v1, /device:TPU:0, one launch (start us, length us, event | category | flops | bytes accessed | tf_op | source)
XLA Modules:
  0.0 125.1 jit_solution(16958725498044610296)
XLA Ops:
  1.2 2.0 %constant_dynamic-slice_fusion.1 = (bf16[512,256]{1,0:T(8,128)(2,1)S(1)}, bf16[512,256]{1,0:T(8,128)(2,1)S(1)}, bf16[512,256]{1,0:T(8,128)(2,1)S(1)}, bf16[512,256]{1,0:T(8,128)(2,1)}) fusion(bf16[512,1024]{1,0:T(8,128)(2,1)} %param.9, s32[]{:T(128)S(6)} %select_n.155, s32[]{:T(128)S(6)} %select_n.154, s32[]{:T(128)S(6)} %select_n.153, s32[]{:T(128)S(6)} %select_n.156), kind=kLoop, calls=%fused_computation.21 | loop fusion | bytes 2097168 | tf_op jit(solution)/shard_map/dynamic_slice | solution.py:304
  3.2 3.7 %collective-permute-start.1 = (bf16[512,512]{1,0:T(8,128)(2,1)S(1)}, bf16[512,512]{1,0:T(8,128)(2,1)S(1)}, u32[]{:S(2)}, u32[]{:S(2)}) collective-permute-start(bf16[512,512]{1,0:T(8,128)(2,1)S(1)} %pad_maximum_fusion.refs_0_), channel_id=1, source_target_pairs={{0,8},{1,9},{2,10},{3,11},{4,0},{5,1},{6,2},{7,3},{8,12},{9,13},{1... | collective-permute-start | bytes 1572872 | tf_op jit(solution)/shard_map/ppermute | solution.py:46
  6.9 1.5 %collective-permute-start.4 = (bf16[512,512]{1,0:T(8,128)(2,1)S(1)}, bf16[512,512]{1,0:T(8,128)(2,1)S(1)}, u32[]{:S(2)}, u32[]{:S(2)}) collective-permute-start(bf16[512,512]{1,0:T(8,128)(2,1)S(1)} %pad_maximum_fusion.refs_0_), channel_id=1, source_target_pairs={{0,2},{1,3},{2,0},{3,1},{4,6},{5,7},{6,4},{7,5},{8,10},{9,11},{10,... | collective-permute-start | bytes 1572872 | tf_op jit(solution)/shard_map/ppermute | solution.py:46
  8.4 10.3 %collective-permute-done.1.refs_2_ = bf16[512,512]{1,0:T(8,128)(2,1)S(1)} collective-permute-done((bf16[512,512]{1,0:T(8,128)(2,1)S(1)}, bf16[512,512]{1,0:T(8,128)(2,1)S(1)}, u32[]{:S(2)}, u32[]{:S(2)}) %collective-permute-start.1) | collective-permute-done | bytes 524320 | tf_op jit(solution)/shard_map/ppermute | solution.py:46
  18.7 2.2 %collective-permute-done.4.refs_1_ = bf16[512,512]{1,0:T(8,128)(2,1)S(1)} collective-permute-done((bf16[512,512]{1,0:T(8,128)(2,1)S(1)}, bf16[512,512]{1,0:T(8,128)(2,1)S(1)}, u32[]{:S(2)}, u32[]{:S(2)}) %collective-permute-start.4) | collective-permute-done | bytes 524320 | tf_op jit(solution)/shard_map/ppermute | solution.py:46
  20.9 1.5 %collective-permute-start.5 = (bf16[512,512]{1,0:T(8,128)(2,1)S(1)}, bf16[512,512]{1,0:T(8,128)(2,1)S(1)}, u32[]{:S(2)}, u32[]{:S(2)}) collective-permute-start(bf16[512,512]{1,0:T(8,128)(2,1)S(1)} %collective-permute-done.1.refs_2_), channel_id=1, source_target_pairs={{0,2},{1,3},{2,0},{3,1},{4,6},{5,7},{6,4},{7,5},{8,10},{9,11},{10,... | collective-permute-start | bytes 1572872 | tf_op jit(solution)/shard_map/ppermute | solution.py:46
  27.2 6.8 %collective-permute-done.5.refs_3_ = bf16[512,512]{1,0:T(8,128)(2,1)S(1)} collective-permute-done((bf16[512,512]{1,0:T(8,128)(2,1)S(1)}, bf16[512,512]{1,0:T(8,128)(2,1)S(1)}, u32[]{:S(2)}, u32[]{:S(2)}) %collective-permute-start.5) | collective-permute-done | bytes 524320 | tf_op jit(solution)/shard_map/ppermute | solution.py:46
  34.1 2.2 %collective-permute-done.2.refs_4_ = bf16[512,512]{1,0:T(8,128)(2,1)} collective-permute-done((bf16[512,512]{1,0:T(8,128)(2,1)S(1)}, bf16[512,512]{1,0:T(8,128)(2,1)}, u32[]{:S(2)}, u32[]{:S(2)}) %collective-permute-start.2) | collective-permute-done | bytes 524320 | tf_op jit(solution)/shard_map/ppermute | solution.py:46
  37.5 1.5 %collective-permute-start.9 = (bf16[512,512]{1,0:T(8,128)(2,1)S(1)}, bf16[512,512]{1,0:T(8,128)(2,1)S(1)}, u32[]{:S(2)}, u32[]{:S(2)}) collective-permute-start(bf16[512,512]{1,0:T(8,128)(2,1)S(1)} %collective-permute-done.5.refs_3_), channel_id=1, source_target_pairs={{0,16},{16,0},{1,17},{17,1},{2,18},{18,2},{3,19},{19,3},{4,20},{20... | collective-permute-start | bytes 1572872 | tf_op jit(solution)/shard_map/ppermute | solution.py:46
  41.2 7.4 %collective-permute-done.6.refs_5_ = bf16[512,512]{1,0:T(8,128)(2,1)} collective-permute-done((bf16[512,512]{1,0:T(8,128)(2,1)}, bf16[512,512]{1,0:T(8,128)(2,1)}, u32[]{:S(2)}, u32[]{:S(2)}) %collective-permute-start.6) | collective-permute-done | bytes 524320 | tf_op jit(solution)/shard_map/ppermute | solution.py:46
  48.6 1.5 %collective-permute-start.7 = (bf16[512,512]{1,0:T(8,128)(2,1)}, bf16[512,512]{1,0:T(8,128)(2,1)}, u32[]{:S(2)}, u32[]{:S(2)}) collective-permute-start(bf16[512,512]{1,0:T(8,128)(2,1)} %collective-permute-done.3.refs_6_), channel_id=1, source_target_pairs={{0,2},{1,3},{2,0},{3,1},{4,6},{5,7},{6,4},{7,5},{8,10},{9,11},{10,... | collective-permute-start | bytes 1572872 | tf_op jit(solution)/shard_map/ppermute | solution.py:46
  54.3 6.6 %collective-permute-done.7.refs_0_ = bf16[512,512]{1,0:T(8,128)(2,1)} collective-permute-done((bf16[512,512]{1,0:T(8,128)(2,1)}, bf16[512,512]{1,0:T(8,128)(2,1)}, u32[]{:S(2)}, u32[]{:S(2)}) %collective-permute-start.7) | collective-permute-done | bytes 524320 | tf_op jit(solution)/shard_map/ppermute | solution.py:46
  60.9 1.5 %collective-permute-start.14 = (bf16[512,512]{1,0:T(8,128)(2,1)S(1)}, bf16[512,512]{1,0:T(8,128)(2,1)S(1)}, u32[]{:S(2)}, u32[]{:S(2)}) collective-permute-start(bf16[512,512]{1,0:T(8,128)(2,1)S(1)} %pad_maximum_fusion.1.refs_0_), channel_id=1, source_target_pairs={{0,2},{1,3},{2,0},{3,1},{4,6},{5,7},{6,4},{7,5},{8,10},{9,11},{10,... | collective-permute-start | bytes 1572872 | tf_op jit(solution)/shard_map/ppermute | solution.py:46
  66.0 2.2 %copy-done = bf16[256,8192]{1,0:T(8,128)(2,1)S(1)} copy-done((bf16[256,8192]{1,0:T(8,128)(2,1)S(1)}, bf16[256,8192]{1,0:T(8,128)(2,1)}, u32[]{:S(2)}) %copy-start) | copy-done | bytes 4194328
  68.2 4.1 %shard_map.89 = (f32[256,512]{1,0:T(8,128)S(1)}, f32[256,512]{1,0:T(8,128)S(1)}) custom-call(s32[7]{0:T(128)S(1)} %stack.72.block_ref, bf16[256,8192]{1,0:T(8,128)(2,1)S(1)} %copy-done, bf16[256,8192]{1,0:T(8,128)(2,1)} %collective-permute-done.peer_ref, bf16[512,512]{1,0:T(8,128)(2,1)S(1)} %pad_maximum_fusion.refs_0_, ...), custom_call_target="tpu_custom_call" | custom-call | flops 1879048192 | bytes 7340032 | tf_op jit(solution)/shard_map/pallas_call | solution.py:96
  72.3 1.7 %shard_map.90 = (f32[256,512]{1,0:T(8,128)S(1)}, f32[256,512]{1,0:T(8,128)S(1)}) custom-call(s32[1]{0:T(128)} %bitcast.3.block_ref, bf16[256,8192]{1,0:T(8,128)(2,1)S(1)} %copy-done, bf16[256,8192]{1,0:T(8,128)(2,1)} %collective-permute-done.peer_ref, bf16[512,512]{1,0:T(8,128)(2,1)} %collective-permute-done.7.refs_0_, ...), custom_call_target="tpu_custom_call" | custom-call | flops 268435456 | bytes 1048576 | tf_op jit(solution)/shard_map/pallas_call | solution.py:96
  74.8 3.4 %shard_map.86 = (f32[256,512]{1,0:T(8,128)S(1)}, f32[256,512]{1,0:T(8,128)S(1)}) custom-call(s32[5]{0:T(128)S(1)} %stack.68.block_ref, bf16[256,8192]{1,0:T(8,128)(2,1)S(1)} %copy-done.1, bf16[256,8192]{1,0:T(8,128)(2,1)} %collective-permute-done.peer_ref, bf16[512,512]{1,0:T(8,128)(2,1)S(1)} %pad_maximum_fusion.1.refs_0_, ...), custom_call_target="tpu_custom_call" | custom-call | flops 1342177280 | bytes 5242880 | tf_op jit(solution)/shard_map/pallas_call | solution.py:96
  78.3 3.6 %shard_map.87 = (f32[256,512]{1,0:T(8,128)S(1)}, f32[256,512]{1,0:T(8,128)}) custom-call(s32[3]{0:T(128)S(1)} %pad_add_fusion.block_ref, bf16[256,8192]{1,0:T(8,128)(2,1)S(1)} %copy-done.1, bf16[256,8192]{1,0:T(8,128)(2,1)} %collective-permute-done.peer_ref, bf16[512,512]{1,0:T(8,128)(2,1)S(1)} %collective-permute-done.11.refs_0_, ...), custom_call_target="tpu_custom_call" | custom-call | flops 805306368 | bytes 3145728 | tf_op jit(solution)/shard_map/pallas_call | solution.py:96
  83.6 4.2 %all-to-all-start = ((bf16[16,8,512]{2,1,0:T(8,128)(2,1)}), bf16[16,8,512]{2,1,0:T(8,128)(2,1)}, u32[]{:S(2)}, u32[]{:S(2)}) async-start(bf16[16,8,512]{2,1,0:T(8,128)(2,1)} %bitcast.20), calls=%async_computation | async-start | bytes 262144 | tf_op jit(solution)/shard_map/all_to_all | solution.py:382
  92.6 3.1 %all-to-all-done = bf16[16,8,512]{2,1,0:T(8,128)(2,1)} async-done(((bf16[16,8,512]{2,1,0:T(8,128)(2,1)}), bf16[16,8,512]{2,1,0:T(8,128)(2,1)}, u32[]{:S(2)}, u32[]{:S(2)}) %all-to-all-start) | async-done | bytes 131104 | tf_op jit(solution)/shard_map/all_to_all | solution.py:382
  95.7 3.5 %all-to-all-start.1 = ((bf16[16,8,512]{2,1,0:T(8,128)(2,1)}), bf16[16,8,512]{2,1,0:T(8,128)(2,1)S(1)}, u32[]{:S(2)}, u32[]{:S(2)}) async-start(bf16[16,8,512]{2,1,0:T(8,128)(2,1)} %bitcast.26), calls=%async_computation.1 | async-start | bytes 262144 | tf_op jit(solution)/shard_map/all_to_all | solution.py:382
  105.0 9.0 %shard_map.92.refs_0_ = bf16[256,4096]{1,0:T(8,128)(2,1)} custom-call(s32[4]{0:T(128)S(1)} %add_add_fusion.1.scalar_ref, bf16[256,4096]{1,0:T(8,128)(2,1)S(1)} %copy-done.2, bf16[256,256]{1,0:T(8,128)(2,1)S(1)} %copy-done.7, bf16[256,512]{1,0:T(8,128)(2,1)S(1)} %get-tuple-element.49.value_ref.mine_ref), custom_call_target="tpu_custom_call" | custom-call | flops 536870912 | bytes 2097152 | tf_op jit(solution)/shard_map/pallas_call | solution.py:213
  114.0 9.0 %shard_map.93 = bf16[256,4096]{1,0:T(8,128)(2,1)} custom-call(s32[4]{0:T(128)S(1)} %add_add_fusion.scalar_ref, bf16[256,4096]{1,0:T(8,128)(2,1)S(1)} %copy-done.2, bf16[256,256]{1,0:T(8,128)(2,1)S(1)} %copy-done.9, bf16[256,512]{1,0:T(8,128)(2,1)S(1)} %get-tuple-element.43.value_ref.other_ref, ...), custom_call_target="tpu_custom_call", output_to_operand_aliasing={{}: (4, {})} | custom-call | flops 536870912 | bytes 2097152 | tf_op jit(solution)/shard_map/pallas_call | solution.py:213
  123.0 2.2 %shard_map.94 = bf16[192,1024]{1,0:T(8,128)(2,1)} custom-call(s32[1]{0:T(128)} %bitcast.16.half_ref, s32[1]{0:T(128)} %bitcast.19.kept_ref, f32[256,1]{1,0:T(8,128)S(1)} %copy-done.5, bf16[256,512]{1,0:T(8,128)(2,1)S(1)} %get-tuple-element.49.value_ref.mine_ref, bf16[256,512]{1,0:T(8,128)(2,1)S(1)} %get-tuple-element.43.value_ref.other_ref, ...), custom_call_target="tpu_custom_call" | custom-call | flops 50331648 | bytes 786432 | tf_op jit(solution)/shard_map/pallas_call | solution.py:266
  (78 shorter events, 25.3 us)
Async XLA Ops:
  0.6 24.1 %copy-start.12 = (s32[1,2]{1,0:T(1,128)S(1)}, s32[1,2]{1,0:T(1,128)}, u32[]{:S(2)}) copy-start(s32[1,2]{1,0:T(1,128)} %param.12) | copy-start | bytes 28
  0.6 25.9 %copy-start.11 = (f32[1024]{0:T(1024)S(1)}, f32[1024]{0:T(1024)}, u32[]{:S(2)}) copy-start(f32[1024]{0:T(1024)} %param.10) | copy-start | bytes 12292
  0.7 38.9 %copy-start.13 = (s32[1,32]{1,0:T(1,128)S(1)}, s32[1,32]{1,0:T(1,128)}, u32[]{:S(2)}) copy-start(s32[1,32]{1,0:T(1,128)} %param.13) | copy-start | bytes 388
  0.7 65.3 %collective-permute-start = (bf16[256,8192]{1,0:T(8,128)(2,1)}, bf16[256,8192]{1,0:T(8,128)(2,1)}, u32[]{:S(2)}, u32[]{:S(2)}) collective-permute-start(bf16[256,8192]{1,0:T(8,128)(2,1)} %own_ref.7), channel_id=1, source_target_pairs={{0,1},{1,0},{2,3},{3,2},{4,5},{5,4},{6,7},{7,6},{8,9},{9,8},{10,11... | collective-permute-start | bytes 12582920 | tf_op jit(solution)/shard_map/ppermute | solution.py:51
  3.2 15.5 %collective-permute-start.1 = (bf16[512,512]{1,0:T(8,128)(2,1)S(1)}, bf16[512,512]{1,0:T(8,128)(2,1)S(1)}, u32[]{:S(2)}, u32[]{:S(2)}) collective-permute-start(bf16[512,512]{1,0:T(8,128)(2,1)S(1)} %pad_maximum_fusion.refs_0_), channel_id=1, source_target_pairs={{0,8},{1,9},{2,10},{3,11},{4,0},{5,1},{6,2},{7,3},{8,12},{9,13},{1... | collective-permute-start | bytes 1572872 | tf_op jit(solution)/shard_map/ppermute | solution.py:46
  6.9 14.0 %collective-permute-start.4 = (bf16[512,512]{1,0:T(8,128)(2,1)S(1)}, bf16[512,512]{1,0:T(8,128)(2,1)S(1)}, u32[]{:S(2)}, u32[]{:S(2)}) collective-permute-start(bf16[512,512]{1,0:T(8,128)(2,1)S(1)} %pad_maximum_fusion.refs_0_), channel_id=1, source_target_pairs={{0,2},{1,3},{2,0},{3,1},{4,6},{5,7},{6,4},{7,5},{8,10},{9,11},{10,... | collective-permute-start | bytes 1572872 | tf_op jit(solution)/shard_map/ppermute | solution.py:46
  20.9 13.2 %collective-permute-start.5 = (bf16[512,512]{1,0:T(8,128)(2,1)S(1)}, bf16[512,512]{1,0:T(8,128)(2,1)S(1)}, u32[]{:S(2)}, u32[]{:S(2)}) collective-permute-start(bf16[512,512]{1,0:T(8,128)(2,1)S(1)} %collective-permute-done.1.refs_2_), channel_id=1, source_target_pairs={{0,2},{1,3},{2,0},{3,1},{4,6},{5,7},{6,4},{7,5},{8,10},{9,11},{10,... | collective-permute-start | bytes 1572872 | tf_op jit(solution)/shard_map/ppermute | solution.py:46
  22.4 13.9 %collective-permute-start.2 = (bf16[512,512]{1,0:T(8,128)(2,1)S(1)}, bf16[512,512]{1,0:T(8,128)(2,1)}, u32[]{:S(2)}, u32[]{:S(2)}) collective-permute-start(bf16[512,512]{1,0:T(8,128)(2,1)S(1)} %pad_maximum_fusion.refs_0_), channel_id=1, source_target_pairs={{8,0},{9,1},{10,2},{11,3},{0,4},{1,5},{2,6},{3,7},{12,8},{13,9},{1... | collective-permute-start | bytes 1572872 | tf_op jit(solution)/shard_map/ppermute | solution.py:46
  22.6 14.9 %collective-permute-start.8 = (bf16[512,512]{1,0:T(8,128)(2,1)S(1)}, bf16[512,512]{1,0:T(8,128)(2,1)S(1)}, u32[]{:S(2)}, u32[]{:S(2)}) collective-permute-start(bf16[512,512]{1,0:T(8,128)(2,1)S(1)} %collective-permute-done.1.refs_2_), channel_id=1, source_target_pairs={{0,16},{16,0},{1,17},{17,1},{2,18},{18,2},{3,19},{19,3},{4,20},{20... | collective-permute-start | bytes 1572872 | tf_op jit(solution)/shard_map/ppermute | solution.py:46
  36.3 12.3 %collective-permute-start.6 = (bf16[512,512]{1,0:T(8,128)(2,1)}, bf16[512,512]{1,0:T(8,128)(2,1)}, u32[]{:S(2)}, u32[]{:S(2)}) collective-permute-start(bf16[512,512]{1,0:T(8,128)(2,1)} %collective-permute-done.2.refs_4_), channel_id=1, source_target_pairs={{0,2},{1,3},{2,0},{3,1},{4,6},{5,7},{6,4},{7,5},{8,10},{9,11},{10,... | collective-permute-start | bytes 1572872 | tf_op jit(solution)/shard_map/ppermute | solution.py:46
  36.8 11.8 %collective-permute-start.3 = (bf16[512,512]{1,0:T(8,128)(2,1)S(1)}, bf16[512,512]{1,0:T(8,128)(2,1)}, u32[]{:S(2)}, u32[]{:S(2)}) collective-permute-start(bf16[512,512]{1,0:T(8,128)(2,1)S(1)} %collective-permute-done.1.refs_2_), channel_id=1, source_target_pairs={{0,8},{1,9},{2,10},{3,11},{4,0},{5,1},{6,2},{7,3},{8,12},{9,13},{1... | collective-permute-start | bytes 1572872 | tf_op jit(solution)/shard_map/ppermute | solution.py:46
  37.5 12.6 %collective-permute-start.9 = (bf16[512,512]{1,0:T(8,128)(2,1)S(1)}, bf16[512,512]{1,0:T(8,128)(2,1)S(1)}, u32[]{:S(2)}, u32[]{:S(2)}) collective-permute-start(bf16[512,512]{1,0:T(8,128)(2,1)S(1)} %collective-permute-done.5.refs_3_), channel_id=1, source_target_pairs={{0,16},{16,0},{1,17},{17,1},{2,18},{18,2},{3,19},{19,3},{4,20},{20... | collective-permute-start | bytes 1572872 | tf_op jit(solution)/shard_map/ppermute | solution.py:46
  39.6 12.8 %copy-start.14 = (pred[32]{0:T(512)(128)(4,1)}, pred[32]{0:T(512)(128)(4,1)S(1)}, u32[]{:S(2)}) copy-start(pred[32]{0:T(512)(128)(4,1)S(1)} %broadcast_compare_fusion) | copy-start | bytes 100
  48.6 12.3 %collective-permute-start.7 = (bf16[512,512]{1,0:T(8,128)(2,1)}, bf16[512,512]{1,0:T(8,128)(2,1)}, u32[]{:S(2)}, u32[]{:S(2)}) collective-permute-start(bf16[512,512]{1,0:T(8,128)(2,1)} %collective-permute-done.3.refs_6_), channel_id=1, source_target_pairs={{0,2},{1,3},{2,0},{3,1},{4,6},{5,7},{6,4},{7,5},{8,10},{9,11},{10,... | collective-permute-start | bytes 1572872 | tf_op jit(solution)/shard_map/ppermute | solution.py:46
  50.9 12.1 %collective-permute-start.10 = (bf16[512,512]{1,0:T(8,128)(2,1)}, bf16[512,512]{1,0:T(8,128)(2,1)}, u32[]{:S(2)}, u32[]{:S(2)}) collective-permute-start(bf16[512,512]{1,0:T(8,128)(2,1)} %collective-permute-done.6.refs_5_), channel_id=1, source_target_pairs={{0,16},{16,0},{1,17},{17,1},{2,18},{18,2},{3,19},{19,3},{4,20},{20... | collective-permute-start | bytes 1572872 | tf_op jit(solution)/shard_map/ppermute | solution.py:46
  52.4 12.1 %collective-permute-start.12 = (bf16[512,512]{1,0:T(8,128)(2,1)S(1)}, bf16[512,512]{1,0:T(8,128)(2,1)}, u32[]{:S(2)}, u32[]{:S(2)}) collective-permute-start(bf16[512,512]{1,0:T(8,128)(2,1)S(1)} %pad_maximum_fusion.1.refs_0_), channel_id=1, source_target_pairs={{8,0},{9,1},{10,2},{11,3},{0,4},{1,5},{2,6},{3,7},{12,8},{13,9},{1... | collective-permute-start | bytes 1572872 | tf_op jit(solution)/shard_map/ppermute | solution.py:46
  60.9 17.4 %collective-permute-start.14 = (bf16[512,512]{1,0:T(8,128)(2,1)S(1)}, bf16[512,512]{1,0:T(8,128)(2,1)S(1)}, u32[]{:S(2)}, u32[]{:S(2)}) collective-permute-start(bf16[512,512]{1,0:T(8,128)(2,1)S(1)} %pad_maximum_fusion.1.refs_0_), channel_id=1, source_target_pairs={{0,2},{1,3},{2,0},{3,1},{4,6},{5,7},{6,4},{7,5},{8,10},{9,11},{10,... | collective-permute-start | bytes 1572872 | tf_op jit(solution)/shard_map/ppermute | solution.py:46
  63.0 15.3 %collective-permute-start.11 = (bf16[512,512]{1,0:T(8,128)(2,1)}, bf16[512,512]{1,0:T(8,128)(2,1)S(1)}, u32[]{:S(2)}, u32[]{:S(2)}) collective-permute-start(bf16[512,512]{1,0:T(8,128)(2,1)} %collective-permute-done.7.refs_0_), channel_id=1, source_target_pairs={{0,16},{16,0},{1,17},{17,1},{2,18},{18,2},{3,19},{19,3},{4,20},{20... | collective-permute-start | bytes 1572872 | tf_op jit(solution)/shard_map/ppermute | solution.py:46
  64.5 13.8 %collective-permute-start.13 = (bf16[512,512]{1,0:T(8,128)(2,1)}, bf16[512,512]{1,0:T(8,128)(2,1)S(1)}, u32[]{:S(2)}, u32[]{:S(2)}) collective-permute-start(bf16[512,512]{1,0:T(8,128)(2,1)} %collective-permute-done.12.refs_4_), channel_id=1, source_target_pairs={{8,0},{9,1},{10,2},{11,3},{0,4},{1,5},{2,6},{3,7},{12,8},{13,9},{1... | collective-permute-start | bytes 1572872 | tf_op jit(solution)/shard_map/ppermute | solution.py:46
  74.1 7.9 %collective-permute-start.16 = (f32[256,512]{1,0:T(8,128)S(1)}, f32[256,512]{1,0:T(8,128)S(1)}, u32[]{:S(2)}, u32[]{:S(2)}) collective-permute-start(f32[256,512]{1,0:T(8,128)S(1)} %get-tuple-element.47), channel_id=1, source_target_pairs={{0,1},{1,0},{2,3},{3,2},{4,5},{5,4},{6,7},{7,6},{8,9},{9,8},{10,11... | collective-permute-start | bytes 1572872 | tf_op jit(solution)/shard_map/ppermute | solution.py:51
  81.9 22.2 %copy-start.2 = (bf16[256,4096]{1,0:T(8,128)(2,1)S(1)}, bf16[256,4096]{1,0:T(8,128)(2,1)}, u32[]{:S(2)}) copy-start(bf16[256,4096]{1,0:T(8,128)(2,1)} %query_ref.3) | copy-start | bytes 6291460
  81.9 8.0 %collective-permute-start.15 = (f32[256,512]{1,0:T(8,128)}, f32[256,512]{1,0:T(8,128)}, u32[]{:S(2)}, u32[]{:S(2)}) collective-permute-start(f32[256,512]{1,0:T(8,128)} %get-tuple-element.41), channel_id=1, source_target_pairs={{0,1},{1,0},{2,3},{3,2},{4,5},{5,4},{6,7},{7,6},{8,9},{9,8},{10,11... | collective-permute-start | bytes 1572872 | tf_op jit(solution)/shard_map/ppermute | solution.py:51
  83.6 12.1 %all-to-all-start = ((bf16[16,8,512]{2,1,0:T(8,128)(2,1)}), bf16[16,8,512]{2,1,0:T(8,128)(2,1)}, u32[]{:S(2)}, u32[]{:S(2)}) async-start(bf16[16,8,512]{2,1,0:T(8,128)(2,1)} %bitcast.20), calls=%async_computation | async-start | bytes 262144 | tf_op jit(solution)/shard_map/all_to_all | solution.py:382
  95.7 27.2 %all-to-all-start.1 = ((bf16[16,8,512]{2,1,0:T(8,128)(2,1)}), bf16[16,8,512]{2,1,0:T(8,128)(2,1)S(1)}, u32[]{:S(2)}, u32[]{:S(2)}) async-start(bf16[16,8,512]{2,1,0:T(8,128)(2,1)} %bitcast.26), calls=%async_computation.1 | async-start | bytes 262144 | tf_op jit(solution)/shard_map/all_to_all | solution.py:382
  (10 other events, 28.8 us)

commit v2 on v1

v2 whole, which is shorter than its diff:
```python
import math

import jax
import jax.numpy as jnp
from jax import lax
from jax.experimental import pallas as pl
from jax.experimental.pallas import tpu as pltpu
from jax.sharding import PartitionSpec as P

HEAD = 128
SPAN = 8
HOME = 32
WORK = 24
ABSENT = 1e30
MASKED = -1e30
MIB = 1 << 20


def ring_place(ring, position):
    return jnp.where(2 * position < ring, 2 * position, 2 * (ring - 1 - position) + 1)


def after(value, *before):
    return lax.optimization_barrier((value, *before))[0] if before else value


class Links:
    def __init__(self, replicas, groups):
        ring = replicas // 4
        places = [p for p in range(0, ring, 2)] + [p for p in range(1, ring, 2)][::-1]
        ahead = {places[i]: places[(i + 1) % ring] for i in range(ring)}
        steps = [
            ((z * 2 + y) * 2 + c, (ahead[z] * 2 + y) * 2 + c)
            for z in range(ring)
            for y in range(2)
            for c in range(2)
        ]
        self.routes = {
            "fore": ("z", "dp", steps),
            "back": ("z", "dp", [(d, s) for s, d in steps]),
            "y": ("y", "dp", [(i, i ^ 2) for i in range(replicas)]),
            "x": ("x", "group", [(i, i ^ 1) for i in range(groups)]),
        }
        self.last = {}

    def send(self, value, route, before=()):
        link, axis, pairs = self.routes[route]
        if link in self.last:
            before = (self.last[link], *before)
        self.last[link] = lax.ppermute(after(value, *before), axis, pairs)
        return self.last[link]


def core_swap(value, replicas):
    return lax.ppermute(value, "dp", [(i, i ^ 1) for i in range(replicas)])


def halves(weight, half):
    depth, width = weight.shape
    quarter = width // 4

    def kernel(half_ref, weight_ref, mine_ref, other_ref, sems):
        copies = []
        for i, out in enumerate((mine_ref, other_ref)):
            which = half_ref[0] if i == 0 else 1 - half_ref[0]
            for j in range(2):
                start = pl.multiple_of((2 * j + which) * quarter, HEAD)
                copies.append(
                    pltpu.make_async_copy(
                        weight_ref.at[:, pl.ds(start, quarter)],
                        out.at[:, pl.ds(j * quarter, quarter)],
                        sems.at[2 * i + j],
                    )
                )
        for copy in copies:
            copy.start()
        for copy in copies:
            copy.wait()

    anywhere = pl.BlockSpec(memory_space=pl.ANY)
    out = jax.ShapeDtypeStruct((depth, width // 2), weight.dtype)
    return pl.pallas_call(
        kernel,
        out_shape=(out, out),
        in_specs=[pl.BlockSpec(memory_space=pltpu.SMEM), anywhere],
        out_specs=(anywhere, anywhere),
        scratch_shapes=[pltpu.SemaphoreType.DMA((4,))],
        cost_estimate=pl.CostEstimate(
            flops=0, bytes_accessed=4 * depth * width, transcendentals=0
        ),
    )(half, weight)


def core_columns(states, core, depth):
    tokens, width = states.shape
    count = width // (2 * depth)

    def kernel(core_ref, states_ref, out_ref, sems):
        copies = []
        for i in range(count):
            start = pl.multiple_of((2 * i + core_ref[0]) * depth, HEAD)
            copies.append(
                pltpu.make_async_copy(
                    states_ref.at[:, pl.ds(start, depth)],
                    out_ref.at[:, pl.ds(i * depth, depth)],
                    sems.at[i],
                )
            )
        for copy in copies:
            copy.start()
        for copy in copies:
            copy.wait()

    anywhere = pl.BlockSpec(memory_space=pl.ANY)
    return pl.pallas_call(
        kernel,
        out_shape=jax.ShapeDtypeStruct((tokens, width // 2), states.dtype),
        in_specs=[pl.BlockSpec(memory_space=pltpu.SMEM), anywhere],
        out_specs=anywhere,
        scratch_shapes=[pltpu.SemaphoreType.DMA((count,))],
        cost_estimate=pl.CostEstimate(
            flops=0, bytes_accessed=2 * tokens * width, transcendentals=0
        ),
    )(core, states)


def multiply(own_states, peer_states, core, pieces, blocks, start=None):
    count = len(pieces)
    depth, columns = pieces[0].shape
    tokens = own_states.shape[0]
    batch = 4

    def kernel(core_ref, block_ref, own_ref, peer_ref, *refs):
        piece_refs = refs[:count]
        refs = refs[count:]
        if start is not None:
            start_refs, refs = refs[:2], refs[2:]
        own_out, peer_out, left, right, sems = refs
        copies = []
        for i in range(count):
            own_at = pl.multiple_of((2 * block_ref[i] + core_ref[0]) * depth, HEAD)
            peer_at = pl.multiple_of(block_ref[i] * depth, HEAD)
            deep = pl.ds(i * depth, depth)
            copies += [
                pltpu.make_async_copy(piece_refs[i], right.at[deep], sems.at[3 * i]),
                pltpu.make_async_copy(
                    own_ref.at[:, pl.ds(own_at, depth)],
                    left.at[pl.ds(0, tokens), deep],
                    sems.at[3 * i + 1],
                ),
                pltpu.make_async_copy(
                    peer_ref.at[:, pl.ds(peer_at, depth)],
                    left.at[pl.ds(tokens, tokens), deep],
                    sems.at[3 * i + 2],
                ),
            ]
        for copy in copies:
            copy.start()
        for i in range(0, count, batch):
            stop = min(i + batch, count)
            for copy in copies[3 * i : 3 * stop]:
                copy.wait()
            deep = slice(i * depth, stop * depth)
            for j, out in enumerate((own_out, peer_out)):
                part = jnp.dot(
                    left[j * tokens : (j + 1) * tokens, deep],
                    right[deep],
                    preferred_element_type=jnp.float32,
                )
                if i > 0:
                    out[...] += part
                elif start is None:
                    out[...] = part
                else:
                    out[...] = start_refs[j][...] + part

    anywhere = pl.BlockSpec(memory_space=pl.ANY)
    inside = pl.BlockSpec(memory_space=pltpu.VMEM)
    scalar = pl.BlockSpec(memory_space=pltpu.SMEM)
    total = jax.ShapeDtypeStruct((tokens, columns), jnp.float32)
    return pl.pallas_call(
        kernel,
        out_shape=(total, total),
        in_specs=[scalar, scalar]
        + [anywhere] * (2 + count)
        + [inside] * (0 if start is None else 2),
        out_specs=(inside, inside),
        scratch_shapes=[
            pltpu.VMEM((2 * tokens, count * depth), jnp.bfloat16),
            pltpu.VMEM((count * depth, columns), jnp.bfloat16),
            pltpu.SemaphoreType.DMA((3 * count,)),
        ],
        compiler_params=pltpu.CompilerParams(vmem_limit_bytes=48 * MIB),
        cost_estimate=pl.CostEstimate(
            flops=4 * count * tokens * depth * columns,
            bytes_accessed=count * (4 * tokens * depth + 2 * depth * columns),
            transcendentals=0,
        ),
    )(core, blocks, own_states, peer_states, *pieces, *(() if start is None else start))


def finish(own_part, peer_part, bias, cosines, sines, destination, live_rows, replicas):
    tokens, columns = own_part.shape
    keys = columns // 2
    rows = replicas * SPAN

    def kernel(own_ref, peer_ref, bias_ref, cos_ref, sin_ref, dest_ref, live_ref, kv_ref, key_ref, out_ref):
        kv = (own_ref[...] + peer_ref[...] + bias_ref[...]).astype(jnp.bfloat16)
        kv = jnp.where(live_ref[...] > 0.5, kv.astype(jnp.float32), 0.0)
        kept = kv.astype(jnp.bfloat16)
        kv_ref[...] = kept
        row = lax.broadcasted_iota(jnp.int32, (rows, tokens), 0)
        token = lax.broadcasted_iota(jnp.int32, (rows, tokens), 1)
        match = (dest_ref[...] == row // SPAN) & (token % SPAN == row % SPAN)
        pick = jnp.where(match, 1.0, 0.0)
        found = jnp.sum(pick, axis=1, keepdims=True)
        spans = jnp.dot(pick.astype(jnp.bfloat16), kept, preferred_element_type=jnp.float32)
        out_ref[...] = jnp.where(found > 0.5, spans, ABSENT).astype(jnp.bfloat16)
        cosine = jnp.concatenate([cos_ref[...], cos_ref[...]], axis=1)
        sine = jnp.concatenate([-sin_ref[...], sin_ref[...]], axis=1)
        for head in range(keys // HEAD):
            part = kv[:, head * HEAD : (head + 1) * HEAD]
            turned = part * cosine + pltpu.roll(part, HEAD // 2, 1) * sine
            key_ref[:, head * HEAD : (head + 1) * HEAD] = turned.astype(jnp.bfloat16)

    return pl.pallas_call(
        kernel,
        out_shape=(
            jax.ShapeDtypeStruct((tokens, columns), jnp.bfloat16),
            jax.ShapeDtypeStruct((tokens, keys), jnp.bfloat16),
            jax.ShapeDtypeStruct((rows, columns), jnp.bfloat16),
        ),
        compiler_params=pltpu.CompilerParams(vmem_limit_bytes=16 * MIB),
        cost_estimate=pl.CostEstimate(
            flops=2 * rows * tokens * columns,
            bytes_accessed=10 * tokens * columns,
            transcendentals=0,
        ),
    )(own_part, peer_part, bias, cosines, sines, destination, live_rows)


def attend(half, flip, mask, live_rows, queries, keys, kv, context=None):
    tokens = queries.shape[0]
    heads = keys.shape[1] // HEAD
    width = queries.shape[1] // (2 * heads)

    def kernel(half_ref, mask_ref, live_ref, query_ref, key_ref, value_ref, *refs):
        context_ref = refs[-1]
        scale = HEAD**-0.5 * math.log2(math.e)
        lanes = [slice(h * HEAD, (h + 1) * HEAD) for h in range(width // HEAD)]
        scores = [
            lax.dot_general(
                query_ref[:, lane],
                key_ref[...],
                (((1,), (1,)), ((), ())),
                preferred_element_type=jnp.float32,
            )
            for lane in lanes
        ]
        weights = []
        for score in scores:
            score = score * scale + mask_ref[...]
            weight = jnp.exp2(score - jnp.max(score, axis=1, keepdims=True))
            inverse = 1.0 / jnp.sum(weight, axis=1, keepdims=True)
            weights.append((weight * inverse).astype(jnp.bfloat16))
        is_live = live_ref[...] > 0.5
        for lane, weight in zip(lanes, weights):
            mixed = jnp.dot(weight, value_ref[...], preferred_element_type=jnp.float32)
            context_ref[:, lane] = jnp.where(is_live, mixed, 0.0).astype(jnp.bfloat16)

    def wide_at(i, s):
        return (0, (1 - s[0] if flip else s[0]) * heads + i)

    in_specs = [
        pl.BlockSpec((tokens, tokens), lambda i, s: (0, 0)),
        pl.BlockSpec((tokens, 1), lambda i, s: (0, 0)),
        pl.BlockSpec((tokens, width), wide_at),
        pl.BlockSpec((tokens, HEAD), lambda i, s: (0, i)),
        pl.BlockSpec((tokens, HEAD), lambda i, s: (0, heads + i)),
    ]
    arguments = [half, mask, live_rows, queries, keys, kv]
    if context is not None:
        in_specs.append(pl.BlockSpec(memory_space=pl.ANY))
        arguments.append(context)
    return pl.pallas_call(
        kernel,
        out_shape=jax.ShapeDtypeStruct(queries.shape, jnp.bfloat16),
        grid_spec=pltpu.PrefetchScalarGridSpec(
            num_scalar_prefetch=1,
            grid=(heads,),
            in_specs=in_specs,
            out_specs=pl.BlockSpec((tokens, width), wide_at),
        ),
        input_output_aliases={} if context is None else {6: 0},
        compiler_params=pltpu.CompilerParams(vmem_limit_bytes=32 * MIB),
        cost_estimate=pl.CostEstimate(
            flops=4 * tokens * tokens * heads * width,
            bytes_accessed=4 * tokens * heads * width,
            transcendentals=tokens * tokens * heads * width // HEAD,
        ),
    )(*arguments)


def place(half, kept_count, keep_rows, mine, other, mine_spans, other_spans):
    rows = WORK * SPAN
    slots, columns = mine_spans.shape
    part = columns // 2

    def kernel(half_ref, kept_ref, keep_ref, mine_ref, other_ref, mine_in, other_in, out_ref):
        present = jnp.where(other_in[:, :HEAD].astype(jnp.float32) > 0.5 * ABSENT, 0.0, 1.0)
        row = lax.broadcasted_iota(jnp.int32, (slots, slots), 0)
        column = lax.broadcasted_iota(jnp.int32, (slots, slots), 1)
        before = (column // SPAN < row // SPAN) & (column % SPAN == 0)
        before = jnp.where(before, 1.0, 0.0).astype(jnp.bfloat16)
        earlier = jnp.dot(
            before, present.astype(jnp.bfloat16), preferred_element_type=jnp.float32
        )
        rank = earlier[:, :1].astype(jnp.int32) + kept_ref[0]
        work = lax.broadcasted_iota(jnp.int32, (slots, rows), 1)
        sender = lax.broadcasted_iota(jnp.int32, (slots, rows), 0)
        hit = (work // SPAN == rank) & (work % SPAN == sender % SPAN) & (present[:, :1] > 0.5)
        hit = jnp.where(hit, 1.0, 0.0).astype(jnp.bfloat16)
        keep = keep_ref[...] > 0.5
        own = half_ref[0]
        for home, spans, which in ((mine_ref, mine_in, own), (other_ref, other_in, 1 - own)):
            moved = lax.dot_general(
                hit, spans[...], (((0,), (0,)), ((), ())), preferred_element_type=jnp.float32
            )
            total = jnp.where(keep, home[...].astype(jnp.float32), moved).astype(jnp.bfloat16)
            out_ref[:, pl.ds(pl.multiple_of(which * part, HEAD), part)] = total[:, :part]
            out_ref[:, pl.ds(pl.multiple_of((2 + which) * part, HEAD), part)] = total[:, part:]

    inside = pl.BlockSpec(memory_space=pltpu.VMEM)
    scalar = pl.BlockSpec(memory_space=pltpu.SMEM)
    home_rows = pl.BlockSpec((rows, columns), lambda i: (0, 0))
    whole = pl.BlockSpec((slots, columns), lambda i: (0, 0))
    return pl.pallas_call(
        kernel,
        grid=(1,),
        out_shape=jax.ShapeDtypeStruct((rows, 2 * columns), jnp.bfloat16),
        in_specs=[
            scalar,
            scalar,
            pl.BlockSpec((rows, 1), lambda i: (0, 0)),
            home_rows,
            home_rows,
            whole,
            whole,
        ],
        out_specs=pl.BlockSpec((rows, 2 * columns), lambda i: (0, 0)),
        compiler_params=pltpu.CompilerParams(vmem_limit_bytes=16 * MIB),
        cost_estimate=pl.CostEstimate(
            flops=4 * rows * slots * columns,
            bytes_accessed=8 * rows * columns,
            transcendentals=0,
        ),
    )(half, kept_count, keep_rows, mine, other, mine_spans, other_spans)


def per_device(states, queries, kv_weight, kv_bias, lengths, bounds, balance):
    replicas = lax.axis_size("dp")
    own_index = lax.axis_index("dp")
    half = (lax.axis_index("group") % 2).astype(jnp.int32)[None]
    core = (own_index % 2).astype(jnp.int32)[None]
    own_y = own_index // 2 % 2
    own_z = own_index // 4
    ring = replicas // 4
    position = jnp.where(own_z % 2 == 0, own_z // 2, ring - 1 - own_z // 2)
    tokens = states.shape[0]
    depth, width = kv_weight.shape
    quarter = width // 4

    def block(offset, across):
        z = ring_place(ring, (position - offset + ring) % ring)
        return (z * 2 + (1 - own_y if across else own_y)).astype(jnp.int32)

    token_ids = jnp.arange(tokens, dtype=jnp.int32)
    is_live = token_ids < lengths[0] * SPAN
    owner = jnp.repeat(balance[0], SPAN)
    is_moved = is_live & (owner != own_index)
    destination = jnp.where(is_moved, owner, -1)[None, :]
    live_rows = is_live.astype(jnp.float32)[:, None]
    keep = is_live & jnp.logical_not(is_moved)
    keep_rows = keep.astype(jnp.float32)[:, None]
    kept_count = (jnp.sum(keep.astype(jnp.int32)) // SPAN)[None]
    chosen, rejected = bounds[0, 0], bounds[0, 1]
    segment = (token_ids >= chosen).astype(jnp.int32) + (token_ids >= rejected).astype(jnp.int32)
    place_ids = jnp.where(token_ids >= rejected, token_ids - (rejected - chosen), token_ids)
    target, source = token_ids[:, None], token_ids[None, :]
    near = (segment[None, :] == segment[:, None]) | (segment[None, :] == 0)
    allowed = ((source <= target) & is_live[None, :] & near) | (source == target)
    mask = jnp.where(allowed, 0.0, MASKED).astype(jnp.float32)
    frequency = jnp.exp(
        jnp.arange(HEAD // 2, dtype=jnp.float32) * (-2.0 * math.log(1000000.0) / HEAD)
    )
    angles = place_ids.astype(jnp.float32)[:, None] * frequency[None, :]
    cosines, sines = jnp.cos(angles), jnp.sin(angles)
    plan = (cosines, sines, destination, live_rows, keep_rows, kept_count, mask)

    links = Links(replicas, lax.axis_size("group"))
    mine_weight, other_weight = halves(kv_weight, half)
    peer_states = core_swap(core_columns(states, 1 - core, depth), replicas)

    def project(pieces, start=None):
        blocks = jnp.stack([b for _, b in pieces])
        return multiply(states, peer_states, core, [p for p, _ in pieces], blocks, start)

    fore = ring // 2
    order = [k for j in range(1, ring) for k in (j, -j)][: ring - 1]
    held = {0: mine_weight}
    mine = [(mine_weight, block(0, False))]
    other = [(other_weight, block(0, False))]
    middle, late = [], []
    crossed = links.send(mine_weight, "y")
    mine.append((crossed, block(0, True)))
    moving = other_weight
    for k in order:
        final = k == order[-1]
        nearer = held[k - 1] if k > 0 else held[k + 1]
        held[k] = links.send(nearer, "fore" if k > 0 else "back", plan if final else ())
        mine.append((held[k], block(k, False)))
        crossed = links.send(held[k], "y")
        if 1 <= k < fore:
            other.append((links.send(held[k], "x"), block(k, False)))
        if final:
            mine_part = project(mine)
            other_part = project(other)
            for j in range(1, ring - fore):
                moving = links.send(moving, "back")
                middle.append((moving, block(-j, False)))
            ready = (*mine_part, *other_part)
            moving = links.send(moving, "back", ready)
            late.append((moving, block(fore - ring, False)))
            late.append((links.send(other_weight, "y", ready), block(0, True)))
            late.append((links.send(crossed, "x", ready), block(k, True)))
            mine_own, mine_peer = project([(crossed, block(k, True))], mine_part)
        else:
            mine.append((crossed, block(k, True)))
            piece = (links.send(crossed, "x"), block(k, True))
            (middle if k == order[-2] else other).append(piece)

    def complete(own_part, peer_part, flip):
        which = 1 - half[0] if flip else half[0]
        bias = jnp.concatenate(
            [
                lax.dynamic_slice_in_dim(kv_bias, (2 * j + which) * quarter, quarter)
                for j in range(2)
            ]
        )
        peer_part = core_swap(peer_part, replicas)
        return finish(own_part, peer_part, bias[None, :], *plan[:4], replicas)

    def exchange(spans):
        spans = spans.reshape(replicas, SPAN, width // 2)
        spans = lax.all_to_all(spans, "dp", split_axis=0, concat_axis=0, tiled=True)
        return spans.reshape(replicas * SPAN, width // 2)

    mine_kv, mine_keys, mine_spans = complete(mine_own, mine_peer, False)
    mine_spans = exchange(mine_spans)
    other_part = project(middle, other_part)
    late = [(after(p, mine_kv, *other_part), b) for p, b in late]
    other_kv, other_keys, other_spans = complete(*project(late, other_part), True)
    other_spans = exchange(other_spans)
    context = attend(half, False, mask, live_rows, queries, mine_keys, mine_kv)
    context = attend(half, True, mask, live_rows, queries, other_keys, other_kv, context)
    work_rows = place(
        half, kept_count, keep_rows, mine_kv, other_kv, mine_spans, other_spans
    )
    return (context, work_rows)


def solution(mesh):
    in_specs = (
        P(("group", "dp"), None),
        P(("group", "dp"), None),
        P("dp", None),
        P(),
        P(("group", "dp")),
        P(("group", "dp"), None),
        P(("group", "dp"), None),
    )
    out_specs = (P(("group", "dp"), None), P(("group", "dp"), None))
    return jax.shard_map(
        per_device, mesh=mesh, in_specs=in_specs, out_specs=out_specs, check_vma=False
    )
```

time: 126 us -> 214 us (1.70)
  Pallas kernels: 35.2 us -> 125 us
  local copies, waits for them, and re-layouts: 10.9 us -> 19.7 us
  waiting for transfers between devices: 39.3 us -> 32.6 us
  other arithmetic: 7.62 us -> 5.36 us
    pallas_call x4 -> x7, Pallas kernels: 12.9 us -> 114 us  [the longest x1 64.7 us: core_columns(): pl.pallas_call(kernel, out_shape=jax.ShapeDtypeStruct((tokens, width // 2...]
    unnamed x30 -> x62, local copies, waits for them, and re-layouts: 6.5 us -> 18.6 us
    pallas_call x2, Pallas kernels: 18 us -> 6.1 us  [attend(): pl.pallas_call(kernel, out_shape=jax.ShapeDtypeStruct(queries.shape, jnp....]
    ppermute x14, waiting for transfers between devices: 36.2 us -> 26.7 us  [send(): self.last[link] = lax.ppermute(after(value, *before), axis, pairs)]
    all_to_all x2, waiting for transfers between devices: 3.13 us -> 5.84 us  [exchange(): spans = lax.all_to_all(spans, 'dp', split_axis=0, concat_axis=0, tiled=True)]
    another operation x2 -> x0, other arithmetic: 2.63 us -> none  [scalars(): return jnp.stack([which, live_tokens, chosen, rejected]).astype(jnp.int32)]
    dynamic_slice x2 -> x1, local copies, waits for them, and re-layouts: 2.64 us -> 0.08 us  [complete(): lax.dynamic_slice_in_dim(kv_bias, (2 * j + which) * quarter, quarter)]
    concatenate x5 -> x2, other arithmetic: 2.49 us -> 0.02 us  [complete(): jnp.concatenate([lax.dynamic_slice_in_dim(kv_bias, (2 * j + which) * quar...]
  transfers between devices with their start and end apart: 19 -> 19, of which waited for: 8 -> 6; matrix products, arithmetic and copies ran while one was open for 10% -> 3% of each run, Pallas kernels for 26% -> 40%
where the time goes in v2:
time: 214 us; the launch traced here: 213 us
  Pallas kernels  125 us (58%)
  waiting for transfers between devices  32.6 us (15%)
  starting transfers between devices  24.9 us (12%)
  local copies, waits for them, and re-layouts  19.7 us (9%)
  between operations  5.39 us (3%)
  other arithmetic  5.36 us (3%)
    pallas_call x1, Pallas kernels, core_columns(): pl.pallas_call(kernel, out_shape=jax.ShapeDtypeStruct((tokens, width // 2...  64.7 us
    pallas_call x1, Pallas kernels, halves(): pl.pallas_call(kernel, out_shape=(out, out), in_specs=[pl.BlockSpec(memor...  32.9 us
    ppermute x14, waiting for transfers between devices, send(): self.last[link] = lax.ppermute(after(value, *before), axis, pairs)  26.7 us
    unnamed x62, local copies, waits for them, and re-layouts  18.6 us
    ppermute x14, starting transfers between devices, send(): self.last[link] = lax.ppermute(after(value, *before), axis, pairs)  17.1 us
    pallas_call x5, Pallas kernels, multiply(): pl.pallas_call(kernel, out_shape=(total, total), in_specs=[scalar, scalar...  16.7 us
    all_to_all x2, starting transfers between devices, exchange(): spans = lax.all_to_all(spans, 'dp', split_axis=0, concat_axis=0, tiled=True)  7.69 us
    pallas_call x2, Pallas kernels, attend(): pl.pallas_call(kernel, out_shape=jax.ShapeDtypeStruct(queries.shape, jnp....  6.1 us
  transfers between devices with their start and end apart: 19, of which 6 were waited for; matrix products, arithmetic and copies ran while one was open for 3% of the time, Pallas kernels for 40%

profile of v2, /device:TPU:0, one launch (start us, length us, event | category | flops | bytes accessed | tf_op | source)
XLA Modules:
  0.0 212.8 jit_solution(14123605649233142033)
XLA Ops:
  0.6 32.9 %shard_map.87 = (bf16[512,512]{1,0:T(8,128)(2,1)}, bf16[512,512]{1,0:T(8,128)(2,1)}) custom-call(s32[1]{0:T(128)} %bitcast.half_ref, bf16[512,1024]{1,0:T(8,128)(2,1)} %weight_ref.1), custom_call_target="tpu_custom_call" | custom-call | bytes 2097152 | tf_op jit(solution)/shard_map/pallas_call | solution.py:82
  33.6 4.1 %collective-permute-start.1 = (bf16[512,512]{1,0:T(8,128)(2,1)}, bf16[512,512]{1,0:T(8,128)(2,1)}, u32[]{:S(2)}, u32[]{:S(2)}) collective-permute-start(bf16[512,512]{1,0:T(8,128)(2,1)} %get-tuple-element.36.refs_0_), channel_id=1, source_target_pairs={{0,8},{1,9},{2,10},{3,11},{4,0},{5,1},{6,2},{7,3},{8,12},{9,13},{1... | collective-permute-start | bytes 1572872 | tf_op jit(solution)/shard_map/ppermute | solution.py:50
  37.6 1.5 collective-permute-start.5
  39.2 64.7 %shard_map.86 = bf16[256,4096]{1,0:T(8,128)(2,1)} custom-call(s32[1]{0:T(128)S(6)} %sub.92.core_ref, bf16[256,8192]{1,0:T(8,128)(2,1)} %own_ref.9), custom_call_target="tpu_custom_call" | custom-call | bytes 4194304 | tf_op jit(solution)/shard_map/pallas_call | solution.py:115
  115.0 1.6 collective-permute-start.8
  116.7 11.9 %collective-permute-done.2.refs_4_ = bf16[512,512]{1,0:T(8,128)(2,1)S(1)} collective-permute-done((bf16[512,512]{1,0:T(8,128)(2,1)}, bf16[512,512]{1,0:T(8,128)(2,1)S(1)}, u32[]{:S(2)}, u32[]{:S(2)}) %collective-permute-start.2) | collective-permute-done | bytes 524320 | tf_op jit(solution)/shard_map/ppermute | solution.py:50
  131.4 1.5 collective-permute-start.9
  133.7 8.7 %collective-permute-done.3.refs_6_ = bf16[512,512]{1,0:T(8,128)(2,1)} collective-permute-done((bf16[512,512]{1,0:T(8,128)(2,1)}, bf16[512,512]{1,0:T(8,128)(2,1)}, u32[]{:S(2)}, u32[]{:S(2)}) %collective-permute-start.3) | collective-permute-done | bytes 524320 | tf_op jit(solution)/shard_map/ppermute | solution.py:50
  145.3 1.5 collective-permute-start.13
  151.4 4.7 %shard_map.88 = (f32[256,512]{1,0:T(8,128)S(1)}, f32[256,512]{1,0:T(8,128)S(1)}) custom-call(s32[1]{0:T(128)} %bitcast.4.core_ref, s32[7]{0:T(128)S(1)} %stack.56.block_ref, bf16[256,8192]{1,0:T(8,128)(2,1)} %own_ref.9, bf16[256,4096]{1,0:T(8,128)(2,1)} %copy-done, bf16[512,512]{1,0:T(8,128)(2,1)S(1)} %copy-done.5, ...), custom_call_target="tpu_custom_call" | custom-call | flops 1879048192 | bytes 7340032 | tf_op jit(solution)/shard_map/pallas_call | solution.py:181
  156.2 1.6 copy-done.1
  157.8 2.5 %shard_map.90 = (f32[256,512]{1,0:T(8,128)S(1)}, f32[256,512]{1,0:T(8,128)}) custom-call(s32[1]{0:T(128)} %bitcast.4.core_ref, s32[1]{0:T(128)} %bitcast.7.block_ref, bf16[256,8192]{1,0:T(8,128)(2,1)} %own_ref.9, bf16[256,4096]{1,0:T(8,128)(2,1)S(1)} %copy-done.1, bf16[512,512]{1,0:T(8,128)(2,1)} %collective-permute-done.11.refs_0_, ...), custom_call_target="tpu_custom_call" | custom-call | flops 268435456 | bytes 1048576 | tf_op jit(solution)/shard_map/pallas_call | solution.py:181
  160.4 2.8 %shard_map.89 = (f32[256,512]{1,0:T(8,128)S(1)}, f32[256,512]{1,0:T(8,128)S(1)}) custom-call(s32[1]{0:T(128)} %bitcast.4.core_ref, s32[3]{0:T(128)S(1)} %pad_add_fusion.1.block_ref, bf16[256,8192]{1,0:T(8,128)(2,1)} %own_ref.9, bf16[256,4096]{1,0:T(8,128)(2,1)S(1)} %copy-done.2, bf16[512,512]{1,0:T(8,128)(2,1)S(1)} %copy-done.4, ...), custom_call_target="tpu_custom_call" | custom-call | flops 805306368 | bytes 3145728 | tf_op jit(solution)/shard_map/pallas_call | solution.py:181
  166.0 1.5 collective-permute-start.14
  170.4 2.7 %shard_map.92 = (f32[256,512]{1,0:T(8,128)S(1)}, f32[256,512]{1,0:T(8,128)S(1)}) custom-call(s32[1]{0:T(128)} %bitcast.4.core_ref, s32[2]{0:T(128)S(1)} %pad_add_fusion.2.block_ref, bf16[256,8192]{1,0:T(8,128)(2,1)} %own_ref.9, bf16[256,4096]{1,0:T(8,128)(2,1)S(1)} %copy-done.2, bf16[512,512]{1,0:T(8,128)(2,1)} %collective-permute-done.13.refs_0_, ...), custom_call_target="tpu_custom_call" | custom-call | flops 536870912 | bytes 2097152 | tf_op jit(solution)/shard_map/pallas_call | solution.py:181
  175.8 4.6 %collective-permute-done.10.refs_0_ = bf16[512,512]{1,0:T(8,128)(2,1)} collective-permute-done((bf16[512,512]{1,0:T(8,128)(2,1)}, bf16[512,512]{1,0:T(8,128)(2,1)}, u32[]{:S(2)}, u32[]{:S(2)}) %collective-permute-start.10) | collective-permute-done | bytes 524320 | tf_op jit(solution)/shard_map/ppermute | solution.py:50
  181.6 4.0 %shard_map.93 = (f32[256,512]{1,0:T(8,128)S(1)}, f32[256,512]{1,0:T(8,128)}) custom-call(s32[1]{0:T(128)} %bitcast.4.core_ref, s32[3]{0:T(128)S(1)} %pad_add_fusion.block_ref, bf16[256,8192]{1,0:T(8,128)(2,1)} %own_ref.9, bf16[256,4096]{1,0:T(8,128)(2,1)S(1)} %copy-done.2, bf16[512,512]{1,0:T(8,128)(2,1)} %collective-permute-done.10.refs_0_, ...), custom_call_target="tpu_custom_call" | custom-call | flops 805306368 | bytes 3145728 | tf_op jit(solution)/shard_map/pallas_call | solution.py:181
  186.4 3.5 %all-to-all-start = ((bf16[16,8,512]{2,1,0:T(8,128)(2,1)}), bf16[16,8,512]{2,1,0:T(8,128)(2,1)S(1)}, u32[]{:S(2)}, u32[]{:S(2)}) async-start(bf16[16,8,512]{2,1,0:T(8,128)(2,1)} %bitcast.24), calls=%async_computation | async-start | bytes 262144 | tf_op jit(solution)/shard_map/all_to_all | solution.py:455
  192.0 5.8 %all-to-all-done = bf16[16,8,512]{2,1,0:T(8,128)(2,1)S(1)} async-done(((bf16[16,8,512]{2,1,0:T(8,128)(2,1)}), bf16[16,8,512]{2,1,0:T(8,128)(2,1)S(1)}, u32[]{:S(2)}, u32[]{:S(2)}) %all-to-all-start) | async-done | bytes 131104 | tf_op jit(solution)/shard_map/all_to_all | solution.py:455
  197.8 4.2 %all-to-all-start.1 = ((bf16[16,8,512]{2,1,0:T(8,128)(2,1)}), bf16[16,8,512]{2,1,0:T(8,128)(2,1)}, u32[]{:S(2)}, u32[]{:S(2)}) async-start(bf16[16,8,512]{2,1,0:T(8,128)(2,1)} %bitcast.20), calls=%async_computation.1 | async-start | bytes 262144 | tf_op jit(solution)/shard_map/all_to_all | solution.py:455
  202.1 1.6 copy-done.3
  204.5 3.0 %shard_map.95.refs_0_ = bf16[256,4096]{1,0:T(8,128)(2,1)} custom-call(s32[1]{0:T(128)} %bitcast.half_ref, f32[256,256]{1,0:T(8,128)S(1)} %fusion.3.mask_ref, f32[256,1]{1,0:T(8,128)S(1)} %fusion.6.live_ref, bf16[256,4096]{1,0:T(8,128)(2,1)S(1)} %copy-done.3, bf16[256,256]{1,0:T(8,128)(2,1)S(1)} %copy-done.26, ...), custom_call_target="tpu_custom_call" | custom-call | flops 536870912 | bytes 2097152 | tf_op jit(solution)/shard_map/pallas_call | solution.py:285
  207.6 3.1 %shard_map.96 = bf16[256,4096]{1,0:T(8,128)(2,1)} custom-call(s32[1]{0:T(128)} %bitcast.half_ref, f32[256,256]{1,0:T(8,128)S(1)} %fusion.3.mask_ref, f32[256,1]{1,0:T(8,128)S(1)} %fusion.6.live_ref, bf16[256,4096]{1,0:T(8,128)(2,1)S(1)} %copy-done.3, bf16[256,256]{1,0:T(8,128)(2,1)S(1)} %copy-done.24, ...), custom_call_target="tpu_custom_call", output_to_operand_aliasing={{}: (6, {})} | custom-call | flops 536870912 | bytes 2097152 | tf_op jit(solution)/shard_map/pallas_call | solution.py:285
  210.7 2.2 %shard_map.97 = bf16[192,1024]{1,0:T(8,128)(2,1)} custom-call(s32[1]{0:T(128)} %bitcast.half_ref, s32[1]{0:T(128)} %bitcast.9.kept_ref, f32[256,1]{1,0:T(8,128)S(1)} %copy-done.22, bf16[256,512]{1,0:T(8,128)(2,1)S(1)} %get-tuple-element.50.value_ref.mine_ref, bf16[256,512]{1,0:T(8,128)(2,1)S(1)} %get-tuple-element.62.value_ref.other_ref, ...), custom_call_target="tpu_custom_call" | custom-call | flops 50331648 | bytes 786432 | tf_op jit(solution)/shard_map/pallas_call | solution.py:337
  (111 shorter events, 31.3 us)
Async XLA Ops:
  33.6 79.5 %collective-permute-start.1 = (bf16[512,512]{1,0:T(8,128)(2,1)}, bf16[512,512]{1,0:T(8,128)(2,1)}, u32[]{:S(2)}, u32[]{:S(2)}) collective-permute-start(bf16[512,512]{1,0:T(8,128)(2,1)} %get-tuple-element.36.refs_0_), channel_id=1, source_target_pairs={{0,8},{1,9},{2,10},{3,11},{4,0},{5,1},{6,2},{7,3},{8,12},{9,13},{1... | collective-permute-start | bytes 1572872 | tf_op jit(solution)/shard_map/ppermute | solution.py:50
  37.6 75.5 %collective-permute-start.5 = (bf16[512,512]{1,0:T(8,128)(2,1)}, bf16[512,512]{1,0:T(8,128)(2,1)}, u32[]{:S(2)}, u32[]{:S(2)}) collective-permute-start(bf16[512,512]{1,0:T(8,128)(2,1)} %get-tuple-element.36.refs_0_), channel_id=1, source_target_pairs={{0,2},{1,3},{2,0},{3,1},{4,6},{5,7},{6,4},{7,5},{8,10},{9,11},{10,... | collective-permute-start | bytes 1572872 | tf_op jit(solution)/shard_map/ppermute | solution.py:50
  39.2 64.8 %copy-start.29 = (s32[1,2]{1,0:T(1,128)S(1)}, s32[1,2]{1,0:T(1,128)}, u32[]{:S(2)}) copy-start(s32[1,2]{1,0:T(1,128)} %param.12) | copy-start | bytes 28
  39.2 68.5 %copy-start.30 = (s32[1,32]{1,0:T(1,128)S(1)}, s32[1,32]{1,0:T(1,128)}, u32[]{:S(2)}) copy-start(s32[1,32]{1,0:T(1,128)} %param.13) | copy-start | bytes 388
  39.2 104.0 %copy-start.4 = (bf16[512,512]{1,0:T(8,128)(2,1)S(1)}, bf16[512,512]{1,0:T(8,128)(2,1)}, u32[]{:S(2)}) copy-start(bf16[512,512]{1,0:T(8,128)(2,1)} %get-tuple-element.55.refs_0_) | copy-start | bytes 1572868
  103.9 43.1 %collective-permute-start = (bf16[256,4096]{1,0:T(8,128)(2,1)}, bf16[256,4096]{1,0:T(8,128)(2,1)S(1)}, u32[]{:S(2)}, u32[]{:S(2)}) collective-permute-start(bf16[256,4096]{1,0:T(8,128)(2,1)} %shard_map.86), channel_id=1, source_target_pairs={{0,1},{1,0},{2,3},{3,2},{4,5},{5,4},{6,7},{7,6},{8,9},{9,8},{10,11... | collective-permute-start | bytes 6291464 | tf_op jit(solution)/shard_map/ppermute | solution.py:55
  113.1 15.5 %collective-permute-start.2 = (bf16[512,512]{1,0:T(8,128)(2,1)}, bf16[512,512]{1,0:T(8,128)(2,1)S(1)}, u32[]{:S(2)}, u32[]{:S(2)}) collective-permute-start(bf16[512,512]{1,0:T(8,128)(2,1)} %get-tuple-element.36.refs_0_), channel_id=1, source_target_pairs={{8,0},{9,1},{10,2},{11,3},{0,4},{1,5},{2,6},{3,7},{12,8},{13,9},{1... | collective-permute-start | bytes 1572872 | tf_op jit(solution)/shard_map/ppermute | solution.py:50
  113.2 16.1 %collective-permute-start.6 = (bf16[512,512]{1,0:T(8,128)(2,1)}, bf16[512,512]{1,0:T(8,128)(2,1)S(1)}, u32[]{:S(2)}, u32[]{:S(2)}) collective-permute-start(bf16[512,512]{1,0:T(8,128)(2,1)} %collective-permute-done.1.refs_2_), channel_id=1, source_target_pairs={{0,2},{1,3},{2,0},{3,1},{4,6},{5,7},{6,4},{7,5},{8,10},{9,11},{10,... | collective-permute-start | bytes 1572872 | tf_op jit(solution)/shard_map/ppermute | solution.py:50
  115.0 15.6 %collective-permute-start.8 = (bf16[512,512]{1,0:T(8,128)(2,1)}, bf16[512,512]{1,0:T(8,128)(2,1)S(1)}, u32[]{:S(2)}, u32[]{:S(2)}) collective-permute-start(bf16[512,512]{1,0:T(8,128)(2,1)} %collective-permute-done.1.refs_2_), channel_id=1, source_target_pairs={{0,16},{16,0},{1,17},{17,1},{2,18},{18,2},{3,19},{19,3},{4,20},{20... | collective-permute-start | bytes 1572872 | tf_op jit(solution)/shard_map/ppermute | solution.py:50
  128.6 13.9 %collective-permute-start.3 = (bf16[512,512]{1,0:T(8,128)(2,1)}, bf16[512,512]{1,0:T(8,128)(2,1)}, u32[]{:S(2)}, u32[]{:S(2)}) collective-permute-start(bf16[512,512]{1,0:T(8,128)(2,1)} %collective-permute-done.1.refs_2_), channel_id=1, source_target_pairs={{0,8},{1,9},{2,10},{3,11},{4,0},{5,1},{6,2},{7,3},{8,12},{9,13},{1... | collective-permute-start | bytes 1572872 | tf_op jit(solution)/shard_map/ppermute | solution.py:50
  129.3 13.4 %collective-permute-start.7 = (bf16[512,512]{1,0:T(8,128)(2,1)S(1)}, bf16[512,512]{1,0:T(8,128)(2,1)}, u32[]{:S(2)}, u32[]{:S(2)}) collective-permute-start(bf16[512,512]{1,0:T(8,128)(2,1)S(1)} %collective-permute-done.2.refs_4_), channel_id=1, source_target_pairs={{0,2},{1,3},{2,0},{3,1},{4,6},{5,7},{6,4},{7,5},{8,10},{9,11},{10,... | collective-permute-start | bytes 1572872 | tf_op jit(solution)/shard_map/ppermute | solution.py:50
  131.4 13.1 %collective-permute-start.9 = (bf16[512,512]{1,0:T(8,128)(2,1)S(1)}, bf16[512,512]{1,0:T(8,128)(2,1)S(1)}, u32[]{:S(2)}, u32[]{:S(2)}) collective-permute-start(bf16[512,512]{1,0:T(8,128)(2,1)S(1)} %collective-permute-done.6.refs_3_), channel_id=1, source_target_pairs={{0,16},{16,0},{1,17},{17,1},{2,18},{18,2},{3,19},{19,3},{4,20},{20... | collective-permute-start | bytes 1572872 | tf_op jit(solution)/shard_map/ppermute | solution.py:50
  142.6 13.5 %collective-permute-start.11 = (bf16[512,512]{1,0:T(8,128)(2,1)}, bf16[512,512]{1,0:T(8,128)(2,1)}, u32[]{:S(2)}, u32[]{:S(2)}) collective-permute-start(bf16[512,512]{1,0:T(8,128)(2,1)} %collective-permute-done.3.refs_6_), channel_id=1, source_target_pairs={{0,2},{1,3},{2,0},{3,1},{4,6},{5,7},{6,4},{7,5},{8,10},{9,11},{10,... | collective-permute-start | bytes 1572872 | tf_op jit(solution)/shard_map/ppermute | solution.py:50
  143.1 21.7 %collective-permute-start.4 = (bf16[512,512]{1,0:T(8,128)(2,1)S(1)}, bf16[512,512]{1,0:T(8,128)(2,1)}, u32[]{:S(2)}, u32[]{:S(2)}) collective-permute-start(bf16[512,512]{1,0:T(8,128)(2,1)S(1)} %copy-done.4), channel_id=1, source_target_pairs={{8,0},{9,1},{10,2},{11,3},{0,4},{1,5},{2,6},{3,7},{12,8},{13,9},{1... | collective-permute-start | bytes 1572872 | tf_op jit(solution)/shard_map/ppermute | solution.py:50
  145.3 22.3 %collective-permute-start.13 = (bf16[512,512]{1,0:T(8,128)(2,1)}, bf16[512,512]{1,0:T(8,128)(2,1)}, u32[]{:S(2)}, u32[]{:S(2)}) collective-permute-start(bf16[512,512]{1,0:T(8,128)(2,1)} %collective-permute-done.7.refs_5_), channel_id=1, source_target_pairs={{0,16},{16,0},{1,17},{17,1},{2,18},{18,2},{3,19},{19,3},{4,20},{20... | collective-permute-start | bytes 1572872 | tf_op jit(solution)/shard_map/ppermute | solution.py:50
  160.3 8.0 %copy-start.28 = (f32[1024]{0:T(1024)S(1)}, f32[1024]{0:T(1024)}, u32[]{:S(2)}) copy-start(f32[1024]{0:T(1024)} %param.10) | copy-start | bytes 12292
  160.3 12.8 %collective-permute-start.12 = (f32[256,512]{1,0:T(8,128)}, f32[256,512]{1,0:T(8,128)}, u32[]{:S(2)}, u32[]{:S(2)}) collective-permute-start(f32[256,512]{1,0:T(8,128)} %get-tuple-element.49), channel_id=1, source_target_pairs={{0,1},{1,0},{2,3},{3,2},{4,5},{5,4},{6,7},{7,6},{8,9},{9,8},{10,11... | collective-permute-start | bytes 1572872 | tf_op jit(solution)/shard_map/ppermute | solution.py:55
  164.8 15.5 %collective-permute-start.10 = (bf16[512,512]{1,0:T(8,128)(2,1)}, bf16[512,512]{1,0:T(8,128)(2,1)}, u32[]{:S(2)}, u32[]{:S(2)}) collective-permute-start(bf16[512,512]{1,0:T(8,128)(2,1)} %collective-permute-done.4.refs_1_), channel_id=1, source_target_pairs={{8,0},{9,1},{10,2},{11,3},{0,4},{1,5},{2,6},{3,7},{12,8},{13,9},{1... | collective-permute-start | bytes 1572872 | tf_op jit(solution)/shard_map/ppermute | solution.py:50
  166.0 14.3 %collective-permute-start.14 = (bf16[512,512]{1,0:T(8,128)(2,1)S(1)}, bf16[512,512]{1,0:T(8,128)(2,1)}, u32[]{:S(2)}, u32[]{:S(2)}) collective-permute-start(bf16[512,512]{1,0:T(8,128)(2,1)S(1)} %copy-done.4), channel_id=1, source_target_pairs={{0,2},{1,3},{2,0},{3,1},{4,6},{5,7},{6,4},{7,5},{8,10},{9,11},{10,... | collective-permute-start | bytes 1572872 | tf_op jit(solution)/shard_map/ppermute | solution.py:50
  167.6 14.1 %collective-permute-start.15 = (bf16[512,512]{1,0:T(8,128)(2,1)}, bf16[512,512]{1,0:T(8,128)(2,1)}, u32[]{:S(2)}, u32[]{:S(2)}) collective-permute-start(bf16[512,512]{1,0:T(8,128)(2,1)} %collective-permute-done.11.refs_0_), channel_id=1, source_target_pairs={{0,16},{16,0},{1,17},{17,1},{2,18},{18,2},{3,19},{19,3},{4,20},{20... | collective-permute-start | bytes 1572872 | tf_op jit(solution)/shard_map/ppermute | solution.py:50
  186.4 3.5 %collective-permute-start.16 = (f32[256,512]{1,0:T(8,128)}, f32[256,512]{1,0:T(8,128)S(1)}, u32[]{:S(2)}, u32[]{:S(2)}) collective-permute-start(f32[256,512]{1,0:T(8,128)} %get-tuple-element.60), channel_id=1, source_target_pairs={{0,1},{1,0},{2,3},{3,2},{4,5},{5,4},{6,7},{7,6},{8,9},{9,8},{10,11... | collective-permute-start | bytes 1572872 | tf_op jit(solution)/shard_map/ppermute | solution.py:55
  186.4 11.4 %all-to-all-start = ((bf16[16,8,512]{2,1,0:T(8,128)(2,1)}), bf16[16,8,512]{2,1,0:T(8,128)(2,1)S(1)}, u32[]{:S(2)}, u32[]{:S(2)}) async-start(bf16[16,8,512]{2,1,0:T(8,128)(2,1)} %bitcast.24), calls=%async_computation | async-start | bytes 262144 | tf_op jit(solution)/shard_map/all_to_all | solution.py:455
  192.0 10.0 %copy-start.23 = (bf16[256,256]{1,0:T(8,128)(2,1)}, bf16[256,256]{1,0:T(8,128)(2,1)S(1)}, u32[]{:S(2)}) copy-start(bf16[256,256]{1,0:T(8,128)(2,1)S(1)} %get-tuple-element.61.key_ref) | copy-start | bytes 393220
  197.8 12.8 %all-to-all-start.1 = ((bf16[16,8,512]{2,1,0:T(8,128)(2,1)}), bf16[16,8,512]{2,1,0:T(8,128)(2,1)}, u32[]{:S(2)}, u32[]{:S(2)}) async-start(bf16[16,8,512]{2,1,0:T(8,128)(2,1)} %bitcast.20), calls=%async_computation.1 | async-start | bytes 262144 | tf_op jit(solution)/shard_map/all_to_all | solution.py:455
  (26 other events, 38.2 us)

commit v3 on v2

v3 whole, which is shorter than its diff:
```python
import math

import jax
import jax.numpy as jnp
from jax import lax
from jax.experimental import pallas as pl
from jax.experimental.pallas import tpu as pltpu
from jax.sharding import PartitionSpec as P

HEAD = 128
SPAN = 8
HOME = 32
WORK = 24
ABSENT = 1e30
MASKED = -1e30
LIMIT = 18 << 20
LIVE, DESTINATION, KEEP = HEAD, HEAD + 1, HEAD + 2


def ring_place(ring, position):
    return jnp.where(2 * position < ring, 2 * position, 2 * (ring - 1 - position) + 1)


def after(value, *before):
    return lax.optimization_barrier((value, *before))[0] if before else value


class Links:
    def __init__(self, replicas, groups):
        ring = replicas // 4
        places = [p for p in range(0, ring, 2)] + [p for p in range(1, ring, 2)][::-1]
        ahead = {places[i]: places[(i + 1) % ring] for i in range(ring)}
        steps = [
            ((z * 2 + y) * 2 + c, (ahead[z] * 2 + y) * 2 + c)
            for z in range(ring)
            for y in range(2)
            for c in range(2)
        ]
        self.routes = {
            "fore": ("z", "dp", steps),
            "back": ("z", "dp", [(d, s) for s, d in steps]),
            "y": ("y", "dp", [(i, i ^ 2) for i in range(replicas)]),
            "x": ("x", "group", [(i, i ^ 1) for i in range(groups)]),
        }
        self.last = {}

    def send(self, value, route, before=()):
        link, axis, pairs = self.routes[route]
        if link in self.last:
            before = (self.last[link], *before)
        self.last[link] = lax.ppermute(after(value, *before), axis, pairs)
        return self.last[link]


def core_swap(value, replicas):
    return lax.ppermute(value, "dp", [(i, i ^ 1) for i in range(replicas)])


def halves(weight, half):
    depth, width = weight.shape
    quarter = width // 4

    def kernel(half_ref, weight_ref, mine_ref, other_ref, sems):
        copies = []
        for i, out in enumerate((mine_ref, other_ref)):
            which = half_ref[0] if i == 0 else 1 - half_ref[0]
            for j in range(2):
                start = pl.multiple_of((2 * j + which) * quarter, HEAD)
                copies.append(
                    pltpu.make_async_copy(
                        weight_ref.at[:, pl.ds(start, quarter)],
                        out.at[:, pl.ds(j * quarter, quarter)],
                        sems.at[2 * i + j],
                    )
                )
        for copy in copies:
            copy.start()
        for copy in copies:
            copy.wait()

    anywhere = pl.BlockSpec(memory_space=pl.ANY)
    inside = pl.BlockSpec(memory_space=pltpu.VMEM)
    out = jax.ShapeDtypeStruct((depth, width // 2), weight.dtype)
    return pl.pallas_call(
        kernel,
        out_shape=(out, out),
        in_specs=[pl.BlockSpec(memory_space=pltpu.SMEM), anywhere],
        out_specs=(inside, inside),
        scratch_shapes=[pltpu.SemaphoreType.DMA((4,))],
        cost_estimate=pl.CostEstimate(
            flops=0, bytes_accessed=4 * depth * width, transcendentals=0
        ),
    )(half, weight)


def core_columns(states, core, depth):
    tokens, width = states.shape
    count = width // (2 * depth)

    def kernel(core_ref, states_ref, out_ref, sems):
        copies = []
        for i in range(count):
            start = pl.multiple_of((2 * i + core_ref[0]) * depth, HEAD)
            copies.append(
                pltpu.make_async_copy(
                    states_ref.at[:, pl.ds(start, depth)],
                    out_ref.at[:, pl.ds(i * depth, depth)],
                    sems.at[i],
                )
            )
        for copy in copies:
            copy.start()
        for copy in copies:
            copy.wait()

    anywhere = pl.BlockSpec(memory_space=pl.ANY)
    return pl.pallas_call(
        kernel,
        out_shape=jax.ShapeDtypeStruct((tokens, width // 2), states.dtype),
        in_specs=[pl.BlockSpec(memory_space=pltpu.SMEM), anywhere],
        out_specs=pl.BlockSpec(memory_space=pltpu.VMEM),
        scratch_shapes=[pltpu.SemaphoreType.DMA((count,))],
        cost_estimate=pl.CostEstimate(
            flops=0, bytes_accessed=2 * tokens * width, transcendentals=0
        ),
    )(core, states)


def accumulate(states, scalars, pieces, places, bias=None, start=None, later=0):
    count = len(pieces)
    depth, columns = pieces[0].shape
    tokens = states[0].shape[0]
    batch = 5
    begun = 4 if start is not None else 1

    def kernel(scalar_ref, *refs):
        state_refs, refs = refs[:2], refs[2:]
        piece_refs, refs = refs[:count], refs[count:]
        start_refs, refs = refs[:begun], refs[begun:]
        if later:
            totals, lefts, refs = refs[:4], refs[4:6], refs[6:]
        else:
            outs, totals, refs = refs[:4], refs[4:8], refs[8:]
        left, right, bias_ref, sems = refs
        used = 0

        def begin(source, target):
            nonlocal used
            copy = pltpu.make_async_copy(source, target, sems.at[used])
            copy.start()
            used += 1
            return copy

        def columns_at(side, index):
            at = scalar_ref[2 + index]
            at = 2 * at + scalar_ref[0] if side else at
            return state_refs[side].at[:, pl.ds(pl.multiple_of(at * depth, HEAD), depth)]

        waits = []
        if start is None:
            first = [begin(start_refs[0], bias_ref)]
        else:
            first = [begin(source, target) for source, target in zip(start_refs, totals)]
        for i in range(count):
            deep = pl.ds(i * depth, depth)
            waits.append(
                [begin(piece_refs[i], right.at[deep])]
                + [begin(columns_at(side, i), left.at[side, :, deep]) for side in range(2)]
            )
        rest = [
            begin(columns_at(side, count + i), lefts[side].at[:, pl.ds(i * depth, depth)])
            for i in range(later)
            for side in range(2)
        ]
        for copy in first:
            copy.wait()
        touched = [start is not None] * 4
        for i in range(0, count, batch):
            stop = min(i + batch, count)
            for copies in waits[i:stop]:
                for copy in copies:
                    copy.wait()
            for j in range(i, stop):
                deep = slice(j * depth, (j + 1) * depth)
                for side in range(2):
                    which = 2 * places[j] + side
                    part = jnp.dot(
                        left[side, :, deep], right[deep], preferred_element_type=jnp.float32
                    )
                    if touched[which]:
                        totals[which][...] += part
                    elif side == 0:
                        totals[which][...] = part
                    else:
                        own = scalar_ref[1] if places[j] == 0 else 1 - scalar_ref[1]
                        part_width = columns // 2
                        for k in range(2):
                            at = pl.multiple_of((2 * k + own) * part_width, HEAD)
                            lanes = slice(k * part_width, (k + 1) * part_width)
                            totals[which][:, lanes] = (
                                part[:, lanes] + bias_ref[:, pl.ds(at, part_width)]
                            )
                    touched[which] = True
        if not later:
            rest += [begin(source, target) for source, target in zip(totals, outs)]
        for copy in rest:
            copy.wait()

    outside = pl.BlockSpec(memory_space=pltpu.HBM)
    inside = pl.BlockSpec(memory_space=pltpu.VMEM)
    sums = (tokens, columns)
    if later:
        out_shape = [jax.ShapeDtypeStruct(sums, jnp.float32)] * 4
        out_shape += [jax.ShapeDtypeStruct((tokens, later * depth), jnp.bfloat16)] * 2
        out_specs, scratch = [inside] * 6, []
    else:
        out_shape = [pltpu.HBM(sums, jnp.float32)] * 4
        out_specs, scratch = [outside] * 4, [pltpu.VMEM(sums, jnp.float32)] * 4
    outer = [*states, *pieces, *((bias,) if start is None else start)]
    return pl.pallas_call(
        kernel,
        out_shape=out_shape,
        in_specs=[pl.BlockSpec(memory_space=pltpu.SMEM)] + [outside] * len(outer),
        out_specs=out_specs,
        scratch_shapes=scratch
        + [
            pltpu.VMEM((2, tokens, count * depth), jnp.bfloat16),
            pltpu.VMEM((count * depth, columns), jnp.bfloat16),
            pltpu.VMEM((1, 2 * columns), jnp.float32),
            pltpu.SemaphoreType.DMA((3 * count + 2 * later + 8,)),
        ],
        compiler_params=pltpu.CompilerParams(vmem_limit_bytes=LIMIT),
        cost_estimate=pl.CostEstimate(
            flops=4 * count * tokens * depth * columns,
            bytes_accessed=count * (4 * tokens * depth + 2 * depth * columns),
            transcendentals=0,
        ),
    )(scalars, *(pltpu.with_memory_space_constraint(a, pltpu.HBM) for a in outer))


def complete(left, pieces, total):
    depth = pieces[0].shape[0]

    def kernel(left_ref, total_ref, *refs):
        out_ref = refs[-1]
        for i, piece in enumerate(refs[:-1]):
            part = jnp.dot(
                left_ref[:, i * depth : (i + 1) * depth],
                piece[...],
                preferred_element_type=jnp.float32,
            )
            out_ref[...] = (total_ref if i == 0 else out_ref)[...] + part

    inside = pl.BlockSpec(memory_space=pltpu.VMEM)
    return pl.pallas_call(
        kernel,
        out_shape=jax.ShapeDtypeStruct(total.shape, total.dtype),
        in_specs=[inside] * (2 + len(pieces)),
        out_specs=inside,
        compiler_params=pltpu.CompilerParams(vmem_limit_bytes=LIMIT),
        cost_estimate=pl.CostEstimate(
            flops=2 * left.size * total.shape[1],
            bytes_accessed=2 * left.size,
            transcendentals=0,
        ),
    )(left, total, *pieces)


def finish(own_part, peer_part, table, replicas, earlier=None):
    tokens, columns = own_part.shape
    keys = columns // 2
    rows = replicas * SPAN

    def kernel(own_ref, peer_ref, table_in, *refs):
        kv_ref, key_ref, out_ref, table_ref, sem = refs[-5:]
        copy = pltpu.make_async_copy(table_in, table_ref, sem)
        copy.start()
        kv = (own_ref[...] + peer_ref[...]).astype(jnp.bfloat16).astype(jnp.float32)
        copy.wait()
        kv = jnp.where(table_ref[:, LIVE : LIVE + 1] > 0.5, kv, 0.0)
        kept = kv.astype(jnp.bfloat16)
        kv_ref[...] = kept
        destination = table_ref[:, DESTINATION : DESTINATION + 1].astype(jnp.int32)
        token = lax.broadcasted_iota(jnp.int32, (tokens, rows), 0)
        row = lax.broadcasted_iota(jnp.int32, (tokens, rows), 1)
        match = (destination == row // SPAN) & (token % SPAN == row % SPAN)
        pick = jnp.where(match, 1.0, 0.0).astype(jnp.bfloat16)
        over_tokens = (((0,), (0,)), ((), ()))
        found = lax.dot_general(
            pick,
            jnp.ones((tokens, HEAD), jnp.bfloat16),
            over_tokens,
            preferred_element_type=jnp.float32,
        )
        spans = lax.dot_general(pick, kept, over_tokens, preferred_element_type=jnp.float32)
        spans = jnp.where(found[:, :1] > 0.5, spans, ABSENT).astype(jnp.bfloat16)
        if earlier is None:
            out_ref[...] = spans
        else:
            out_ref[:, :columns] = refs[0][...]
            out_ref[:, columns:] = spans
        cosine, sine = table_ref[:, : HEAD // 2], table_ref[:, HEAD // 2 : HEAD]
        cosine = jnp.concatenate([cosine, cosine], axis=1)
        sine = jnp.concatenate([-sine, sine], axis=1)
        for head in range(keys // HEAD):
            part = kv[:, head * HEAD : (head + 1) * HEAD]
            turned = part * cosine + pltpu.roll(part, HEAD // 2, 1) * sine
            key_ref[:, head * HEAD : (head + 1) * HEAD] = turned.astype(jnp.bfloat16)

    inside = pl.BlockSpec(memory_space=pltpu.VMEM)
    sent = columns if earlier is None else 2 * columns
    more = () if earlier is None else (earlier,)
    return pl.pallas_call(
        kernel,
        out_shape=(
            jax.ShapeDtypeStruct((tokens, columns), jnp.bfloat16),
            jax.ShapeDtypeStruct((tokens, keys), jnp.bfloat16),
            jax.ShapeDtypeStruct((rows, sent), jnp.bfloat16),
        ),
        in_specs=[inside] * 2 + [pl.BlockSpec(memory_space=pltpu.HBM)] + [inside] * len(more),
        out_specs=(inside,) * 3,
        scratch_shapes=[pltpu.VMEM(table.shape, table.dtype), pltpu.SemaphoreType.DMA],
        compiler_params=pltpu.CompilerParams(vmem_limit_bytes=LIMIT),
        cost_estimate=pl.CostEstimate(
            flops=2 * rows * tokens * columns,
            bytes_accessed=10 * tokens * columns,
            transcendentals=0,
        ),
    )(own_part, peer_part, pltpu.with_memory_space_constraint(table, pltpu.HBM), *more)


def attend(half, flip, mask, table, queries, keys, kv, context=None):
    tokens = queries.shape[0]
    heads = keys.shape[1] // HEAD
    width = queries.shape[1] // (2 * heads)

    def kernel(half_ref, mask_ref, table_ref, query_ref, key_ref, value_ref, *refs):
        context_ref = refs[-1]
        scale = HEAD**-0.5 * math.log2(math.e)
        lanes = [slice(h * HEAD, (h + 1) * HEAD) for h in range(width // HEAD)]
        scores = [
            lax.dot_general(
                query_ref[:, lane],
                key_ref[...],
                (((1,), (1,)), ((), ())),
                preferred_element_type=jnp.float32,
            )
            for lane in lanes
        ]
        weights = []
        for score in scores:
            score = score * scale + mask_ref[...]
            weight = jnp.exp2(score - jnp.max(score, axis=1, keepdims=True))
            inverse = 1.0 / jnp.sum(weight, axis=1, keepdims=True)
            weights.append((weight * inverse).astype(jnp.bfloat16))
        is_live = table_ref[:, LIVE - HEAD : LIVE - HEAD + 1] > 0.5
        for lane, weight in zip(lanes, weights):
            mixed = jnp.dot(weight, value_ref[...], preferred_element_type=jnp.float32)
            context_ref[:, lane] = jnp.where(is_live, mixed, 0.0).astype(jnp.bfloat16)

    def wide_at(i, s):
        return (0, (1 - s[0] if flip else s[0]) * heads + i)

    in_specs = [
        pl.BlockSpec((tokens, tokens), lambda i, s: (0, 0)),
        pl.BlockSpec((tokens, HEAD), lambda i, s: (0, 1)),
        pl.BlockSpec((tokens, width), wide_at),
        pl.BlockSpec((tokens, HEAD), lambda i, s: (0, i)),
        pl.BlockSpec((tokens, HEAD), lambda i, s: (0, heads + i)),
    ]
    arguments = [half, mask, table, queries, keys, kv]
    if context is not None:
        in_specs.append(pl.BlockSpec(memory_space=pl.ANY))
        arguments.append(context)
    return pl.pallas_call(
        kernel,
        out_shape=jax.ShapeDtypeStruct(queries.shape, jnp.bfloat16),
        grid_spec=pltpu.PrefetchScalarGridSpec(
            num_scalar_prefetch=1,
            grid=(heads,),
            in_specs=in_specs,
            out_specs=pl.BlockSpec((tokens, width), wide_at),
        ),
        input_output_aliases={} if context is None else {6: 0},
        compiler_params=pltpu.CompilerParams(vmem_limit_bytes=LIMIT),
        cost_estimate=pl.CostEstimate(
            flops=4 * tokens * tokens * heads * width,
            bytes_accessed=4 * tokens * heads * width,
            transcendentals=tokens * tokens * heads * width // HEAD,
        ),
    )(*arguments)


def place(scalars, table, mine, other, spans):
    rows = WORK * SPAN
    slots, width = spans.shape
    part = width // 4

    def kernel(scalar_ref, table_ref, mine_ref, other_ref, spans_ref, out_ref, total_ref):
        @pl.when(pl.program_id(0) == 0)
        def _():
            present = spans_ref[:, :HEAD].astype(jnp.float32)
            present = jnp.where(present > 0.5 * ABSENT, 0.0, 1.0)
            row = lax.broadcasted_iota(jnp.int32, (slots, slots), 0)
            column = lax.broadcasted_iota(jnp.int32, (slots, slots), 1)
            before = (column // SPAN < row // SPAN) & (column % SPAN == 0)
            before = jnp.where(before, 1.0, 0.0).astype(jnp.bfloat16)
            earlier = jnp.dot(
                before, present.astype(jnp.bfloat16), preferred_element_type=jnp.float32
            )
            rank = earlier[:, :1].astype(jnp.int32) + scalar_ref[1]
            target = lax.broadcasted_iota(jnp.int32, (slots, rows), 1)
            sender = lax.broadcasted_iota(jnp.int32, (slots, rows), 0)
            hit = (target // SPAN == rank) & (target % SPAN == sender % SPAN)
            hit = jnp.where(hit & (present[:, :1] > 0.5), 1.0, 0.0).astype(jnp.bfloat16)
            moved = lax.dot_general(
                hit, spans_ref[...], (((0,), (0,)), ((), ())), preferred_element_type=jnp.float32
            ).astype(jnp.bfloat16)
            keep = table_ref[:, KEEP : KEEP + 1] > 0.5
            for i in range(4):
                home = (mine_ref, other_ref)[i // 2][:, (i % 2) * part : (i % 2 + 1) * part]
                home = home.astype(jnp.float32)
                came = moved[:, i * part : (i + 1) * part].astype(jnp.float32)
                total_ref[i] = jnp.where(keep, home, came).astype(jnp.bfloat16)

        out_ref[...] = total_ref[pl.program_id(0)]

    def out_at(i, s):
        return (0, 2 * (i % 2) + jnp.where(i < 2, s[0], 1 - s[0]))

    home = pl.BlockSpec((rows, width // 2), lambda i, s: (0, 0))
    return pl.pallas_call(
        kernel,
        out_shape=jax.ShapeDtypeStruct((rows, width), jnp.bfloat16),
        grid_spec=pltpu.PrefetchScalarGridSpec(
            num_scalar_prefetch=1,
            grid=(4,),
            in_specs=[
                pl.BlockSpec((rows, table.shape[1]), lambda i, s: (0, 0)),
                home,
                home,
                pl.BlockSpec((slots, width), lambda i, s: (0, 0)),
            ],
            out_specs=pl.BlockSpec((rows, part), out_at),
            scratch_shapes=[pltpu.VMEM((4, rows, part), jnp.bfloat16)],
        ),
        compiler_params=pltpu.CompilerParams(vmem_limit_bytes=LIMIT),
        cost_estimate=pl.CostEstimate(
            flops=2 * rows * slots * width,
            bytes_accessed=4 * rows * width,
            transcendentals=0,
        ),
    )(scalars, table, mine, other, spans)


def per_device(states, queries, kv_weight, kv_bias, lengths, bounds, balance):
    replicas = lax.axis_size("dp")
    own_index = lax.axis_index("dp")
    half = (lax.axis_index("group") % 2).astype(jnp.int32)[None]
    core = (own_index % 2).astype(jnp.int32)[None]
    own_y = own_index // 2 % 2
    own_z = own_index // 4
    ring = replicas // 4
    position = jnp.where(own_z % 2 == 0, own_z // 2, ring - 1 - own_z // 2)
    tokens = states.shape[0]
    depth, width = kv_weight.shape

    def block(offset, across):
        z = ring_place(ring, (position - offset + ring) % ring)
        return (z * 2 + (1 - own_y if across else own_y)).astype(jnp.int32)

    token_ids = jnp.arange(tokens, dtype=jnp.int32)
    is_live = token_ids < lengths[0] * SPAN
    owner = jnp.repeat(balance[0], SPAN)
    is_moved = is_live & (owner != own_index)
    destination = jnp.where(is_moved, owner, -1)
    keep = is_live & jnp.logical_not(is_moved)
    kept_count = jnp.sum(keep.astype(jnp.int32)) // SPAN
    chosen, rejected = bounds[0, 0], bounds[0, 1]
    segment = (token_ids >= chosen).astype(jnp.int32) + (token_ids >= rejected).astype(jnp.int32)
    place_ids = jnp.where(token_ids >= rejected, token_ids - (rejected - chosen), token_ids)
    target, source = token_ids[:, None], token_ids[None, :]
    near = (segment[None, :] == segment[:, None]) | (segment[None, :] == 0)
    allowed = ((source <= target) & is_live[None, :] & near) | (source == target)
    mask = jnp.where(allowed, 0.0, MASKED).astype(jnp.float32)
    frequency = jnp.exp(
        jnp.arange(HEAD // 2, dtype=jnp.float32) * (-2.0 * math.log(1000000.0) / HEAD)
    )
    angles = place_ids.astype(jnp.float32)[:, None] * frequency[None, :]
    columns = [jnp.cos(angles), jnp.sin(angles)]
    columns += [c.astype(jnp.float32)[:, None] for c in (is_live, destination, keep)]
    columns.append(jnp.zeros((tokens, HEAD - 3), jnp.float32))
    table = jnp.concatenate(columns, axis=1)
    scalars = jnp.stack([half[0], kept_count])
    plan = (table, mask, scalars)

    links = Links(replicas, lax.axis_size("group"))
    mine_weight, other_weight = halves(kv_weight, half)
    peer_states = core_swap(core_columns(states, 1 - core, depth), replicas)

    both = (peer_states, states)

    def listed(pieces):
        return jnp.stack([core[0], half[0]] + [b for _, b in pieces])

    fore = ring // 2
    order = [k for j in range(1, ring) for k in (j, -j)][: ring - 1]
    held = {0: mine_weight}
    mine = [(mine_weight, block(0, False))]
    other = [(other_weight, block(0, False))]
    middle, late = [], []
    crossed = links.send(mine_weight, "y")
    mine.append((crossed, block(0, True)))
    moving = other_weight
    for k in order:
        final = k == order[-1]
        nearer = held[k - 1] if k > 0 else held[k + 1]
        held[k] = links.send(nearer, "fore" if k > 0 else "back", plan if final else ())
        mine.append((held[k], block(k, False)))
        crossed = links.send(held[k], "y")
        if 1 <= k < fore:
            other.append((links.send(held[k], "x"), block(k, False)))
        if final:
            early = mine + other
            sums = accumulate(
                both,
                listed(early),
                [p for p, _ in early],
                [0] * len(mine) + [1] * len(other),
                bias=kv_bias[None, :],
            )
            for j in range(1, ring - fore):
                moving = links.send(moving, "back")
                middle.append((moving, block(-j, False)))
            moving = links.send(moving, "back", sums)
            late.append((moving, block(fore - ring, False)))
            late.append((links.send(other_weight, "y", sums), block(0, True)))
            late.append((links.send(crossed, "x", sums), block(k, True)))
            middle = [(crossed, block(k, True))] + middle
            mine_peer, mine_own, other_peer, other_own, left_peer, left_own = accumulate(
                both,
                listed(middle + late),
                [p for p, _ in middle],
                [0] + [1] * (len(middle) - 1),
                start=sums,
                later=len(late),
            )
        else:
            mine.append((crossed, block(k, True)))
            piece = (links.send(crossed, "x"), block(k, True))
            (middle if k == order[-2] else other).append(piece)

    mine_peer = core_swap(mine_peer, replicas)
    mine_kv, mine_keys, mine_spans = finish(mine_own, mine_peer, table, replicas)
    last = [p for p, _ in late]
    other_peer = core_swap(complete(left_peer, last, other_peer), replicas)
    other_own = complete(left_own, last, other_own)
    other_kv, other_keys, spans = finish(other_own, other_peer, table, replicas, mine_spans)
    spans = spans.reshape(replicas, SPAN, width)
    spans = lax.all_to_all(spans, "dp", split_axis=0, concat_axis=0, tiled=True)
    spans = spans.reshape(replicas * SPAN, width)
    context = attend(half, False, mask, table, queries, mine_keys, mine_kv)
    context = attend(half, True, mask, table, queries, other_keys, other_kv, context)
    work_rows = place(scalars, table, mine_kv, other_kv, spans)
    return (context, work_rows)


def solution(mesh):
    in_specs = (
        P(("group", "dp"), None),
        P(("group", "dp"), None),
        P("dp", None),
        P(),
        P(("group", "dp")),
        P(("group", "dp"), None),
        P(("group", "dp"), None),
    )
    out_specs = (P(("group", "dp"), None), P(("group", "dp"), None))
    return jax.shard_map(
        per_device, mesh=mesh, in_specs=in_specs, out_specs=out_specs, check_vma=False
    )
```

time: 214 us -> 104 us (0.49)
  Pallas kernels: 125 us -> 29.4 us
  local copies, waits for them, and re-layouts: 19.7 us -> 7.55 us
  starting transfers between devices: 24.9 us -> 21.9 us
  waiting for transfers between devices: 32.6 us -> 34.8 us
    pallas_call x1, Pallas kernels: 64.7 us -> 2.93 us  [core_columns(): pl.pallas_call(kernel, out_shape=jax.ShapeDtypeStruct((tokens, width // 2...]
    pallas_call x1, Pallas kernels: 32.9 us -> 2.24 us  [halves(): pl.pallas_call(kernel, out_shape=(out, out), in_specs=[pl.BlockSpec(memor...]
    unnamed x62 -> x30, local copies, waits for them, and re-layouts: 18.6 us -> 5.68 us
    ppermute x14, waiting for transfers between devices: 26.7 us -> 31.8 us  [send(): self.last[link] = lax.ppermute(after(value, *before), axis, pairs)]
    all_to_all x2 -> x1, starting transfers between devices: 7.69 us -> 3.99 us  [per_device(): spans = lax.all_to_all(spans, 'dp', split_axis=0, concat_axis=0, tiled=True)]
    pallas_call x6 -> x5, Pallas kernels: 18.8 us -> 15.2 us  [the longest x2 11.7 us: accumulate(): pl.pallas_call(kernel, out_shape=out_shape, in_specs=[pl.BlockSpec(memory...]
    all_to_all x2 -> x1, waiting for transfers between devices: 5.84 us -> 2.98 us  [per_device(): spans = lax.all_to_all(spans, 'dp', split_axis=0, concat_axis=0, tiled=True)]
  transfers between devices with their start and end apart: 19 -> 18, of which waited for: 6 -> 10; matrix products, arithmetic and copies ran while one was open for 3% -> 6% of each run, Pallas kernels for 40% -> 22%
where the time goes in v3:
time: 104 us
  waiting for transfers between devices  34.8 us (33%)
  Pallas kernels  29.4 us (28%)
  starting transfers between devices  21.9 us (21%)
  local copies, waits for them, and re-layouts  7.55 us (7%)
  between operations  5.43 us (5%)
  other arithmetic  4.6 us (4%)
    ppermute x14, waiting for transfers between devices, send(): self.last[link] = lax.ppermute(after(value, *before), axis, pairs)  31.8 us
    ppermute x14, starting transfers between devices, send(): self.last[link] = lax.ppermute(after(value, *before), axis, pairs)  17.7 us
    pallas_call x2, Pallas kernels, accumulate(): pl.pallas_call(kernel, out_shape=out_shape, in_specs=[pl.BlockSpec(memory...  11.7 us
    pallas_call x2, Pallas kernels, attend(): pl.pallas_call(kernel, out_shape=jax.ShapeDtypeStruct(queries.shape, jnp....  6.14 us
    unnamed x30, local copies, waits for them, and re-layouts  5.68 us
    all_to_all x1, starting transfers between devices, per_device(): spans = lax.all_to_all(spans, 'dp', split_axis=0, concat_axis=0, tiled=True)  3.99 us
    all_to_all x1, waiting for transfers between devices, per_device(): spans = lax.all_to_all(spans, 'dp', split_axis=0, concat_axis=0, tiled=True)  2.98 us
    pallas_call x1, Pallas kernels, core_columns(): pl.pallas_call(kernel, out_shape=jax.ShapeDtypeStruct((tokens, width // 2...  2.93 us
  transfers between devices with their start and end apart: 18, of which 10 were waited for; matrix products, arithmetic and copies ran while one was open for 6% of the time, Pallas kernels for 22%

profile of v3, /device:TPU:0, one launch (start us, length us, event | category | flops | bytes accessed | tf_op | source)
XLA Modules:
  0.0 103.7 jit_solution(5840749412493972214)
XLA Ops:
  0.6 2.2 %shard_map.87 = (bf16[512,512]{1,0:T(8,128)(2,1)}, bf16[512,512]{1,0:T(8,128)(2,1)}) custom-call(s32[1]{0:T(128)} %bitcast.half_ref, bf16[512,1024]{1,0:T(8,128)(2,1)} %weight_ref.1), custom_call_target="tpu_custom_call" | custom-call | bytes 2097152 | tf_op jit(solution)/shard_map/pallas_call | solution.py:84
  2.9 4.1 %collective-permute-start.1 = (bf16[512,512]{1,0:T(8,128)(2,1)}, bf16[512,512]{1,0:T(8,128)(2,1)}, u32[]{:S(2)}, u32[]{:S(2)}) collective-permute-start(bf16[512,512]{1,0:T(8,128)(2,1)} %get-tuple-element.32.refs_2_), channel_id=1, source_target_pairs={{0,8},{1,9},{2,10},{3,11},{4,0},{5,1},{6,2},{7,3},{8,12},{9,13},{1... | collective-permute-start | bytes 1572872 | tf_op jit(solution)/shard_map/ppermute | solution.py:51
  7.0 1.5 %collective-permute-start.4 = (bf16[512,512]{1,0:T(8,128)(2,1)}, bf16[512,512]{1,0:T(8,128)(2,1)S(1)}, u32[]{:S(2)}, u32[]{:S(2)}) collective-permute-start(bf16[512,512]{1,0:T(8,128)(2,1)} %get-tuple-element.32.refs_2_), channel_id=1, source_target_pairs={{0,2},{1,3},{2,0},{3,1},{4,6},{5,7},{6,4},{7,5},{8,10},{9,11},{10,... | collective-permute-start | bytes 1572872 | tf_op jit(solution)/shard_map/ppermute | solution.py:51
  8.5 2.9 %shard_map.86 = bf16[256,4096]{1,0:T(8,128)(2,1)} custom-call(s32[1]{0:T(128)S(6)} %sub.93.core_ref, bf16[256,8192]{1,0:T(8,128)(2,1)} %refs_1_.3), custom_call_target="tpu_custom_call" | custom-call | bytes 4194304 | tf_op jit(solution)/shard_map/pallas_call | solution.py:117
  22.4 1.5 %collective-permute-start.8 = (bf16[512,512]{1,0:T(8,128)(2,1)}, bf16[512,512]{1,0:T(8,128)(2,1)S(1)}, u32[]{:S(2)}, u32[]{:S(2)}) collective-permute-start(bf16[512,512]{1,0:T(8,128)(2,1)} %collective-permute-done.1.refs_4_), channel_id=1, source_target_pairs={{0,16},{16,0},{1,17},{17,1},{2,18},{18,2},{3,19},{19,3},{4,20},{20... | collective-permute-start | bytes 1572872 | tf_op jit(solution)/shard_map/ppermute | solution.py:51
  24.1 11.8 %collective-permute-done.5.refs_5_ = bf16[512,512]{1,0:T(8,128)(2,1)} collective-permute-done((bf16[512,512]{1,0:T(8,128)(2,1)}, bf16[512,512]{1,0:T(8,128)(2,1)}, u32[]{:S(2)}, u32[]{:S(2)}) %collective-permute-start.5) | collective-permute-done | bytes 524320 | tf_op jit(solution)/shard_map/ppermute | solution.py:51
  37.0 1.5 %collective-permute-start.6 = (bf16[512,512]{1,0:T(8,128)(2,1)}, bf16[512,512]{1,0:T(8,128)(2,1)}, u32[]{:S(2)}, u32[]{:S(2)}) collective-permute-start(bf16[512,512]{1,0:T(8,128)(2,1)} %collective-permute-done.2.refs_6_), channel_id=1, source_target_pairs={{0,2},{1,3},{2,0},{3,1},{4,6},{5,7},{6,4},{7,5},{8,10},{9,11},{10,... | collective-permute-start | bytes 1572872 | tf_op jit(solution)/shard_map/ppermute | solution.py:51
  38.6 1.5 %collective-permute-start.9 = (bf16[512,512]{1,0:T(8,128)(2,1)}, bf16[512,512]{1,0:T(8,128)(2,1)}, u32[]{:S(2)}, u32[]{:S(2)}) collective-permute-start(bf16[512,512]{1,0:T(8,128)(2,1)} %collective-permute-done.5.refs_5_), channel_id=1, source_target_pairs={{0,16},{16,0},{1,17},{17,1},{2,18},{18,2},{3,19},{19,3},{4,20},{20... | collective-permute-start | bytes 1572872 | tf_op jit(solution)/shard_map/ppermute | solution.py:51
  41.7 8.7 %collective-permute-done.6.refs_7_ = bf16[512,512]{1,0:T(8,128)(2,1)} collective-permute-done((bf16[512,512]{1,0:T(8,128)(2,1)}, bf16[512,512]{1,0:T(8,128)(2,1)}, u32[]{:S(2)}, u32[]{:S(2)}) %collective-permute-start.6) | collective-permute-done | bytes 524320 | tf_op jit(solution)/shard_map/ppermute | solution.py:51
  50.3 1.5 %collective-permute-done.9.refs_11_ = bf16[512,512]{1,0:T(8,128)(2,1)} collective-permute-done((bf16[512,512]{1,0:T(8,128)(2,1)}, bf16[512,512]{1,0:T(8,128)(2,1)}, u32[]{:S(2)}, u32[]{:S(2)}) %collective-permute-start.9) | collective-permute-done | bytes 524320 | tf_op jit(solution)/shard_map/ppermute | solution.py:51
  51.8 1.5 %collective-permute-start.10 = (bf16[512,512]{1,0:T(8,128)(2,1)}, bf16[512,512]{1,0:T(8,128)(2,1)S(1)}, u32[]{:S(2)}, u32[]{:S(2)}) collective-permute-start(bf16[512,512]{1,0:T(8,128)(2,1)} %collective-permute-done.6.refs_7_), channel_id=1, source_target_pairs={{0,16},{16,0},{1,17},{17,1},{2,18},{18,2},{3,19},{19,3},{4,20},{20... | collective-permute-start | bytes 1572872 | tf_op jit(solution)/shard_map/ppermute | solution.py:51
  56.8 7.5 %shard_map.88 = (f32[256,512]{1,0:T(8,128)}, f32[256,512]{1,0:T(8,128)}, f32[256,512]{1,0:T(8,128)}, f32[256,512]{1,0:T(8,128)}) custom-call(s32[12]{0:T(128)S(1)} %stack.58.scalar_ref, bf16[256,4096]{1,0:T(8,128)(2,1)} %copy-done.9, bf16[256,8192]{1,0:T(8,128)(2,1)} %refs_1_.3, bf16[512,512]{1,0:T(8,128)(2,1)} %get-tuple-element.32.refs_2_, ...), custom_call_target="tpu_custom_call" | custom-call | flops 2684354560 | bytes 10485760 | tf_op jit(solution)/shard_map/pallas_call | solution.py:220
  64.4 1.6 %collective-permute-done.7.refs_2_ = bf16[512,512]{1,0:T(8,128)(2,1)} collective-permute-done((bf16[512,512]{1,0:T(8,128)(2,1)}, bf16[512,512]{1,0:T(8,128)(2,1)}, u32[]{:S(2)}, u32[]{:S(2)}) %collective-permute-start.7) | collective-permute-done | bytes 524320 | tf_op jit(solution)/shard_map/ppermute | solution.py:51
  66.0 1.3 %collective-permute-start.14 = (bf16[512,512]{1,0:T(8,128)(2,1)}, bf16[512,512]{1,0:T(8,128)(2,1)S(1)}, u32[]{:S(2)}, u32[]{:S(2)}) collective-permute-start(bf16[512,512]{1,0:T(8,128)(2,1)} %collective-permute-done.7.refs_2_), channel_id=1, source_target_pairs={{0,16},{16,0},{1,17},{17,1},{2,18},{18,2},{3,19},{19,3},{4,20},{20... | collective-permute-start | bytes 1572872 | tf_op jit(solution)/shard_map/ppermute | solution.py:51
  68.9 4.2 %shard_map.89 = (f32[256,512]{1,0:T(8,128)S(1)}, f32[256,512]{1,0:T(8,128)S(1)}, f32[256,512]{1,0:T(8,128)S(1)}, f32[256,512]{1,0:T(8,128)S(1)}, bf16[256,1536]{...) custom-call(s32[8]{0:T(128)S(1)} %stack.51.scalar_ref, bf16[256,4096]{1,0:T(8,128)(2,1)} %copy-done.9, ...), custom_call_target="tpu_custom_call" | custom-call | flops 805306368 | bytes 3145728 | tf_op jit(solution)/shard_map/pallas_call | solution.py:220
  73.1 3.9 %collective-permute-done.14.refs_2_ = bf16[512,512]{1,0:T(8,128)(2,1)S(1)} collective-permute-done((bf16[512,512]{1,0:T(8,128)(2,1)}, bf16[512,512]{1,0:T(8,128)(2,1)S(1)}, u32[]{:S(2)}, u32[]{:S(2)}) %collective-permute-start.14) | collective-permute-done | bytes 524320 | tf_op jit(solution)/shard_map/ppermute | solution.py:51
  77.0 1.3 %collective-permute-done.13.refs_1_ = bf16[512,512]{1,0:T(8,128)(2,1)S(1)} collective-permute-done((bf16[512,512]{1,0:T(8,128)(2,1)}, bf16[512,512]{1,0:T(8,128)(2,1)S(1)}, u32[]{:S(2)}, u32[]{:S(2)}) %collective-permute-start.13) | collective-permute-done | bytes 524320 | tf_op jit(solution)/shard_map/ppermute | solution.py:51
  80.3 1.4 %shard_map.92 = (bf16[256,512]{1,0:T(8,128)(2,1)S(1)}, bf16[256,256]{1,0:T(8,128)(2,1)S(1)}, bf16[128,512]{1,0:T(8,128)(2,1)S(1)}) custom-call(f32[256,512]{1,0:T(8,128)S(1)} %get-tuple-element.52.own_ref, f32[256,512]{1,0:T(8,128)S(1)} %collective-permute-done.16.peer_ref, f32[256,256]{1,0:T(8,128)} %concatenate.3.table_in.table_ref), custom_call_target="tpu_custom_call" | custom-call | flops 33554432 | bytes 1310720 | tf_op jit(solution)/shard_map/pallas_call | solution.py:313
  85.1 1.5 %shard_map.93 = (bf16[256,512]{1,0:T(8,128)(2,1)S(1)}, bf16[256,256]{1,0:T(8,128)(2,1)S(1)}, bf16[128,1024]{1,0:T(8,128)(2,1)S(1)}) custom-call(f32[256,512]{1,0:T(8,128)S(1)} %shard_map.90.own_ref, f32[256,512]{1,0:T(8,128)S(1)} %collective-permute-done.15.peer_ref, f32[256,256]{1,0:T(8,128)} %concatenate.3.table_in.table_ref, ...), custom_call_target="tpu_custom_call" | custom-call | flops 33554432 | bytes 1310720 | tf_op jit(solution)/shard_map/pallas_call | solution.py:313
  87.3 4.0 %all-to-all-start = ((bf16[16,8,1024]{2,1,0:T(8,128)(2,1)}), bf16[16,8,1024]{2,1,0:T(8,128)(2,1)S(1)}, u32[]{:S(2)}, u32[]{:S(2)}) async-start(bf16[16,8,1024]{2,1,0:T(8,128)(2,1)} %bitcast.21), calls=%async_computation | async-start | bytes 524288 | tf_op jit(solution)/shard_map/all_to_all | solution.py:560
  92.2 3.1 %shard_map.94.refs_0_ = bf16[256,4096]{1,0:T(8,128)(2,1)} custom-call(s32[1]{0:T(128)} %bitcast.half_ref, f32[256,256]{1,0:T(8,128)S(1)} %fusion.3.mask_ref, f32[256,256]{1,0:T(8,128)S(1)} %copy-done, bf16[256,4096]{1,0:T(8,128)(2,1)S(1)} %copy-done.1, bf16[256,256]{1,0:T(8,128)(2,1)S(1)} %copy-done.8, bf16[256,512]{1,0:T(8,128)(2,1)S(1)} %get-tuple-element.58.value_ref.mine_ref), custom_call_target="tpu_custom_call" | custom-call | flops 536870912 | bytes 2097152 | tf_op jit(solution)/shard_map/pallas_call | solution.py:375
  95.3 3.1 %shard_map.95 = bf16[256,4096]{1,0:T(8,128)(2,1)} custom-call(s32[1]{0:T(128)} %bitcast.half_ref, f32[256,256]{1,0:T(8,128)S(1)} %fusion.3.mask_ref, f32[256,256]{1,0:T(8,128)S(1)} %copy-done, bf16[256,4096]{1,0:T(8,128)(2,1)S(1)} %copy-done.1, bf16[256,256]{1,0:T(8,128)(2,1)S(1)} %get-tuple-element.55.key_ref, ...), custom_call_target="tpu_custom_call", output_to_operand_aliasing={{}: (6, {})} | custom-call | flops 536870912 | bytes 2097152 | tf_op jit(solution)/shard_map/pallas_call | solution.py:375
  98.4 3.0 %all-to-all-done = bf16[16,8,1024]{2,1,0:T(8,128)(2,1)S(1)} async-done(((bf16[16,8,1024]{2,1,0:T(8,128)(2,1)}), bf16[16,8,1024]{2,1,0:T(8,128)(2,1)S(1)}, u32[]{:S(2)}, u32[]{:S(2)}) %all-to-all-start) | async-done | bytes 262176 | tf_op jit(solution)/shard_map/all_to_all | solution.py:560
  101.3 2.4 %shard_map.96 = bf16[192,1024]{1,0:T(8,128)(2,1)} custom-call(s32[2]{0:T(128)S(1)} %pad_add_fusion.scalar_ref, f32[256,256]{1,0:T(8,128)S(1)} %copy-done, bf16[256,512]{1,0:T(8,128)(2,1)S(1)} %get-tuple-element.58.value_ref.mine_ref, bf16[256,512]{1,0:T(8,128)(2,1)S(1)} %get-tuple-element.56.value_ref.other_ref, bf16[128,1024]{1,0:T(8,128)(2,1)S(1)} %bitcast.20), custom_call_target="tpu_custom_call" | custom-call | flops 50331648 | bytes 786432 | tf_op jit(solution)/shard_map/pallas_call | solution.py:432
  (71 shorter events, 21.3 us)
Async XLA Ops:
  2.9 18.3 %collective-permute-start.1 = (bf16[512,512]{1,0:T(8,128)(2,1)}, bf16[512,512]{1,0:T(8,128)(2,1)}, u32[]{:S(2)}, u32[]{:S(2)}) collective-permute-start(bf16[512,512]{1,0:T(8,128)(2,1)} %get-tuple-element.32.refs_2_), channel_id=1, source_target_pairs={{0,8},{1,9},{2,10},{3,11},{4,0},{5,1},{6,2},{7,3},{8,12},{9,13},{1... | collective-permute-start | bytes 1572872 | tf_op jit(solution)/shard_map/ppermute | solution.py:51
  7.0 14.2 %collective-permute-start.4 = (bf16[512,512]{1,0:T(8,128)(2,1)}, bf16[512,512]{1,0:T(8,128)(2,1)S(1)}, u32[]{:S(2)}, u32[]{:S(2)}) collective-permute-start(bf16[512,512]{1,0:T(8,128)(2,1)} %get-tuple-element.32.refs_2_), channel_id=1, source_target_pairs={{0,2},{1,3},{2,0},{3,1},{4,6},{5,7},{6,4},{7,5},{8,10},{9,11},{10,... | collective-permute-start | bytes 1572872 | tf_op jit(solution)/shard_map/ppermute | solution.py:51
  8.5 3.0 %copy-start.14 = (s32[1,32]{1,0:T(1,128)S(1)}, s32[1,32]{1,0:T(1,128)}, u32[]{:S(2)}) copy-start(s32[1,32]{1,0:T(1,128)} %param.13) | copy-start | bytes 388
  8.5 3.7 %copy-start.13 = (s32[1,2]{1,0:T(1,128)S(1)}, s32[1,2]{1,0:T(1,128)}, u32[]{:S(2)}) copy-start(s32[1,2]{1,0:T(1,128)} %param.12) | copy-start | bytes 28
  11.4 44.1 %collective-permute-start = (bf16[256,4096]{1,0:T(8,128)(2,1)}, bf16[256,4096]{1,0:T(8,128)(2,1)S(1)}, u32[]{:S(2)}, u32[]{:S(2)}) collective-permute-start(bf16[256,4096]{1,0:T(8,128)(2,1)} %shard_map.86), channel_id=1, source_target_pairs={{0,1},{1,0},{2,3},{3,2},{4,5},{5,4},{6,7},{7,6},{8,9},{9,8},{10,11... | collective-permute-start | bytes 6291464 | tf_op jit(solution)/shard_map/ppermute | solution.py:56
  21.2 2.7 %copy-start.11 = (bf16[512,512]{1,0:T(8,128)(2,1)}, bf16[512,512]{1,0:T(8,128)(2,1)S(1)}, u32[]{:S(2)}) copy-start(bf16[512,512]{1,0:T(8,128)(2,1)S(1)} %collective-permute-done.4.refs_3_) | copy-start | bytes 1572868
  21.2 14.7 %collective-permute-start.5 = (bf16[512,512]{1,0:T(8,128)(2,1)}, bf16[512,512]{1,0:T(8,128)(2,1)}, u32[]{:S(2)}, u32[]{:S(2)}) collective-permute-start(bf16[512,512]{1,0:T(8,128)(2,1)} %collective-permute-done.1.refs_4_), channel_id=1, source_target_pairs={{0,2},{1,3},{2,0},{3,1},{4,6},{5,7},{6,4},{7,5},{8,10},{9,11},{10,... | collective-permute-start | bytes 1572872 | tf_op jit(solution)/shard_map/ppermute | solution.py:51
  22.1 14.9 %collective-permute-start.2 = (bf16[512,512]{1,0:T(8,128)(2,1)}, bf16[512,512]{1,0:T(8,128)(2,1)}, u32[]{:S(2)}, u32[]{:S(2)}) collective-permute-start(bf16[512,512]{1,0:T(8,128)(2,1)} %get-tuple-element.32.refs_2_), channel_id=1, source_target_pairs={{8,0},{9,1},{10,2},{11,3},{0,4},{1,5},{2,6},{3,7},{12,8},{13,9},{1... | collective-permute-start | bytes 1572872 | tf_op jit(solution)/shard_map/ppermute | solution.py:51
  22.4 16.2 %collective-permute-start.8 = (bf16[512,512]{1,0:T(8,128)(2,1)}, bf16[512,512]{1,0:T(8,128)(2,1)S(1)}, u32[]{:S(2)}, u32[]{:S(2)}) collective-permute-start(bf16[512,512]{1,0:T(8,128)(2,1)} %collective-permute-done.1.refs_4_), channel_id=1, source_target_pairs={{0,16},{16,0},{1,17},{17,1},{2,18},{18,2},{3,19},{19,3},{4,20},{20... | collective-permute-start | bytes 1572872 | tf_op jit(solution)/shard_map/ppermute | solution.py:51
  37.0 13.3 %collective-permute-start.6 = (bf16[512,512]{1,0:T(8,128)(2,1)}, bf16[512,512]{1,0:T(8,128)(2,1)}, u32[]{:S(2)}, u32[]{:S(2)}) collective-permute-start(bf16[512,512]{1,0:T(8,128)(2,1)} %collective-permute-done.2.refs_6_), channel_id=1, source_target_pairs={{0,2},{1,3},{2,0},{3,1},{4,6},{5,7},{6,4},{7,5},{8,10},{9,11},{10,... | collective-permute-start | bytes 1572872 | tf_op jit(solution)/shard_map/ppermute | solution.py:51
  38.6 13.2 %collective-permute-start.9 = (bf16[512,512]{1,0:T(8,128)(2,1)}, bf16[512,512]{1,0:T(8,128)(2,1)}, u32[]{:S(2)}, u32[]{:S(2)}) collective-permute-start(bf16[512,512]{1,0:T(8,128)(2,1)} %collective-permute-done.5.refs_5_), channel_id=1, source_target_pairs={{0,16},{16,0},{1,17},{17,1},{2,18},{18,2},{3,19},{19,3},{4,20},{20... | collective-permute-start | bytes 1572872 | tf_op jit(solution)/shard_map/ppermute | solution.py:51
  41.0 13.0 %collective-permute-start.3 = (bf16[512,512]{1,0:T(8,128)(2,1)}, bf16[512,512]{1,0:T(8,128)(2,1)}, u32[]{:S(2)}, u32[]{:S(2)}) collective-permute-start(bf16[512,512]{1,0:T(8,128)(2,1)} %collective-permute-done.1.refs_4_), channel_id=1, source_target_pairs={{0,8},{1,9},{2,10},{3,11},{4,0},{5,1},{6,2},{7,3},{8,12},{9,13},{1... | collective-permute-start | bytes 1572872 | tf_op jit(solution)/shard_map/ppermute | solution.py:51
  51.8 12.5 %collective-permute-start.10 = (bf16[512,512]{1,0:T(8,128)(2,1)}, bf16[512,512]{1,0:T(8,128)(2,1)S(1)}, u32[]{:S(2)}, u32[]{:S(2)}) collective-permute-start(bf16[512,512]{1,0:T(8,128)(2,1)} %collective-permute-done.6.refs_7_), channel_id=1, source_target_pairs={{0,16},{16,0},{1,17},{17,1},{2,18},{18,2},{3,19},{19,3},{4,20},{20... | collective-permute-start | bytes 1572872 | tf_op jit(solution)/shard_map/ppermute | solution.py:51
  53.9 12.0 %collective-permute-start.7 = (bf16[512,512]{1,0:T(8,128)(2,1)}, bf16[512,512]{1,0:T(8,128)(2,1)}, u32[]{:S(2)}, u32[]{:S(2)}) collective-permute-start(bf16[512,512]{1,0:T(8,128)(2,1)} %collective-permute-done.3.refs_8_), channel_id=1, source_target_pairs={{0,2},{1,3},{2,0},{3,1},{4,6},{5,7},{6,4},{7,5},{8,10},{9,11},{10,... | collective-permute-start | bytes 1572872 | tf_op jit(solution)/shard_map/ppermute | solution.py:51
  54.3 13.3 %collective-permute-start.11 = (bf16[512,512]{1,0:T(8,128)(2,1)}, bf16[512,512]{1,0:T(8,128)(2,1)}, u32[]{:S(2)}, u32[]{:S(2)}) collective-permute-start(bf16[512,512]{1,0:T(8,128)(2,1)} %get-tuple-element.48.refs_9_), channel_id=1, source_target_pairs={{8,0},{9,1},{10,2},{11,3},{0,4},{1,5},{2,6},{3,7},{12,8},{13,9},{1... | collective-permute-start | bytes 1572872 | tf_op jit(solution)/shard_map/ppermute | solution.py:51
  66.0 11.0 %collective-permute-start.14 = (bf16[512,512]{1,0:T(8,128)(2,1)}, bf16[512,512]{1,0:T(8,128)(2,1)S(1)}, u32[]{:S(2)}, u32[]{:S(2)}) collective-permute-start(bf16[512,512]{1,0:T(8,128)(2,1)} %collective-permute-done.7.refs_2_), channel_id=1, source_target_pairs={{0,16},{16,0},{1,17},{17,1},{2,18},{18,2},{3,19},{19,3},{4,20},{20... | collective-permute-start | bytes 1572872 | tf_op jit(solution)/shard_map/ppermute | solution.py:51
  67.3 11.0 %collective-permute-start.13 = (bf16[512,512]{1,0:T(8,128)(2,1)}, bf16[512,512]{1,0:T(8,128)(2,1)S(1)}, u32[]{:S(2)}, u32[]{:S(2)}) collective-permute-start(bf16[512,512]{1,0:T(8,128)(2,1)} %get-tuple-element.48.refs_9_), channel_id=1, source_target_pairs={{0,2},{1,3},{2,0},{3,1},{4,6},{5,7},{6,4},{7,5},{8,10},{9,11},{10,... | collective-permute-start | bytes 1572872 | tf_op jit(solution)/shard_map/ppermute | solution.py:51
  67.6 12.0 %collective-permute-start.12 = (bf16[512,512]{1,0:T(8,128)(2,1)}, bf16[512,512]{1,0:T(8,128)(2,1)S(1)}, u32[]{:S(2)}, u32[]{:S(2)}) collective-permute-start(bf16[512,512]{1,0:T(8,128)(2,1)} %collective-permute-done.11.refs_4_), channel_id=1, source_target_pairs={{8,0},{9,1},{10,2},{11,3},{0,4},{1,5},{2,6},{3,7},{12,8},{13,9},{1... | collective-permute-start | bytes 1572872 | tf_op jit(solution)/shard_map/ppermute | solution.py:51
  73.1 7.2 %collective-permute-start.16 = (f32[256,512]{1,0:T(8,128)S(1)}, f32[256,512]{1,0:T(8,128)S(1)}, u32[]{:S(2)}, u32[]{:S(2)}) collective-permute-start(f32[256,512]{1,0:T(8,128)S(1)} %get-tuple-element.53), channel_id=1, source_target_pairs={{0,1},{1,0},{2,3},{3,2},{4,5},{5,4},{6,7},{7,6},{8,9},{9,8},{10,11... | collective-permute-start | bytes 1572872 | tf_op jit(solution)/shard_map/ppermute | solution.py:56
  78.3 3.4 %copy-start.2 = (bf16[512,512]{1,0:T(8,128)(2,1)}, bf16[512,512]{1,0:T(8,128)(2,1)S(1)}, u32[]{:S(2)}) copy-start(bf16[512,512]{1,0:T(8,128)(2,1)S(1)} %collective-permute-done.13.refs_1_) | copy-start | bytes 1572868
  80.2 4.8 %collective-permute-start.15 = (f32[256,512]{1,0:T(8,128)S(1)}, f32[256,512]{1,0:T(8,128)S(1)}, u32[]{:S(2)}, u32[]{:S(2)}) collective-permute-start(f32[256,512]{1,0:T(8,128)S(1)} %shard_map.91), channel_id=1, source_target_pairs={{0,1},{1,0},{2,3},{3,2},{4,5},{5,4},{6,7},{7,6},{8,9},{9,8},{10,11... | collective-permute-start | bytes 1572872 | tf_op jit(solution)/shard_map/ppermute | solution.py:56
  84.5 6.8 %copy-start = (f32[256,256]{1,0:T(8,128)S(1)}, f32[256,256]{1,0:T(8,128)}, u32[]{:S(2)}) copy-start(f32[256,256]{1,0:T(8,128)} %concatenate.3.table_in.table_ref) | copy-start | bytes 786436
  84.5 6.8 %copy-start.1 = (bf16[256,4096]{1,0:T(8,128)(2,1)S(1)}, bf16[256,4096]{1,0:T(8,128)(2,1)}, u32[]{:S(2)}) copy-start(bf16[256,4096]{1,0:T(8,128)(2,1)} %query_ref.3) | copy-start | bytes 6291460
  87.3 14.0 %all-to-all-start = ((bf16[16,8,1024]{2,1,0:T(8,128)(2,1)}), bf16[16,8,1024]{2,1,0:T(8,128)(2,1)S(1)}, u32[]{:S(2)}, u32[]{:S(2)}) async-start(bf16[16,8,1024]{2,1,0:T(8,128)(2,1)} %bitcast.21), calls=%async_computation | async-start | bytes 524288 | tf_op jit(solution)/shard_map/all_to_all | solution.py:560
  (9 other events, 10.9 us)

commit v4 on v3

--- a/solution.py
+++ b/solution.py
@@ -14,6 +14,7 @@
 ABSENT = 1e30
 MASKED = -1e30
 LIMIT = 18 << 20
+LAG = {"x": 1, "y": 2, "z": 1}
 LIVE, DESTINATION, KEEP = HEAD, HEAD + 1, HEAD + 2
 
 
@@ -42,14 +43,16 @@
             "y": ("y", "dp", [(i, i ^ 2) for i in range(replicas)]),
             "x": ("x", "group", [(i, i ^ 1) for i in range(groups)]),
         }
-        self.last = {}
-
-    def send(self, value, route, before=()):
+        self.sent = {"x": [], "y": [], "z": []}
+
+    def send(self, value, route, before=(), lag=None):
         link, axis, pairs = self.routes[route]
-        if link in self.last:
-            before = (self.last[link], *before)
-        self.last[link] = lax.ppermute(after(value, *before), axis, pairs)
-        return self.last[link]
+        sent = self.sent[link]
+        lag = LAG[link] if lag is None else lag
+        if len(sent) >= lag:
+            before = (sent[-lag], *before)
+        sent.append(lax.ppermute(after(value, *before), axis, pairs))
+        return sent[-1]
 
 
 def core_swap(value, replicas):
@@ -496,7 +499,8 @@
 
     links = Links(replicas, lax.axis_size("group"))
     mine_weight, other_weight = halves(kv_weight, half)
-    peer_states = core_swap(core_columns(states, 1 - core, depth), replicas)
+    peer_columns = core_columns(states, 1 - core, depth)
+    peer_states = core_swap(peer_columns, replicas)
 
     both = (peer_states, states)
 
@@ -515,7 +519,9 @@
     for k in order:
         final = k == order[-1]
         nearer = held[k - 1] if k > 0 else held[k + 1]
-        held[k] = links.send(nearer, "fore" if k > 0 else "back", plan if final else ())
+        second = k == order[1]
+        before = (peer_columns,) if second else plan if final else ()
+        held[k] = links.send(nearer, "fore" if k > 0 else "back", before, lag=2 if second else None)
         mine.append((held[k], block(k, False)))
         crossed = links.send(held[k], "y")
         if 1 <= k < fore:
@@ -551,10 +557,11 @@
             (middle if k == order[-2] else other).append(piece)
 
     mine_peer = core_swap(mine_peer, replicas)
-    mine_kv, mine_keys, mine_spans = finish(mine_own, mine_peer, table, replicas)
     last = [p for p, _ in late]
     other_peer = core_swap(complete(left_peer, last, other_peer), replicas)
     other_own = complete(left_own, last, other_own)
+    mine_own = after(mine_own, other_own)
+    mine_kv, mine_keys, mine_spans = finish(mine_own, mine_peer, table, replicas)
     other_kv, other_keys, spans = finish(other_own, other_peer, table, replicas, mine_spans)
     spans = spans.reshape(replicas, SPAN, width)
     spans = lax.all_to_all(spans, "dp", split_axis=0, concat_axis=0, tiled=True)

time: 104 us -> 97.2 us (0.935)
  waiting for transfers between devices: 34.8 us -> 28.7 us
  local copies, waits for them, and re-layouts: 7.55 us -> 4.8 us
  starting transfers between devices: 21.9 us -> 23.7 us
    ppermute x14, waiting for transfers between devices: 31.8 us -> 25.8 us  [send(): sent.append(lax.ppermute(after(value, *before), axis, pairs))]
    unnamed x30 -> x28, local copies, waits for them, and re-layouts: 5.68 us -> 2.94 us
    ppermute x14, starting transfers between devices: 17.7 us -> 19.2 us  [send(): sent.append(lax.ppermute(after(value, *before), axis, pairs))]
  transfers between devices with their start and end apart: 18 -> 18, of which waited for: 10 -> 10; matrix products, arithmetic and copies ran while one was open for 6% -> 7% of each run, Pallas kernels for 22% -> 24%
where the time goes in v4:
time: 97.2 us; the launch traced here: 96.8 us
  Pallas kernels  29.5 us (30%)
  waiting for transfers between devices  28.7 us (30%)
  starting transfers between devices  23.7 us (24%)
  between operations  5.47 us (6%)
  local copies, waits for them, and re-layouts  4.8 us (5%)
  other arithmetic  4.56 us (5%)
    ppermute x14, waiting for transfers between devices, send(): sent.append(lax.ppermute(after(value, *before), axis, pairs))  25.8 us
    ppermute x14, starting transfers between devices, send(): sent.append(lax.ppermute(after(value, *before), axis, pairs))  19.2 us
    pallas_call x2, Pallas kernels, accumulate(): pl.pallas_call(kernel, out_shape=out_shape, in_specs=[pl.BlockSpec(memory...  11.7 us
    pallas_call x2, Pallas kernels, attend(): pl.pallas_call(kernel, out_shape=jax.ShapeDtypeStruct(queries.shape, jnp....  6.14 us
    all_to_all x1, starting transfers between devices, per_device(): spans = lax.all_to_all(spans, 'dp', split_axis=0, concat_axis=0, tiled=True)  4.3 us
    pallas_call x2, Pallas kernels, finish(): pl.pallas_call(kernel, out_shape=(jax.ShapeDtypeStruct((tokens, columns),...  2.98 us
    all_to_all x1, waiting for transfers between devices, per_device(): spans = lax.all_to_all(spans, 'dp', split_axis=0, concat_axis=0, tiled=True)  2.98 us
    pallas_call x1, Pallas kernels, core_columns(): pl.pallas_call(kernel, out_shape=jax.ShapeDtypeStruct((tokens, width // 2...  2.96 us
  transfers between devices with their start and end apart: 18, of which 10 were waited for; matrix products, arithmetic and copies ran while one was open for 7% of the time, Pallas kernels for 24%

profile of v4, /device:TPU:0, one launch (start us, length us, event | category | flops | bytes accessed | tf_op | source)
XLA Modules:
  0.0 96.8 jit_solution(9793763098899800219)
XLA Ops:
  0.6 2.2 %shard_map.87 = (bf16[512,512]{1,0:T(8,128)(2,1)}, bf16[512,512]{1,0:T(8,128)(2,1)}) custom-call(s32[1]{0:T(128)} %bitcast.half_ref, bf16[512,1024]{1,0:T(8,128)(2,1)} %weight_ref.1), custom_call_target="tpu_custom_call" | custom-call | bytes 2097152 | tf_op jit(solution)/shard_map/pallas_call | solution.py:87
  2.9 4.1 %collective-permute-start.1 = (bf16[512,512]{1,0:T(8,128)(2,1)}, bf16[512,512]{1,0:T(8,128)(2,1)}, u32[]{:S(2)}, u32[]{:S(2)}) collective-permute-start(bf16[512,512]{1,0:T(8,128)(2,1)} %get-tuple-element.32.refs_2_), channel_id=1, source_target_pairs={{0,8},{1,9},{2,10},{3,11},{4,0},{5,1},{6,2},{7,3},{8,12},{9,13},{1... | collective-permute-start | bytes 1572872 | tf_op jit(solution)/shard_map/ppermute | solution.py:54
  6.9 1.5 %collective-permute-start.6 = (bf16[512,512]{1,0:T(8,128)(2,1)}, bf16[512,512]{1,0:T(8,128)(2,1)}, u32[]{:S(2)}, u32[]{:S(2)}) collective-permute-start(bf16[512,512]{1,0:T(8,128)(2,1)} %get-tuple-element.32.refs_2_), channel_id=1, source_target_pairs={{0,2},{1,3},{2,0},{3,1},{4,6},{5,7},{6,4},{7,5},{8,10},{9,11},{10,... | collective-permute-start | bytes 1572872 | tf_op jit(solution)/shard_map/ppermute | solution.py:54
  8.5 3.0 %shard_map.86 = bf16[256,4096]{1,0:T(8,128)(2,1)} custom-call(s32[1]{0:T(128)S(6)} %sub.93.core_ref, bf16[256,8192]{1,0:T(8,128)(2,1)} %refs_1_.3), custom_call_target="tpu_custom_call" | custom-call | bytes 4194304 | tf_op jit(solution)/shard_map/pallas_call | solution.py:120
  19.7 1.4 %collective-permute-start.4 = (bf16[512,512]{1,0:T(8,128)(2,1)}, bf16[512,512]{1,0:T(8,128)(2,1)S(1)}, u32[]{:S(2)}, u32[]{:S(2)}) collective-permute-start(bf16[512,512]{1,0:T(8,128)(2,1)} %collective-permute-done.1.refs_4_), channel_id=1, source_target_pairs={{0,2},{1,3},{2,0},{3,1},{4,6},{5,7},{6,4},{7,5},{8,10},{9,11},{10,... | collective-permute-start | bytes 1572872 | tf_op jit(solution)/shard_map/ppermute | solution.py:54
  21.1 1.5 %collective-permute-start.8 = (bf16[512,512]{1,0:T(8,128)(2,1)}, bf16[512,512]{1,0:T(8,128)(2,1)S(1)}, u32[]{:S(2)}, u32[]{:S(2)}) collective-permute-start(bf16[512,512]{1,0:T(8,128)(2,1)} %collective-permute-done.1.refs_4_), channel_id=1, source_target_pairs={{0,16},{16,0},{1,17},{17,1},{2,18},{18,2},{3,19},{19,3},{4,20},{20... | collective-permute-start | bytes 1572872 | tf_op jit(solution)/shard_map/ppermute | solution.py:54
  25.3 6.1 %collective-permute-done.2.refs_6_ = bf16[512,512]{1,0:T(8,128)(2,1)} collective-permute-done((bf16[512,512]{1,0:T(8,128)(2,1)S(1)}, bf16[512,512]{1,0:T(8,128)(2,1)}, u32[]{:S(2)}, u32[]{:S(2)}) %collective-permute-start.2) | collective-permute-done | bytes 524320 | tf_op jit(solution)/shard_map/ppermute | solution.py:54
  32.1 1.5 %collective-permute-start.7 = (bf16[512,512]{1,0:T(8,128)(2,1)}, bf16[512,512]{1,0:T(8,128)(2,1)}, u32[]{:S(2)}, u32[]{:S(2)}) collective-permute-start(bf16[512,512]{1,0:T(8,128)(2,1)} %collective-permute-done.2.refs_6_), channel_id=1, source_target_pairs={{0,2},{1,3},{2,0},{3,1},{4,6},{5,7},{6,4},{7,5},{8,10},{9,11},{10,... | collective-permute-start | bytes 1572872 | tf_op jit(solution)/shard_map/ppermute | solution.py:54
  34.4 1.5 %collective-permute-start.9 = (bf16[512,512]{1,0:T(8,128)(2,1)S(1)}, bf16[512,512]{1,0:T(8,128)(2,1)S(1)}, u32[]{:S(2)}, u32[]{:S(2)}) collective-permute-start(bf16[512,512]{1,0:T(8,128)(2,1)S(1)} %collective-permute-done.4.refs_5_), channel_id=1, source_target_pairs={{0,16},{16,0},{1,17},{17,1},{2,18},{18,2},{3,19},{19,3},{4,20},{20... | collective-permute-start | bytes 1572872 | tf_op jit(solution)/shard_map/ppermute | solution.py:54
  35.9 9.7 %collective-permute-done.3.refs_8_ = bf16[512,512]{1,0:T(8,128)(2,1)S(1)} collective-permute-done((bf16[512,512]{1,0:T(8,128)(2,1)}, bf16[512,512]{1,0:T(8,128)(2,1)S(1)}, u32[]{:S(2)}, u32[]{:S(2)}) %collective-permute-start.3) | collective-permute-done | bytes 524320 | tf_op jit(solution)/shard_map/ppermute | solution.py:54
  45.6 1.5 %collective-permute-start.5 = (bf16[512,512]{1,0:T(8,128)(2,1)S(1)}, bf16[512,512]{1,0:T(8,128)(2,1)}, u32[]{:S(2)}, u32[]{:S(2)}) collective-permute-start(bf16[512,512]{1,0:T(8,128)(2,1)S(1)} %collective-permute-done.3.refs_8_), channel_id=1, source_target_pairs={{0,2},{1,3},{2,0},{3,1},{4,6},{5,7},{6,4},{7,5},{8,10},{9,11},{10,... | collective-permute-start | bytes 1572872 | tf_op jit(solution)/shard_map/ppermute | solution.py:54
  47.8 1.5 %collective-permute-start.10 = (bf16[512,512]{1,0:T(8,128)(2,1)}, bf16[512,512]{1,0:T(8,128)(2,1)S(1)}, u32[]{:S(2)}, u32[]{:S(2)}) collective-permute-start(bf16[512,512]{1,0:T(8,128)(2,1)} %collective-permute-done.7.refs_7_), channel_id=1, source_target_pairs={{0,16},{16,0},{1,17},{17,1},{2,18},{18,2},{3,19},{19,3},{4,20},{20... | collective-permute-start | bytes 1572872 | tf_op jit(solution)/shard_map/ppermute | solution.py:54
  51.5 7.5 %shard_map.88 = (f32[256,512]{1,0:T(8,128)}, f32[256,512]{1,0:T(8,128)}, f32[256,512]{1,0:T(8,128)}, f32[256,512]{1,0:T(8,128)}) custom-call(s32[12]{0:T(128)S(1)} %stack.58.scalar_ref, bf16[256,4096]{1,0:T(8,128)(2,1)} %copy-done.5, bf16[256,8192]{1,0:T(8,128)(2,1)} %refs_1_.3, bf16[512,512]{1,0:T(8,128)(2,1)} %get-tuple-element.32.refs_2_, ...), custom_call_target="tpu_custom_call" | custom-call | flops 2684354560 | bytes 10485760 | tf_op jit(solution)/shard_map/pallas_call | solution.py:223
  60.4 1.5 %collective-permute-start.14 = (bf16[512,512]{1,0:T(8,128)(2,1)}, bf16[512,512]{1,0:T(8,128)(2,1)S(1)}, u32[]{:S(2)}, u32[]{:S(2)}) collective-permute-start(bf16[512,512]{1,0:T(8,128)(2,1)} %collective-permute-done.5.refs_2_), channel_id=1, source_target_pairs={{0,16},{16,0},{1,17},{17,1},{2,18},{18,2},{3,19},{19,3},{4,20},{20... | collective-permute-start | bytes 1572872 | tf_op jit(solution)/shard_map/ppermute | solution.py:54
  63.6 4.2 %shard_map.89 = (f32[256,512]{1,0:T(8,128)S(1)}, f32[256,512]{1,0:T(8,128)S(1)}, f32[256,512]{1,0:T(8,128)S(1)}, f32[256,512]{1,0:T(8,128)S(1)}, bf16[256,1536]{...) custom-call(s32[8]{0:T(128)S(1)} %stack.51.scalar_ref, bf16[256,4096]{1,0:T(8,128)(2,1)} %copy-done.5, ...), custom_call_target="tpu_custom_call" | custom-call | flops 805306368 | bytes 3145728 | tf_op jit(solution)/shard_map/pallas_call | solution.py:223
  67.9 4.3 %collective-permute-done.14.refs_2_ = bf16[512,512]{1,0:T(8,128)(2,1)S(1)} collective-permute-done((bf16[512,512]{1,0:T(8,128)(2,1)}, bf16[512,512]{1,0:T(8,128)(2,1)S(1)}, u32[]{:S(2)}, u32[]{:S(2)}) %collective-permute-start.14) | collective-permute-done | bytes 524320 | tf_op jit(solution)/shard_map/ppermute | solution.py:54
  73.4 1.6 %collective-permute-done.12.refs_0_ = bf16[512,512]{1,0:T(8,128)(2,1)S(1)} collective-permute-done((bf16[512,512]{1,0:T(8,128)(2,1)}, bf16[512,512]{1,0:T(8,128)(2,1)S(1)}, u32[]{:S(2)}, u32[]{:S(2)}) %collective-permute-start.12) | collective-permute-done | bytes 524320 | tf_op jit(solution)/shard_map/ppermute | solution.py:54
  76.3 1.5 %shard_map.92 = (bf16[256,512]{1,0:T(8,128)(2,1)S(1)}, bf16[256,256]{1,0:T(8,128)(2,1)S(1)}, bf16[128,512]{1,0:T(8,128)(2,1)S(1)}) custom-call(f32[256,512]{1,0:T(8,128)S(1)} %get-tuple-element.52.own_ref, f32[256,512]{1,0:T(8,128)S(1)} %collective-permute-done.16.peer_ref, f32[256,256]{1,0:T(8,128)} %concatenate.3.table_in.table_ref), custom_call_target="tpu_custom_call" | custom-call | flops 33554432 | bytes 1310720 | tf_op jit(solution)/shard_map/pallas_call | solution.py:316
  77.9 1.4 %shard_map.93 = (bf16[256,512]{1,0:T(8,128)(2,1)S(1)}, bf16[256,256]{1,0:T(8,128)(2,1)S(1)}, bf16[128,1024]{1,0:T(8,128)(2,1)S(1)}) custom-call(f32[256,512]{1,0:T(8,128)S(1)} %shard_map.90.own_ref, f32[256,512]{1,0:T(8,128)S(1)} %collective-permute-done.15.peer_ref, f32[256,256]{1,0:T(8,128)} %concatenate.3.table_in.table_ref, ...), custom_call_target="tpu_custom_call" | custom-call | flops 33554432 | bytes 1310720 | tf_op jit(solution)/shard_map/pallas_call | solution.py:316
  80.0 4.3 %all-to-all-start = ((bf16[16,8,1024]{2,1,0:T(8,128)(2,1)}), bf16[16,8,1024]{2,1,0:T(8,128)(2,1)S(1)}, u32[]{:S(2)}, u32[]{:S(2)}) async-start(bf16[16,8,1024]{2,1,0:T(8,128)(2,1)} %bitcast.21), calls=%async_computation | async-start | bytes 524288 | tf_op jit(solution)/shard_map/all_to_all | solution.py:567
  85.3 3.1 %shard_map.94.refs_0_ = bf16[256,4096]{1,0:T(8,128)(2,1)} custom-call(s32[1]{0:T(128)} %bitcast.half_ref, f32[256,256]{1,0:T(8,128)S(1)} %fusion.3.mask_ref, f32[256,256]{1,0:T(8,128)S(1)} %copy-done, bf16[256,4096]{1,0:T(8,128)(2,1)S(1)} %copy-done.1, bf16[256,256]{1,0:T(8,128)(2,1)S(1)} %copy-done.4, bf16[256,512]{1,0:T(8,128)(2,1)S(1)} %get-tuple-element.58.value_ref.mine_ref), custom_call_target="tpu_custom_call" | custom-call | flops 536870912 | bytes 2097152 | tf_op jit(solution)/shard_map/pallas_call | solution.py:378
  88.3 3.1 %shard_map.95 = bf16[256,4096]{1,0:T(8,128)(2,1)} custom-call(s32[1]{0:T(128)} %bitcast.half_ref, f32[256,256]{1,0:T(8,128)S(1)} %fusion.3.mask_ref, f32[256,256]{1,0:T(8,128)S(1)} %copy-done, bf16[256,4096]{1,0:T(8,128)(2,1)S(1)} %copy-done.1, bf16[256,256]{1,0:T(8,128)(2,1)S(1)} %get-tuple-element.55.key_ref, ...), custom_call_target="tpu_custom_call", output_to_operand_aliasing={{}: (6, {})} | custom-call | flops 536870912 | bytes 2097152 | tf_op jit(solution)/shard_map/pallas_call | solution.py:378
  91.4 3.0 %all-to-all-done = bf16[16,8,1024]{2,1,0:T(8,128)(2,1)S(1)} async-done(((bf16[16,8,1024]{2,1,0:T(8,128)(2,1)}), bf16[16,8,1024]{2,1,0:T(8,128)(2,1)S(1)}, u32[]{:S(2)}, u32[]{:S(2)}) %all-to-all-start) | async-done | bytes 262176 | tf_op jit(solution)/shard_map/all_to_all | solution.py:567
  94.4 2.4 %shard_map.96 = bf16[192,1024]{1,0:T(8,128)(2,1)} custom-call(s32[2]{0:T(128)S(1)} %pad_add_fusion.scalar_ref, f32[256,256]{1,0:T(8,128)S(1)} %copy-done, bf16[256,512]{1,0:T(8,128)(2,1)S(1)} %get-tuple-element.58.value_ref.mine_ref, bf16[256,512]{1,0:T(8,128)(2,1)S(1)} %get-tuple-element.56.value_ref.other_ref, bf16[128,1024]{1,0:T(8,128)(2,1)S(1)} %bitcast.20), custom_call_target="tpu_custom_call" | custom-call | flops 50331648 | bytes 786432 | tf_op jit(solution)/shard_map/pallas_call | solution.py:435
  (69 shorter events, 17.9 us)
Async XLA Ops:
  2.9 16.9 %collective-permute-start.1 = (bf16[512,512]{1,0:T(8,128)(2,1)}, bf16[512,512]{1,0:T(8,128)(2,1)}, u32[]{:S(2)}, u32[]{:S(2)}) collective-permute-start(bf16[512,512]{1,0:T(8,128)(2,1)} %get-tuple-element.32.refs_2_), channel_id=1, source_target_pairs={{0,8},{1,9},{2,10},{3,11},{4,0},{5,1},{6,2},{7,3},{8,12},{9,13},{1... | collective-permute-start | bytes 1572872 | tf_op jit(solution)/shard_map/ppermute | solution.py:54
  6.9 25.1 %collective-permute-start.6 = (bf16[512,512]{1,0:T(8,128)(2,1)}, bf16[512,512]{1,0:T(8,128)(2,1)}, u32[]{:S(2)}, u32[]{:S(2)}) collective-permute-start(bf16[512,512]{1,0:T(8,128)(2,1)} %get-tuple-element.32.refs_2_), channel_id=1, source_target_pairs={{0,2},{1,3},{2,0},{3,1},{4,6},{5,7},{6,4},{7,5},{8,10},{9,11},{10,... | collective-permute-start | bytes 1572872 | tf_op jit(solution)/shard_map/ppermute | solution.py:54
  8.5 4.6 %copy-start.12 = (s32[1,2]{1,0:T(1,128)S(1)}, s32[1,2]{1,0:T(1,128)}, u32[]{:S(2)}) copy-start(s32[1,2]{1,0:T(1,128)} %param.12) | copy-start | bytes 28
  11.4 38.8 %collective-permute-start = (bf16[256,4096]{1,0:T(8,128)(2,1)}, bf16[256,4096]{1,0:T(8,128)(2,1)S(1)}, u32[]{:S(2)}, u32[]{:S(2)}) collective-permute-start(bf16[256,4096]{1,0:T(8,128)(2,1)} %shard_map.86), channel_id=1, source_target_pairs={{0,1},{1,0},{2,3},{3,2},{4,5},{5,4},{6,7},{7,6},{8,9},{9,8},{10,11... | collective-permute-start | bytes 6291464 | tf_op jit(solution)/shard_map/ppermute | solution.py:59
  11.5 20.0 %collective-permute-start.2 = (bf16[512,512]{1,0:T(8,128)(2,1)S(1)}, bf16[512,512]{1,0:T(8,128)(2,1)}, u32[]{:S(2)}, u32[]{:S(2)}) collective-permute-start(bf16[512,512]{1,0:T(8,128)(2,1)S(1)} %copy-done.7), channel_id=1, source_target_pairs={{8,0},{9,1},{10,2},{11,3},{0,4},{1,5},{2,6},{3,7},{12,8},{13,9},{1... | collective-permute-start | bytes 1572872 | tf_op jit(solution)/shard_map/ppermute | solution.py:54
  19.7 14.5 %collective-permute-start.4 = (bf16[512,512]{1,0:T(8,128)(2,1)}, bf16[512,512]{1,0:T(8,128)(2,1)S(1)}, u32[]{:S(2)}, u32[]{:S(2)}) collective-permute-start(bf16[512,512]{1,0:T(8,128)(2,1)} %collective-permute-done.1.refs_4_), channel_id=1, source_target_pairs={{0,2},{1,3},{2,0},{3,1},{4,6},{5,7},{6,4},{7,5},{8,10},{9,11},{10,... | collective-permute-start | bytes 1572872 | tf_op jit(solution)/shard_map/ppermute | solution.py:54
  21.1 13.3 %collective-permute-start.8 = (bf16[512,512]{1,0:T(8,128)(2,1)}, bf16[512,512]{1,0:T(8,128)(2,1)S(1)}, u32[]{:S(2)}, u32[]{:S(2)}) collective-permute-start(bf16[512,512]{1,0:T(8,128)(2,1)} %collective-permute-done.1.refs_4_), channel_id=1, source_target_pairs={{0,16},{16,0},{1,17},{17,1},{2,18},{18,2},{3,19},{19,3},{4,20},{20... | collective-permute-start | bytes 1572872 | tf_op jit(solution)/shard_map/ppermute | solution.py:54
  31.5 14.1 %collective-permute-start.3 = (bf16[512,512]{1,0:T(8,128)(2,1)}, bf16[512,512]{1,0:T(8,128)(2,1)S(1)}, u32[]{:S(2)}, u32[]{:S(2)}) collective-permute-start(bf16[512,512]{1,0:T(8,128)(2,1)} %collective-permute-done.1.refs_4_), channel_id=1, source_target_pairs={{0,8},{1,9},{2,10},{3,11},{4,0},{5,1},{6,2},{7,3},{8,12},{9,13},{1... | collective-permute-start | bytes 1572872 | tf_op jit(solution)/shard_map/ppermute | solution.py:54
  32.1 15.0 %collective-permute-start.7 = (bf16[512,512]{1,0:T(8,128)(2,1)}, bf16[512,512]{1,0:T(8,128)(2,1)}, u32[]{:S(2)}, u32[]{:S(2)}) collective-permute-start(bf16[512,512]{1,0:T(8,128)(2,1)} %collective-permute-done.2.refs_6_), channel_id=1, source_target_pairs={{0,2},{1,3},{2,0},{3,1},{4,6},{5,7},{6,4},{7,5},{8,10},{9,11},{10,... | collective-permute-start | bytes 1572872 | tf_op jit(solution)/shard_map/ppermute | solution.py:54
  34.2 12.9 %copy-start.8 = (bf16[512,512]{1,0:T(8,128)(2,1)}, bf16[512,512]{1,0:T(8,128)(2,1)S(1)}, u32[]{:S(2)}) copy-start(bf16[512,512]{1,0:T(8,128)(2,1)S(1)} %collective-permute-done.4.refs_5_) | copy-start | bytes 1572868
  34.4 13.3 %copy-start.9 = (bf16[512,512]{1,0:T(8,128)(2,1)}, bf16[512,512]{1,0:T(8,128)(2,1)S(1)}, u32[]{:S(2)}) copy-start(bf16[512,512]{1,0:T(8,128)(2,1)S(1)} %collective-permute-done.8.refs_10_) | copy-start | bytes 1572868
  34.4 13.3 %collective-permute-start.9 = (bf16[512,512]{1,0:T(8,128)(2,1)S(1)}, bf16[512,512]{1,0:T(8,128)(2,1)S(1)}, u32[]{:S(2)}, u32[]{:S(2)}) collective-permute-start(bf16[512,512]{1,0:T(8,128)(2,1)S(1)} %collective-permute-done.4.refs_5_), channel_id=1, source_target_pairs={{0,16},{16,0},{1,17},{17,1},{2,18},{18,2},{3,19},{19,3},{4,20},{20... | collective-permute-start | bytes 1572872 | tf_op jit(solution)/shard_map/ppermute | solution.py:54
  45.6 4.6 %copy-start.10 = (bf16[512,512]{1,0:T(8,128)(2,1)}, bf16[512,512]{1,0:T(8,128)(2,1)S(1)}, u32[]{:S(2)}) copy-start(bf16[512,512]{1,0:T(8,128)(2,1)S(1)} %collective-permute-done.3.refs_8_) | copy-start | bytes 1572868
  45.6 13.4 %collective-permute-start.5 = (bf16[512,512]{1,0:T(8,128)(2,1)S(1)}, bf16[512,512]{1,0:T(8,128)(2,1)}, u32[]{:S(2)}, u32[]{:S(2)}) collective-permute-start(bf16[512,512]{1,0:T(8,128)(2,1)S(1)} %collective-permute-done.3.refs_8_), channel_id=1, source_target_pairs={{0,2},{1,3},{2,0},{3,1},{4,6},{5,7},{6,4},{7,5},{8,10},{9,11},{10,... | collective-permute-start | bytes 1572872 | tf_op jit(solution)/shard_map/ppermute | solution.py:54
  47.8 12.6 %collective-permute-start.10 = (bf16[512,512]{1,0:T(8,128)(2,1)}, bf16[512,512]{1,0:T(8,128)(2,1)S(1)}, u32[]{:S(2)}, u32[]{:S(2)}) collective-permute-start(bf16[512,512]{1,0:T(8,128)(2,1)} %collective-permute-done.7.refs_7_), channel_id=1, source_target_pairs={{0,16},{16,0},{1,17},{17,1},{2,18},{18,2},{3,19},{19,3},{4,20},{20... | collective-permute-start | bytes 1572872 | tf_op jit(solution)/shard_map/ppermute | solution.py:54
  49.2 13.8 %collective-permute-start.11 = (bf16[512,512]{1,0:T(8,128)(2,1)}, bf16[512,512]{1,0:T(8,128)(2,1)}, u32[]{:S(2)}, u32[]{:S(2)}) collective-permute-start(bf16[512,512]{1,0:T(8,128)(2,1)} %get-tuple-element.47.refs_9_), channel_id=1, source_target_pairs={{8,0},{9,1},{10,2},{11,3},{0,4},{1,5},{2,6},{3,7},{12,8},{13,9},{1... | collective-permute-start | bytes 1572872 | tf_op jit(solution)/shard_map/ppermute | solution.py:54
  60.4 11.8 %collective-permute-start.14 = (bf16[512,512]{1,0:T(8,128)(2,1)}, bf16[512,512]{1,0:T(8,128)(2,1)S(1)}, u32[]{:S(2)}, u32[]{:S(2)}) collective-permute-start(bf16[512,512]{1,0:T(8,128)(2,1)} %collective-permute-done.5.refs_2_), channel_id=1, source_target_pairs={{0,16},{16,0},{1,17},{17,1},{2,18},{18,2},{3,19},{19,3},{4,20},{20... | collective-permute-start | bytes 1572872 | tf_op jit(solution)/shard_map/ppermute | solution.py:54
  61.9 11.5 %collective-permute-start.13 = (bf16[512,512]{1,0:T(8,128)(2,1)}, bf16[512,512]{1,0:T(8,128)(2,1)S(1)}, u32[]{:S(2)}, u32[]{:S(2)}) collective-permute-start(bf16[512,512]{1,0:T(8,128)(2,1)} %get-tuple-element.47.refs_9_), channel_id=1, source_target_pairs={{0,2},{1,3},{2,0},{3,1},{4,6},{5,7},{6,4},{7,5},{8,10},{9,11},{10,... | collective-permute-start | bytes 1572872 | tf_op jit(solution)/shard_map/ppermute | solution.py:54
  63.1 12.0 %collective-permute-start.12 = (bf16[512,512]{1,0:T(8,128)(2,1)}, bf16[512,512]{1,0:T(8,128)(2,1)S(1)}, u32[]{:S(2)}, u32[]{:S(2)}) collective-permute-start(bf16[512,512]{1,0:T(8,128)(2,1)} %collective-permute-done.11.refs_4_), channel_id=1, source_target_pairs={{8,0},{9,1},{10,2},{11,3},{0,4},{1,5},{2,6},{3,7},{12,8},{13,9},{1... | collective-permute-start | bytes 1572872 | tf_op jit(solution)/shard_map/ppermute | solution.py:54
  67.8 8.5 %collective-permute-start.16 = (f32[256,512]{1,0:T(8,128)S(1)}, f32[256,512]{1,0:T(8,128)S(1)}, u32[]{:S(2)}, u32[]{:S(2)}) collective-permute-start(f32[256,512]{1,0:T(8,128)S(1)} %get-tuple-element.53), channel_id=1, source_target_pairs={{0,1},{1,0},{2,3},{3,2},{4,5},{5,4},{6,7},{7,6},{8,9},{9,8},{10,11... | collective-permute-start | bytes 1572872 | tf_op jit(solution)/shard_map/ppermute | solution.py:59
  75.6 2.3 %collective-permute-start.15 = (f32[256,512]{1,0:T(8,128)S(1)}, f32[256,512]{1,0:T(8,128)S(1)}, u32[]{:S(2)}, u32[]{:S(2)}) collective-permute-start(f32[256,512]{1,0:T(8,128)S(1)} %shard_map.91), channel_id=1, source_target_pairs={{0,1},{1,0},{2,3},{3,2},{4,5},{5,4},{6,7},{7,6},{8,9},{9,8},{10,11... | collective-permute-start | bytes 1572872 | tf_op jit(solution)/shard_map/ppermute | solution.py:59
  76.3 8.1 %copy-start = (f32[256,256]{1,0:T(8,128)S(1)}, f32[256,256]{1,0:T(8,128)}, u32[]{:S(2)}) copy-start(f32[256,256]{1,0:T(8,128)} %concatenate.3.table_in.table_ref) | copy-start | bytes 786436
  76.3 8.1 %copy-start.1 = (bf16[256,4096]{1,0:T(8,128)(2,1)S(1)}, bf16[256,4096]{1,0:T(8,128)(2,1)}, u32[]{:S(2)}) copy-start(bf16[256,4096]{1,0:T(8,128)(2,1)} %query_ref.3) | copy-start | bytes 6291460
  80.0 14.4 %all-to-all-start = ((bf16[16,8,1024]{2,1,0:T(8,128)(2,1)}), bf16[16,8,1024]{2,1,0:T(8,128)(2,1)S(1)}, u32[]{:S(2)}, u32[]{:S(2)}) async-start(bf16[16,8,1024]{2,1,0:T(8,128)(2,1)} %bitcast.21), calls=%async_computation | async-start | bytes 524288 | tf_op jit(solution)/shard_map/all_to_all | solution.py:567
  (8 other events, 15.2 us)

commit v5 on v4

--- a/solution.py
+++ b/solution.py
@@ -129,7 +129,7 @@
     )(core, states)
 
 
-def accumulate(states, scalars, pieces, places, bias=None, start=None, later=0):
+def accumulate(states, scalars, pieces, places, bias=None, start=None, later=0, table=None, rows=0):
     count = len(pieces)
     depth, columns = pieces[0].shape
     tokens = states[0].shape[0]
@@ -141,7 +141,8 @@
         piece_refs, refs = refs[:count], refs[count:]
         start_refs, refs = refs[:begun], refs[begun:]
         if later:
-            totals, lefts, refs = refs[:4], refs[4:6], refs[6:]
+            table_in, totals, lefts, pick_ref = refs[0], refs[1:5], refs[5:7], refs[7]
+            table_ref, refs = refs[8], refs[9:]
         else:
             outs, totals, refs = refs[:4], refs[4:8], refs[8:]
         left, right, bias_ref, sems = refs
@@ -175,8 +176,17 @@
             for i in range(later)
             for side in range(2)
         ]
+        if later:
+            table_copy = begin(table_in, table_ref)
         for copy in first:
             copy.wait()
+        if later:
+            table_copy.wait()
+            destination = table_ref[:, DESTINATION : DESTINATION + 1].astype(jnp.int32)
+            token = lax.broadcasted_iota(jnp.int32, (tokens, rows), 0)
+            row = lax.broadcasted_iota(jnp.int32, (tokens, rows), 1)
+            match = (destination == row // SPAN) & (token % SPAN == row % SPAN)
+            pick_ref[...] = jnp.where(match, 1.0, 0.0).astype(jnp.bfloat16)
         touched = [start is not None] * 4
         for i in range(0, count, batch):
             stop = min(i + batch, count)
@@ -215,11 +225,13 @@
     if later:
         out_shape = [jax.ShapeDtypeStruct(sums, jnp.float32)] * 4
         out_shape += [jax.ShapeDtypeStruct((tokens, later * depth), jnp.bfloat16)] * 2
-        out_specs, scratch = [inside] * 6, []
+        out_shape += [jax.ShapeDtypeStruct((tokens, rows), jnp.bfloat16)]
+        out_specs, scratch = [inside] * 7, [pltpu.VMEM(table.shape, table.dtype)]
     else:
         out_shape = [pltpu.HBM(sums, jnp.float32)] * 4
         out_specs, scratch = [outside] * 4, [pltpu.VMEM(sums, jnp.float32)] * 4
     outer = [*states, *pieces, *((bias,) if start is None else start)]
+    outer += [table] if later else []
     return pl.pallas_call(
         kernel,
         out_shape=out_shape,
@@ -269,82 +281,86 @@
     )(left, total, *pieces)
 
 
-def finish(own_part, peer_part, table, replicas, earlier=None):
+def finish(own_part, peer_part, pick, earlier=None):
     tokens, columns = own_part.shape
-    keys = columns // 2
-    rows = replicas * SPAN
-
-    def kernel(own_ref, peer_ref, table_in, *refs):
-        kv_ref, key_ref, out_ref, table_ref, sem = refs[-5:]
-        copy = pltpu.make_async_copy(table_in, table_ref, sem)
-        copy.start()
-        kv = (own_ref[...] + peer_ref[...]).astype(jnp.bfloat16).astype(jnp.float32)
-        copy.wait()
-        kv = jnp.where(table_ref[:, LIVE : LIVE + 1] > 0.5, kv, 0.0)
-        kept = kv.astype(jnp.bfloat16)
-        kv_ref[...] = kept
-        destination = table_ref[:, DESTINATION : DESTINATION + 1].astype(jnp.int32)
-        token = lax.broadcasted_iota(jnp.int32, (tokens, rows), 0)
-        row = lax.broadcasted_iota(jnp.int32, (tokens, rows), 1)
-        match = (destination == row // SPAN) & (token % SPAN == row % SPAN)
-        pick = jnp.where(match, 1.0, 0.0).astype(jnp.bfloat16)
+    rows = pick.shape[1]
+    last = earlier is not None
+
+    def kernel(own_ref, peer_ref, pick_ref, *refs):
+        if last:
+            earlier_ref, kv_ref, out_ref, spans_ref, sems = refs
+            first = pltpu.make_async_copy(
+                earlier_ref, out_ref.at[:, pl.ds(0, columns)], sems.at[0]
+            )
+            first.start()
+        else:
+            kv_ref, spans_ref = refs
+        kv = (own_ref[...] + peer_ref[...]).astype(jnp.bfloat16)
+        kv_ref[...] = kv
         over_tokens = (((0,), (0,)), ((), ()))
         found = lax.dot_general(
-            pick,
+            pick_ref[...],
             jnp.ones((tokens, HEAD), jnp.bfloat16),
             over_tokens,
             preferred_element_type=jnp.float32,
         )
-        spans = lax.dot_general(pick, kept, over_tokens, preferred_element_type=jnp.float32)
-        spans = jnp.where(found[:, :1] > 0.5, spans, ABSENT).astype(jnp.bfloat16)
-        if earlier is None:
-            out_ref[...] = spans
-        else:
-            out_ref[:, :columns] = refs[0][...]
-            out_ref[:, columns:] = spans
-        cosine, sine = table_ref[:, : HEAD // 2], table_ref[:, HEAD // 2 : HEAD]
-        cosine = jnp.concatenate([cosine, cosine], axis=1)
-        sine = jnp.concatenate([-sine, sine], axis=1)
-        for head in range(keys // HEAD):
-            part = kv[:, head * HEAD : (head + 1) * HEAD]
-            turned = part * cosine + pltpu.roll(part, HEAD // 2, 1) * sine
-            key_ref[:, head * HEAD : (head + 1) * HEAD] = turned.astype(jnp.bfloat16)
+        spans = lax.dot_general(
+            pick_ref[...], kv, over_tokens, preferred_element_type=jnp.float32
+        )
+        spans_ref[...] = jnp.where(found[:, :1] > 0.5, spans, ABSENT).astype(jnp.bfloat16)
+        if last:
+            second = pltpu.make_async_copy(
+                spans_ref, out_ref.at[:, pl.ds(columns, columns)], sems.at[1]
+            )
+            second.start()
+            first.wait()
+            second.wait()
 
     inside = pl.BlockSpec(memory_space=pltpu.VMEM)
-    sent = columns if earlier is None else 2 * columns
-    more = () if earlier is None else (earlier,)
+    kv_shape = jax.ShapeDtypeStruct((tokens, columns), jnp.bfloat16)
+    if last:
+        out_shape = (kv_shape, pltpu.HBM((rows, 2 * columns), jnp.bfloat16))
+        out_specs = (inside, pl.BlockSpec(memory_space=pltpu.HBM))
+        scratch = [pltpu.VMEM((rows, columns), jnp.bfloat16), pltpu.SemaphoreType.DMA((2,))]
+    else:
+        out_shape = (kv_shape, jax.ShapeDtypeStruct((rows, columns), jnp.bfloat16))
+        out_specs, scratch = (inside, inside), []
+    more = (earlier,) if last else ()
     return pl.pallas_call(
         kernel,
-        out_shape=(
-            jax.ShapeDtypeStruct((tokens, columns), jnp.bfloat16),
-            jax.ShapeDtypeStruct((tokens, keys), jnp.bfloat16),
-            jax.ShapeDtypeStruct((rows, sent), jnp.bfloat16),
-        ),
-        in_specs=[inside] * 2 + [pl.BlockSpec(memory_space=pltpu.HBM)] + [inside] * len(more),
-        out_specs=(inside,) * 3,
-        scratch_shapes=[pltpu.VMEM(table.shape, table.dtype), pltpu.SemaphoreType.DMA],
+        out_shape=out_shape,
+        in_specs=[inside] * (3 + len(more)),
+        out_specs=out_specs,
+        scratch_shapes=scratch,
         compiler_params=pltpu.CompilerParams(vmem_limit_bytes=LIMIT),
         cost_estimate=pl.CostEstimate(
             flops=2 * rows * tokens * columns,
             bytes_accessed=10 * tokens * columns,
             transcendentals=0,
         ),
-    )(own_part, peer_part, pltpu.with_memory_space_constraint(table, pltpu.HBM), *more)
-
-
-def attend(half, flip, mask, table, queries, keys, kv, context=None):
+    )(own_part, peer_part, pick, *more)
+
+
+def attend(half, flip, mask, table, queries, kv, context=None):
     tokens = queries.shape[0]
-    heads = keys.shape[1] // HEAD
+    heads = kv.shape[1] // (2 * HEAD)
     width = queries.shape[1] // (2 * heads)
 
     def kernel(half_ref, mask_ref, table_ref, query_ref, key_ref, value_ref, *refs):
         context_ref = refs[-1]
         scale = HEAD**-0.5 * math.log2(math.e)
         lanes = [slice(h * HEAD, (h + 1) * HEAD) for h in range(width // HEAD)]
+        is_live = table_ref[:, LIVE : LIVE + 1] > 0.5
+        cosine, sine = table_ref[:, : HEAD // 2], table_ref[:, HEAD // 2 : HEAD]
+        cosine = jnp.concatenate([cosine, cosine], axis=1)
+        sine = jnp.concatenate([-sine, sine], axis=1)
+        key = jnp.where(is_live, key_ref[...].astype(jnp.float32), 0.0)
+        key = (key * cosine + pltpu.roll(key, HEAD // 2, 1) * sine).astype(jnp.bfloat16)
+        value = jnp.where(is_live, value_ref[...].astype(jnp.float32), 0.0).astype(jnp.bfloat16)
         scores = [
             lax.dot_general(
                 query_ref[:, lane],
-                key_ref[...],
+                key,
                 (((1,), (1,)), ((), ())),
                 preferred_element_type=jnp.float32,
             )
@@ -356,9 +372,8 @@
             weight = jnp.exp2(score - jnp.max(score, axis=1, keepdims=True))
             inverse = 1.0 / jnp.sum(weight, axis=1, keepdims=True)
             weights.append((weight * inverse).astype(jnp.bfloat16))
-        is_live = table_ref[:, LIVE - HEAD : LIVE - HEAD + 1] > 0.5
         for lane, weight in zip(lanes, weights):
-            mixed = jnp.dot(weight, value_ref[...], preferred_element_type=jnp.float32)
+            mixed = jnp.dot(weight, value, preferred_element_type=jnp.float32)
             context_ref[:, lane] = jnp.where(is_live, mixed, 0.0).astype(jnp.bfloat16)
 
     def wide_at(i, s):
@@ -366,12 +381,12 @@
 
     in_specs = [
         pl.BlockSpec((tokens, tokens), lambda i, s: (0, 0)),
-        pl.BlockSpec((tokens, HEAD), lambda i, s: (0, 1)),
+        pl.BlockSpec(table.shape, lambda i, s: (0, 0)),
         pl.BlockSpec((tokens, width), wide_at),
         pl.BlockSpec((tokens, HEAD), lambda i, s: (0, i)),
         pl.BlockSpec((tokens, HEAD), lambda i, s: (0, heads + i)),
     ]
-    arguments = [half, mask, table, queries, keys, kv]
+    arguments = [half, mask, table, queries, kv, kv]
     if context is not None:
         in_specs.append(pl.BlockSpec(memory_space=pl.ANY))
         arguments.append(context)
@@ -399,37 +414,39 @@
     slots, width = spans.shape
     part = width // 4
 
-    def kernel(scalar_ref, table_ref, mine_ref, other_ref, spans_ref, out_ref, total_ref):
-        @pl.when(pl.program_id(0) == 0)
-        def _():
-            present = spans_ref[:, :HEAD].astype(jnp.float32)
-            present = jnp.where(present > 0.5 * ABSENT, 0.0, 1.0)
-            row = lax.broadcasted_iota(jnp.int32, (slots, slots), 0)
-            column = lax.broadcasted_iota(jnp.int32, (slots, slots), 1)
-            before = (column // SPAN < row // SPAN) & (column % SPAN == 0)
-            before = jnp.where(before, 1.0, 0.0).astype(jnp.bfloat16)
-            earlier = jnp.dot(
-                before, present.astype(jnp.bfloat16), preferred_element_type=jnp.float32
-            )
-            rank = earlier[:, :1].astype(jnp.int32) + scalar_ref[1]
-            target = lax.broadcasted_iota(jnp.int32, (slots, rows), 1)
-            sender = lax.broadcasted_iota(jnp.int32, (slots, rows), 0)
-            hit = (target // SPAN == rank) & (target % SPAN == sender % SPAN)
-            hit = jnp.where(hit & (present[:, :1] > 0.5), 1.0, 0.0).astype(jnp.bfloat16)
-            moved = lax.dot_general(
-                hit, spans_ref[...], (((0,), (0,)), ((), ())), preferred_element_type=jnp.float32
-            ).astype(jnp.bfloat16)
-            keep = table_ref[:, KEEP : KEEP + 1] > 0.5
-            for i in range(4):
-                home = (mine_ref, other_ref)[i // 2][:, (i % 2) * part : (i % 2 + 1) * part]
-                home = home.astype(jnp.float32)
-                came = moved[:, i * part : (i + 1) * part].astype(jnp.float32)
-                total_ref[i] = jnp.where(keep, home, came).astype(jnp.bfloat16)
-
-        out_ref[...] = total_ref[pl.program_id(0)]
-
-    def out_at(i, s):
-        return (0, 2 * (i % 2) + jnp.where(i < 2, s[0], 1 - s[0]))
+    def kernel(scalar_ref, table_ref, mine_ref, other_ref, spans_ref, out_ref, total_ref, sems):
+        present = spans_ref[:, :HEAD].astype(jnp.float32)
+        present = jnp.where(present > 0.5 * ABSENT, 0.0, 1.0)
+        row = lax.broadcasted_iota(jnp.int32, (slots, slots), 0)
+        column = lax.broadcasted_iota(jnp.int32, (slots, slots), 1)
+        before = (column // SPAN < row // SPAN) & (column % SPAN == 0)
+        before = jnp.where(before, 1.0, 0.0).astype(jnp.bfloat16)
+        earlier = jnp.dot(before, present.astype(jnp.bfloat16), preferred_element_type=jnp.float32)
+        rank = earlier[:, :1].astype(jnp.int32) + scalar_ref[1]
+        target = lax.broadcasted_iota(jnp.int32, (slots, rows), 1)
+        sender = lax.broadcasted_iota(jnp.int32, (slots, rows), 0)
+        hit = (target // SPAN == rank) & (target % SPAN == sender % SPAN)
+        hit = jnp.where(hit & (present[:, :1] > 0.5), 1.0, 0.0).astype(jnp.bfloat16)
+        keep = table_ref[:, KEEP : KEEP + 1] > 0.5
+        copies = []
+        for i in range(4):
+            lanes = slice(i * part, (i + 1) * part)
+            came = lax.dot_general(
+                hit,
+                spans_ref[:, lanes],
+                (((0,), (0,)), ((), ())),
+                preferred_element_type=jnp.float32,
+            )
+            home = (mine_ref, other_ref)[i // 2][:, (i % 2) * part : (i % 2 + 1) * part]
+            total_ref[i] = jnp.where(keep, home.astype(jnp.float32), came).astype(jnp.bfloat16)
+            which = scalar_ref[0] if i < 2 else 1 - scalar_ref[0]
+            at = pl.multiple_of((2 * (i % 2) + which) * part, HEAD)
+            copies.append(
+                pltpu.make_async_copy(total_ref.at[i], out_ref.at[:, pl.ds(at, part)], sems.at[i])
+            )
+            copies[-1].start()
+        for copy in copies:
+            copy.wait()
 
     home = pl.BlockSpec((rows, width // 2), lambda i, s: (0, 0))
     return pl.pallas_call(
@@ -437,15 +454,18 @@
         out_shape=jax.ShapeDtypeStruct((rows, width), jnp.bfloat16),
         grid_spec=pltpu.PrefetchScalarGridSpec(
             num_scalar_prefetch=1,
-            grid=(4,),
+            grid=(1,),
             in_specs=[
                 pl.BlockSpec((rows, table.shape[1]), lambda i, s: (0, 0)),
                 home,
                 home,
                 pl.BlockSpec((slots, width), lambda i, s: (0, 0)),
             ],
-            out_specs=pl.BlockSpec((rows, part), out_at),
-            scratch_shapes=[pltpu.VMEM((4, rows, part), jnp.bfloat16)],
+            out_specs=pl.BlockSpec(memory_space=pl.ANY),
+            scratch_shapes=[
+                pltpu.VMEM((4, rows, part), jnp.bfloat16),
+                pltpu.SemaphoreType.DMA((4,)),
+            ],
         ),
         compiler_params=pltpu.CompilerParams(vmem_limit_bytes=LIMIT),
         cost_estimate=pl.CostEstimate(
@@ -543,13 +563,15 @@
             late.append((links.send(other_weight, "y", sums), block(0, True)))
             late.append((links.send(crossed, "x", sums), block(k, True)))
             middle = [(crossed, block(k, True))] + middle
-            mine_peer, mine_own, other_peer, other_own, left_peer, left_own = accumulate(
+            mine_peer, mine_own, other_peer, other_own, left_peer, left_own, pick = accumulate(
                 both,
                 listed(middle + late),
                 [p for p, _ in middle],
                 [0] + [1] * (len(middle) - 1),
                 start=sums,
                 later=len(late),
+                table=table,
+                rows=replicas * SPAN,
             )
         else:
             mine.append((crossed, block(k, True)))
@@ -561,13 +583,13 @@
     other_peer = core_swap(complete(left_peer, last, other_peer), replicas)
     other_own = complete(left_own, last, other_own)
     mine_own = after(mine_own, other_own)
-    mine_kv, mine_keys, mine_spans = finish(mine_own, mine_peer, table, replicas)
-    other_kv, other_keys, spans = finish(other_own, other_peer, table, replicas, mine_spans)
+    mine_kv, mine_spans = finish(mine_own, mine_peer, pick)
+    other_kv, spans = finish(other_own, other_peer, pick, mine_spans)
     spans = spans.reshape(replicas, SPAN, width)
     spans = lax.all_to_all(spans, "dp", split_axis=0, concat_axis=0, tiled=True)
     spans = spans.reshape(replicas * SPAN, width)
-    context = attend(half, False, mask, table, queries, mine_keys, mine_kv)
-    context = attend(half, True, mask, table, queries, other_keys, other_kv, context)
+    context = attend(half, False, mask, table, queries, mine_kv)
+    context = attend(half, True, mask, table, queries, other_kv, context)
     work_rows = place(scalars, table, mine_kv, other_kv, spans)
     return (context, work_rows)
 

time: 97.2 us -> 93.8 us (0.965)
  waiting for transfers between devices: 28.7 us -> 27 us
  Pallas kernels: 29.5 us -> 28.4 us
    ppermute x14, waiting for transfers between devices: 25.8 us -> 22.8 us  [send(): sent.append(lax.ppermute(after(value, *before), axis, pairs))]
    pallas_call x2, Pallas kernels: 2.98 us -> 1.28 us  [finish(): pl.pallas_call(kernel, out_shape=out_shape, in_specs=[inside] * (3 + len(...]
    unnamed x28 -> x18, local copies, waits for them, and re-layouts: 2.94 us -> 2.14 us
  transfers between devices with their start and end apart: 18 -> 18, of which waited for: 10 -> 11; matrix products, arithmetic and copies ran while one was open for 7% -> 7% of each run, Pallas kernels for 24% -> 25%
where the time goes in v5:
time: 93.8 us; the launch traced here: 93.4 us
  Pallas kernels  28.4 us (30%)
  waiting for transfers between devices  27 us (29%)
  starting transfers between devices  24.2 us (26%)
  between operations  5.38 us (6%)
  other arithmetic  4.44 us (5%)
  local copies, waits for them, and re-layouts  3.97 us (4%)
    ppermute x14, waiting for transfers between devices, send(): sent.append(lax.ppermute(after(value, *before), axis, pairs))  22.8 us
    ppermute x14, starting transfers between devices, send(): sent.append(lax.ppermute(after(value, *before), axis, pairs))  19.8 us
    pallas_call x2, Pallas kernels, accumulate(): pl.pallas_call(kernel, out_shape=out_shape, in_specs=[pl.BlockSpec(memory...  12.3 us
    pallas_call x2, Pallas kernels, attend(): pl.pallas_call(kernel, out_shape=jax.ShapeDtypeStruct(queries.shape, jnp....  6.78 us
    all_to_all x1, starting transfers between devices, per_device(): spans = lax.all_to_all(spans, 'dp', split_axis=0, concat_axis=0, tiled=True)  4.19 us
    all_to_all x1, waiting for transfers between devices, per_device(): spans = lax.all_to_all(spans, 'dp', split_axis=0, concat_axis=0, tiled=True)  3.25 us
    pallas_call x1, Pallas kernels, core_columns(): pl.pallas_call(kernel, out_shape=jax.ShapeDtypeStruct((tokens, width // 2...  2.93 us
    pallas_call x1, Pallas kernels, halves(): pl.pallas_call(kernel, out_shape=(out, out), in_specs=[pl.BlockSpec(memor...  2.23 us
  transfers between devices with their start and end apart: 18, of which 11 were waited for; matrix products, arithmetic and copies ran while one was open for 7% of the time, Pallas kernels for 25%

profile of v5, /device:TPU:0, one launch (start us, length us, event | category | flops | bytes accessed | tf_op | source)
XLA Modules:
  0.0 93.4 jit_solution(5035551392799136744)
XLA Ops:
  0.6 2.2 %shard_map.87 = (bf16[512,512]{1,0:T(8,128)(2,1)}, bf16[512,512]{1,0:T(8,128)(2,1)}) custom-call(s32[1]{0:T(128)} %bitcast.half_ref, bf16[512,1024]{1,0:T(8,128)(2,1)} %weight_ref.1), custom_call_target="tpu_custom_call" | custom-call | bytes 2097152 | tf_op jit(solution)/shard_map/pallas_call | solution.py:87
  2.9 4.1 %collective-permute-start.1 = (bf16[512,512]{1,0:T(8,128)(2,1)}, bf16[512,512]{1,0:T(8,128)(2,1)}, u32[]{:S(2)}, u32[]{:S(2)}) collective-permute-start(bf16[512,512]{1,0:T(8,128)(2,1)} %get-tuple-element.31.refs_2_), channel_id=1, source_target_pairs={{0,8},{1,9},{2,10},{3,11},{4,0},{5,1},{6,2},{7,3},{8,12},{9,13},{1... | collective-permute-start | bytes 1572872 | tf_op jit(solution)/shard_map/ppermute | solution.py:54
  7.0 1.5 %collective-permute-start.6 = (bf16[512,512]{1,0:T(8,128)(2,1)}, bf16[512,512]{1,0:T(8,128)(2,1)}, u32[]{:S(2)}, u32[]{:S(2)}) collective-permute-start(bf16[512,512]{1,0:T(8,128)(2,1)} %get-tuple-element.31.refs_2_), channel_id=1, source_target_pairs={{0,2},{1,3},{2,0},{3,1},{4,6},{5,7},{6,4},{7,5},{8,10},{9,11},{10,... | collective-permute-start | bytes 1572872 | tf_op jit(solution)/shard_map/ppermute | solution.py:54
  8.5 2.9 %shard_map.86 = bf16[256,4096]{1,0:T(8,128)(2,1)} custom-call(s32[1]{0:T(128)S(6)} %sub.93.core_ref, bf16[256,8192]{1,0:T(8,128)(2,1)} %refs_1_.3), custom_call_target="tpu_custom_call" | custom-call | bytes 4194304 | tf_op jit(solution)/shard_map/pallas_call | solution.py:120
  19.7 1.5 %collective-permute-start.4 = (bf16[512,512]{1,0:T(8,128)(2,1)}, bf16[512,512]{1,0:T(8,128)(2,1)S(1)}, u32[]{:S(2)}, u32[]{:S(2)}) collective-permute-start(bf16[512,512]{1,0:T(8,128)(2,1)} %collective-permute-done.1.refs_4_), channel_id=1, source_target_pairs={{0,2},{1,3},{2,0},{3,1},{4,6},{5,7},{6,4},{7,5},{8,10},{9,11},{10,... | collective-permute-start | bytes 1572872 | tf_op jit(solution)/shard_map/ppermute | solution.py:54
  21.2 1.5 %collective-permute-start.8 = (bf16[512,512]{1,0:T(8,128)(2,1)}, bf16[512,512]{1,0:T(8,128)(2,1)S(1)}, u32[]{:S(2)}, u32[]{:S(2)}) collective-permute-start(bf16[512,512]{1,0:T(8,128)(2,1)} %collective-permute-done.1.refs_4_), channel_id=1, source_target_pairs={{0,16},{16,0},{1,17},{17,1},{2,18},{18,2},{3,19},{19,3},{4,20},{20... | collective-permute-start | bytes 1572872 | tf_op jit(solution)/shard_map/ppermute | solution.py:54
  25.3 6.2 %collective-permute-done.2.refs_6_ = bf16[512,512]{1,0:T(8,128)(2,1)} collective-permute-done((bf16[512,512]{1,0:T(8,128)(2,1)}, bf16[512,512]{1,0:T(8,128)(2,1)}, u32[]{:S(2)}, u32[]{:S(2)}) %collective-permute-start.2) | collective-permute-done | bytes 524320 | tf_op jit(solution)/shard_map/ppermute | solution.py:54
  32.1 1.5 %collective-permute-start.7 = (bf16[512,512]{1,0:T(8,128)(2,1)}, bf16[512,512]{1,0:T(8,128)(2,1)}, u32[]{:S(2)}, u32[]{:S(2)}) collective-permute-start(bf16[512,512]{1,0:T(8,128)(2,1)} %collective-permute-done.2.refs_6_), channel_id=1, source_target_pairs={{0,2},{1,3},{2,0},{3,1},{4,6},{5,7},{6,4},{7,5},{8,10},{9,11},{10,... | collective-permute-start | bytes 1572872 | tf_op jit(solution)/shard_map/ppermute | solution.py:54
  34.3 1.5 %collective-permute-start.9 = (bf16[512,512]{1,0:T(8,128)(2,1)S(1)}, bf16[512,512]{1,0:T(8,128)(2,1)S(1)}, u32[]{:S(2)}, u32[]{:S(2)}) collective-permute-start(bf16[512,512]{1,0:T(8,128)(2,1)S(1)} %collective-permute-done.4.refs_5_), channel_id=1, source_target_pairs={{0,16},{16,0},{1,17},{17,1},{2,18},{18,2},{3,19},{19,3},{4,20},{20... | collective-permute-start | bytes 1572872 | tf_op jit(solution)/shard_map/ppermute | solution.py:54
  35.8 9.9 %collective-permute-done.3.refs_8_ = bf16[512,512]{1,0:T(8,128)(2,1)} collective-permute-done((bf16[512,512]{1,0:T(8,128)(2,1)}, bf16[512,512]{1,0:T(8,128)(2,1)}, u32[]{:S(2)}, u32[]{:S(2)}) %collective-permute-start.3) | collective-permute-done | bytes 524320 | tf_op jit(solution)/shard_map/ppermute | solution.py:54
  45.7 1.3 %collective-permute-start.11 = (bf16[512,512]{1,0:T(8,128)(2,1)}, bf16[512,512]{1,0:T(8,128)(2,1)}, u32[]{:S(2)}, u32[]{:S(2)}) collective-permute-start(bf16[512,512]{1,0:T(8,128)(2,1)} %get-tuple-element.46.refs_9_), channel_id=1, source_target_pairs={{8,0},{9,1},{10,2},{11,3},{0,4},{1,5},{2,6},{3,7},{12,8},{13,9},{1... | collective-permute-start | bytes 1572872 | tf_op jit(solution)/shard_map/ppermute | solution.py:54
  47.0 1.5 %collective-permute-start.5 = (bf16[512,512]{1,0:T(8,128)(2,1)}, bf16[512,512]{1,0:T(8,128)(2,1)}, u32[]{:S(2)}, u32[]{:S(2)}) collective-permute-start(bf16[512,512]{1,0:T(8,128)(2,1)} %collective-permute-done.3.refs_8_), channel_id=1, source_target_pairs={{0,2},{1,3},{2,0},{3,1},{4,6},{5,7},{6,4},{7,5},{8,10},{9,11},{10,... | collective-permute-start | bytes 1572872 | tf_op jit(solution)/shard_map/ppermute | solution.py:54
  49.4 1.5 %collective-permute-start.10 = (bf16[512,512]{1,0:T(8,128)(2,1)}, bf16[512,512]{1,0:T(8,128)(2,1)S(1)}, u32[]{:S(2)}, u32[]{:S(2)}) collective-permute-start(bf16[512,512]{1,0:T(8,128)(2,1)} %collective-permute-done.7.refs_7_), channel_id=1, source_target_pairs={{0,16},{16,0},{1,17},{17,1},{2,18},{18,2},{3,19},{19,3},{4,20},{20... | collective-permute-start | bytes 1572872 | tf_op jit(solution)/shard_map/ppermute | solution.py:54
  51.0 1.3 %copy-done.2 = bf16[256,4096]{1,0:T(8,128)(2,1)} copy-done((bf16[256,4096]{1,0:T(8,128)(2,1)}, bf16[256,4096]{1,0:T(8,128)(2,1)S(1)}, u32[]{:S(2)}) %copy-start.2) | copy-done | bytes 2097176
  52.3 7.5 %shard_map.88 = (f32[256,512]{1,0:T(8,128)}, f32[256,512]{1,0:T(8,128)}, f32[256,512]{1,0:T(8,128)}, f32[256,512]{1,0:T(8,128)}) custom-call(s32[12]{0:T(128)S(1)} %stack.58.scalar_ref, bf16[256,4096]{1,0:T(8,128)(2,1)} %copy-done.2, bf16[256,8192]{1,0:T(8,128)(2,1)} %refs_1_.3, bf16[512,512]{1,0:T(8,128)(2,1)} %get-tuple-element.31.refs_2_, ...), custom_call_target="tpu_custom_call" | custom-call | flops 2684354560 | bytes 10485760 | tf_op jit(solution)/shard_map/pallas_call | solution.py:235
  60.0 1.6 %collective-permute-start.12 = (bf16[512,512]{1,0:T(8,128)(2,1)}, bf16[512,512]{1,0:T(8,128)(2,1)S(1)}, u32[]{:S(2)}, u32[]{:S(2)}) collective-permute-start(bf16[512,512]{1,0:T(8,128)(2,1)} %collective-permute-done.11.refs_4_), channel_id=1, source_target_pairs={{8,0},{9,1},{10,2},{11,3},{0,4},{1,5},{2,6},{3,7},{12,8},{13,9},{1... | collective-permute-start | bytes 1572872 | tf_op jit(solution)/shard_map/ppermute | solution.py:54
  62.0 1.2 %collective-permute-start.14 = (bf16[512,512]{1,0:T(8,128)(2,1)}, bf16[512,512]{1,0:T(8,128)(2,1)S(1)}, u32[]{:S(2)}, u32[]{:S(2)}) collective-permute-start(bf16[512,512]{1,0:T(8,128)(2,1)} %collective-permute-done.5.refs_2_), channel_id=1, source_target_pairs={{0,16},{16,0},{1,17},{17,1},{2,18},{18,2},{3,19},{19,3},{4,20},{20... | collective-permute-start | bytes 1572872 | tf_op jit(solution)/shard_map/ppermute | solution.py:54
  63.3 4.9 %shard_map.89 = (f32[256,512]{1,0:T(8,128)S(1)}, f32[256,512]{1,0:T(8,128)S(1)}, f32[256,512]{1,0:T(8,128)S(1)}, f32[256,512]{1,0:T(8,128)S(1)}, bf16[256,1536]{...) custom-call(s32[8]{0:T(128)S(1)} %stack.51.scalar_ref, bf16[256,4096]{1,0:T(8,128)(2,1)} %copy-done.2, ...), custom_call_target="tpu_custom_call" | custom-call | flops 805306368 | bytes 3145728 | tf_op jit(solution)/shard_map/pallas_call | solution.py:235
  68.2 5.0 %collective-permute-done.12.refs_0_ = bf16[512,512]{1,0:T(8,128)(2,1)S(1)} collective-permute-done((bf16[512,512]{1,0:T(8,128)(2,1)}, bf16[512,512]{1,0:T(8,128)(2,1)S(1)}, u32[]{:S(2)}, u32[]{:S(2)}) %collective-permute-start.12) | collective-permute-done | bytes 524320 | tf_op jit(solution)/shard_map/ppermute | solution.py:54
  77.4 4.2 %all-to-all-start = ((bf16[16,8,1024]{2,1,0:T(8,128)(2,1)}), bf16[16,8,1024]{2,1,0:T(8,128)(2,1)S(1)}, u32[]{:S(2)}, u32[]{:S(2)}) async-start(bf16[16,8,1024]{2,1,0:T(8,128)(2,1)} %bitcast.21), calls=%async_computation | async-start | bytes 524288 | tf_op jit(solution)/shard_map/all_to_all | solution.py:589
  81.6 3.4 %shard_map.94.refs_0_ = bf16[256,4096]{1,0:T(8,128)(2,1)} custom-call(s32[1]{0:T(128)} %bitcast.half_ref, f32[256,256]{1,0:T(8,128)S(1)} %fusion.3.mask_ref, f32[256,256]{1,0:T(8,128)S(1)} %copy-done.1, bf16[256,4096]{1,0:T(8,128)(2,1)S(1)} %copy-done, bf16[256,512]{1,0:T(8,128)(2,1)S(1)} %get-tuple-element.56.key_ref.value_ref.mine_ref, ...), custom_call_target="tpu_custom_call" | custom-call | flops 536870912 | bytes 2097152 | tf_op jit(solution)/shard_map/pallas_call | solution.py:393
  85.0 3.4 %shard_map.95 = bf16[256,4096]{1,0:T(8,128)(2,1)} custom-call(s32[1]{0:T(128)} %bitcast.half_ref, f32[256,256]{1,0:T(8,128)S(1)} %fusion.3.mask_ref, f32[256,256]{1,0:T(8,128)S(1)} %copy-done.1, bf16[256,4096]{1,0:T(8,128)(2,1)S(1)} %copy-done, bf16[256,512]{1,0:T(8,128)(2,1)S(1)} %get-tuple-element.55.key_ref.value_ref.other_ref, ...), custom_call_target="tpu_custom_call", output_to_operand_aliasing={{}: (6, {})} | custom-call | flops 536870912 | bytes 2097152 | tf_op jit(solution)/shard_map/pallas_call | solution.py:393
  88.4 3.2 %all-to-all-done = bf16[16,8,1024]{2,1,0:T(8,128)(2,1)S(1)} async-done(((bf16[16,8,1024]{2,1,0:T(8,128)(2,1)}), bf16[16,8,1024]{2,1,0:T(8,128)(2,1)S(1)}, u32[]{:S(2)}, u32[]{:S(2)}) %all-to-all-start) | async-done | bytes 262176 | tf_op jit(solution)/shard_map/all_to_all | solution.py:589
  91.6 1.8 %shard_map.96 = bf16[192,1024]{1,0:T(8,128)(2,1)} custom-call(s32[2]{0:T(128)S(1)} %pad_add_fusion.scalar_ref, f32[256,256]{1,0:T(8,128)S(1)} %copy-done.1, bf16[256,512]{1,0:T(8,128)(2,1)S(1)} %get-tuple-element.56.key_ref.value_ref.mine_ref, bf16[256,512]{1,0:T(8,128)(2,1)S(1)} %get-tuple-element.55.key_ref.value_ref.other_ref, bf16[128,1024]{1,0:T(8,128)(2,1)S(1)} %bitcast.20), custom_call_target="tpu_custom_call" | custom-call | flops 50331648 | bytes 786432 | tf_op jit(solution)/shard_map/pallas_call | solution.py:452
  (59 shorter events, 13.4 us)
Async XLA Ops:
  2.9 16.8 %collective-permute-start.1 = (bf16[512,512]{1,0:T(8,128)(2,1)}, bf16[512,512]{1,0:T(8,128)(2,1)}, u32[]{:S(2)}, u32[]{:S(2)}) collective-permute-start(bf16[512,512]{1,0:T(8,128)(2,1)} %get-tuple-element.31.refs_2_), channel_id=1, source_target_pairs={{0,8},{1,9},{2,10},{3,11},{4,0},{5,1},{6,2},{7,3},{8,12},{9,13},{1... | collective-permute-start | bytes 1572872 | tf_op jit(solution)/shard_map/ppermute | solution.py:54
  7.0 25.1 %collective-permute-start.6 = (bf16[512,512]{1,0:T(8,128)(2,1)}, bf16[512,512]{1,0:T(8,128)(2,1)}, u32[]{:S(2)}, u32[]{:S(2)}) collective-permute-start(bf16[512,512]{1,0:T(8,128)(2,1)} %get-tuple-element.31.refs_2_), channel_id=1, source_target_pairs={{0,2},{1,3},{2,0},{3,1},{4,6},{5,7},{6,4},{7,5},{8,10},{9,11},{10,... | collective-permute-start | bytes 1572872 | tf_op jit(solution)/shard_map/ppermute | solution.py:54
  8.5 3.7 %copy-start.8 = (s32[1,32]{1,0:T(1,128)S(1)}, s32[1,32]{1,0:T(1,128)}, u32[]{:S(2)}) copy-start(s32[1,32]{1,0:T(1,128)} %param.13) | copy-start | bytes 388
  8.5 4.6 %copy-start.7 = (s32[1,2]{1,0:T(1,128)S(1)}, s32[1,2]{1,0:T(1,128)}, u32[]{:S(2)}) copy-start(s32[1,2]{1,0:T(1,128)} %param.12) | copy-start | bytes 28
  11.4 39.5 %collective-permute-start = (bf16[256,4096]{1,0:T(8,128)(2,1)}, bf16[256,4096]{1,0:T(8,128)(2,1)S(1)}, u32[]{:S(2)}, u32[]{:S(2)}) collective-permute-start(bf16[256,4096]{1,0:T(8,128)(2,1)} %shard_map.86), channel_id=1, source_target_pairs={{0,1},{1,0},{2,3},{3,2},{4,5},{5,4},{6,7},{7,6},{8,9},{9,8},{10,11... | collective-permute-start | bytes 6291464 | tf_op jit(solution)/shard_map/ppermute | solution.py:59
  11.5 20.0 %collective-permute-start.2 = (bf16[512,512]{1,0:T(8,128)(2,1)}, bf16[512,512]{1,0:T(8,128)(2,1)}, u32[]{:S(2)}, u32[]{:S(2)}) collective-permute-start(bf16[512,512]{1,0:T(8,128)(2,1)} %get-tuple-element.31.refs_2_), channel_id=1, source_target_pairs={{8,0},{9,1},{10,2},{11,3},{0,4},{1,5},{2,6},{3,7},{12,8},{13,9},{1... | collective-permute-start | bytes 1572872 | tf_op jit(solution)/shard_map/ppermute | solution.py:54
  19.7 14.4 %collective-permute-start.4 = (bf16[512,512]{1,0:T(8,128)(2,1)}, bf16[512,512]{1,0:T(8,128)(2,1)S(1)}, u32[]{:S(2)}, u32[]{:S(2)}) collective-permute-start(bf16[512,512]{1,0:T(8,128)(2,1)} %collective-permute-done.1.refs_4_), channel_id=1, source_target_pairs={{0,2},{1,3},{2,0},{3,1},{4,6},{5,7},{6,4},{7,5},{8,10},{9,11},{10,... | collective-permute-start | bytes 1572872 | tf_op jit(solution)/shard_map/ppermute | solution.py:54
  21.2 13.1 %collective-permute-start.8 = (bf16[512,512]{1,0:T(8,128)(2,1)}, bf16[512,512]{1,0:T(8,128)(2,1)S(1)}, u32[]{:S(2)}, u32[]{:S(2)}) collective-permute-start(bf16[512,512]{1,0:T(8,128)(2,1)} %collective-permute-done.1.refs_4_), channel_id=1, source_target_pairs={{0,16},{16,0},{1,17},{17,1},{2,18},{18,2},{3,19},{19,3},{4,20},{20... | collective-permute-start | bytes 1572872 | tf_op jit(solution)/shard_map/ppermute | solution.py:54
  31.5 14.2 %collective-permute-start.3 = (bf16[512,512]{1,0:T(8,128)(2,1)}, bf16[512,512]{1,0:T(8,128)(2,1)}, u32[]{:S(2)}, u32[]{:S(2)}) collective-permute-start(bf16[512,512]{1,0:T(8,128)(2,1)} %collective-permute-done.1.refs_4_), channel_id=1, source_target_pairs={{0,8},{1,9},{2,10},{3,11},{4,0},{5,1},{6,2},{7,3},{8,12},{9,13},{1... | collective-permute-start | bytes 1572872 | tf_op jit(solution)/shard_map/ppermute | solution.py:54
  32.1 16.4 %collective-permute-start.7 = (bf16[512,512]{1,0:T(8,128)(2,1)}, bf16[512,512]{1,0:T(8,128)(2,1)}, u32[]{:S(2)}, u32[]{:S(2)}) collective-permute-start(bf16[512,512]{1,0:T(8,128)(2,1)} %collective-permute-done.2.refs_6_), channel_id=1, source_target_pairs={{0,2},{1,3},{2,0},{3,1},{4,6},{5,7},{6,4},{7,5},{8,10},{9,11},{10,... | collective-permute-start | bytes 1572872 | tf_op jit(solution)/shard_map/ppermute | solution.py:54
  34.1 14.5 %copy-start.4 = (bf16[512,512]{1,0:T(8,128)(2,1)}, bf16[512,512]{1,0:T(8,128)(2,1)S(1)}, u32[]{:S(2)}) copy-start(bf16[512,512]{1,0:T(8,128)(2,1)S(1)} %collective-permute-done.4.refs_5_) | copy-start | bytes 1572868
  34.3 14.2 %copy-start.5 = (bf16[512,512]{1,0:T(8,128)(2,1)}, bf16[512,512]{1,0:T(8,128)(2,1)S(1)}, u32[]{:S(2)}) copy-start(bf16[512,512]{1,0:T(8,128)(2,1)S(1)} %collective-permute-done.8.refs_10_) | copy-start | bytes 1572868
  34.3 14.2 %collective-permute-start.9 = (bf16[512,512]{1,0:T(8,128)(2,1)S(1)}, bf16[512,512]{1,0:T(8,128)(2,1)S(1)}, u32[]{:S(2)}, u32[]{:S(2)}) collective-permute-start(bf16[512,512]{1,0:T(8,128)(2,1)S(1)} %collective-permute-done.4.refs_5_), channel_id=1, source_target_pairs={{0,16},{16,0},{1,17},{17,1},{2,18},{18,2},{3,19},{19,3},{4,20},{20... | collective-permute-start | bytes 1572872 | tf_op jit(solution)/shard_map/ppermute | solution.py:54
  45.7 14.3 %collective-permute-start.11 = (bf16[512,512]{1,0:T(8,128)(2,1)}, bf16[512,512]{1,0:T(8,128)(2,1)}, u32[]{:S(2)}, u32[]{:S(2)}) collective-permute-start(bf16[512,512]{1,0:T(8,128)(2,1)} %get-tuple-element.46.refs_9_), channel_id=1, source_target_pairs={{8,0},{9,1},{10,2},{11,3},{0,4},{1,5},{2,6},{3,7},{12,8},{13,9},{1... | collective-permute-start | bytes 1572872 | tf_op jit(solution)/shard_map/ppermute | solution.py:54
  47.0 14.9 %collective-permute-start.5 = (bf16[512,512]{1,0:T(8,128)(2,1)}, bf16[512,512]{1,0:T(8,128)(2,1)}, u32[]{:S(2)}, u32[]{:S(2)}) collective-permute-start(bf16[512,512]{1,0:T(8,128)(2,1)} %collective-permute-done.3.refs_8_), channel_id=1, source_target_pairs={{0,2},{1,3},{2,0},{3,1},{4,6},{5,7},{6,4},{7,5},{8,10},{9,11},{10,... | collective-permute-start | bytes 1572872 | tf_op jit(solution)/shard_map/ppermute | solution.py:54
  49.4 12.6 %collective-permute-start.10 = (bf16[512,512]{1,0:T(8,128)(2,1)}, bf16[512,512]{1,0:T(8,128)(2,1)S(1)}, u32[]{:S(2)}, u32[]{:S(2)}) collective-permute-start(bf16[512,512]{1,0:T(8,128)(2,1)} %collective-permute-done.7.refs_7_), channel_id=1, source_target_pairs={{0,16},{16,0},{1,17},{17,1},{2,18},{18,2},{3,19},{19,3},{4,20},{20... | collective-permute-start | bytes 1572872 | tf_op jit(solution)/shard_map/ppermute | solution.py:54
  60.0 13.2 %collective-permute-start.12 = (bf16[512,512]{1,0:T(8,128)(2,1)}, bf16[512,512]{1,0:T(8,128)(2,1)S(1)}, u32[]{:S(2)}, u32[]{:S(2)}) collective-permute-start(bf16[512,512]{1,0:T(8,128)(2,1)} %collective-permute-done.11.refs_4_), channel_id=1, source_target_pairs={{8,0},{9,1},{10,2},{11,3},{0,4},{1,5},{2,6},{3,7},{12,8},{13,9},{1... | collective-permute-start | bytes 1572872 | tf_op jit(solution)/shard_map/ppermute | solution.py:54
  61.6 12.0 %collective-permute-start.13 = (bf16[512,512]{1,0:T(8,128)(2,1)}, bf16[512,512]{1,0:T(8,128)(2,1)S(1)}, u32[]{:S(2)}, u32[]{:S(2)}) collective-permute-start(bf16[512,512]{1,0:T(8,128)(2,1)} %get-tuple-element.46.refs_9_), channel_id=1, source_target_pairs={{0,2},{1,3},{2,0},{3,1},{4,6},{5,7},{6,4},{7,5},{8,10},{9,11},{10,... | collective-permute-start | bytes 1572872 | tf_op jit(solution)/shard_map/ppermute | solution.py:54
  62.0 11.9 %collective-permute-start.14 = (bf16[512,512]{1,0:T(8,128)(2,1)}, bf16[512,512]{1,0:T(8,128)(2,1)S(1)}, u32[]{:S(2)}, u32[]{:S(2)}) collective-permute-start(bf16[512,512]{1,0:T(8,128)(2,1)} %collective-permute-done.5.refs_2_), channel_id=1, source_target_pairs={{0,16},{16,0},{1,17},{17,1},{2,18},{18,2},{3,19},{19,3},{4,20},{20... | collective-permute-start | bytes 1572872 | tf_op jit(solution)/shard_map/ppermute | solution.py:54
  68.2 7.0 %collective-permute-start.16 = (f32[256,512]{1,0:T(8,128)S(1)}, f32[256,512]{1,0:T(8,128)S(1)}, u32[]{:S(2)}, u32[]{:S(2)}) collective-permute-start(f32[256,512]{1,0:T(8,128)S(1)} %get-tuple-element.53), channel_id=1, source_target_pairs={{0,1},{1,0},{2,3},{3,2},{4,5},{5,4},{6,7},{7,6},{8,9},{9,8},{10,11... | collective-permute-start | bytes 1572872 | tf_op jit(solution)/shard_map/ppermute | solution.py:59
  74.4 2.0 %collective-permute-start.15 = (f32[256,512]{1,0:T(8,128)S(1)}, f32[256,512]{1,0:T(8,128)S(1)}, u32[]{:S(2)}, u32[]{:S(2)}) collective-permute-start(f32[256,512]{1,0:T(8,128)S(1)} %shard_map.91), channel_id=1, source_target_pairs={{0,1},{1,0},{2,3},{3,2},{4,5},{5,4},{6,7},{7,6},{8,9},{9,8},{10,11... | collective-permute-start | bytes 1572872 | tf_op jit(solution)/shard_map/ppermute | solution.py:59
  75.1 6.5 %copy-start = (bf16[256,4096]{1,0:T(8,128)(2,1)S(1)}, bf16[256,4096]{1,0:T(8,128)(2,1)}, u32[]{:S(2)}) copy-start(bf16[256,4096]{1,0:T(8,128)(2,1)} %query_ref.3) | copy-start | bytes 6291460
  75.1 6.5 %copy-start.1 = (f32[256,256]{1,0:T(8,128)S(1)}, f32[256,256]{1,0:T(8,128)}, u32[]{:S(2)}) copy-start(f32[256,256]{1,0:T(8,128)} %concatenate.3.refs_9_.table_ref) | copy-start | bytes 786436
  77.4 14.2 %all-to-all-start = ((bf16[16,8,1024]{2,1,0:T(8,128)(2,1)}), bf16[16,8,1024]{2,1,0:T(8,128)(2,1)S(1)}, u32[]{:S(2)}, u32[]{:S(2)}) async-start(bf16[16,8,1024]{2,1,0:T(8,128)(2,1)} %bitcast.21), calls=%async_computation | async-start | bytes 524288 | tf_op jit(solution)/shard_map/all_to_all | solution.py:589
  (3 other events, 3.4 us)

commit v6 on v5

--- a/solution.py
+++ b/solution.py
@@ -59,39 +59,33 @@
     return lax.ppermute(value, "dp", [(i, i ^ 1) for i in range(replicas)])
 
 
-def halves(weight, half):
+def head_pair(weight, half, flip):
     depth, width = weight.shape
     quarter = width // 4
 
-    def kernel(half_ref, weight_ref, mine_ref, other_ref, sems):
-        copies = []
-        for i, out in enumerate((mine_ref, other_ref)):
-            which = half_ref[0] if i == 0 else 1 - half_ref[0]
-            for j in range(2):
-                start = pl.multiple_of((2 * j + which) * quarter, HEAD)
-                copies.append(
-                    pltpu.make_async_copy(
-                        weight_ref.at[:, pl.ds(start, quarter)],
-                        out.at[:, pl.ds(j * quarter, quarter)],
-                        sems.at[2 * i + j],
-                    )
-                )
+    def kernel(half_ref, weight_ref, out_ref, sems):
+        which = 1 - half_ref[0] if flip else half_ref[0]
+        copies = [
+            pltpu.make_async_copy(
+                weight_ref.at[:, pl.ds(pl.multiple_of((2 * j + which) * quarter, HEAD), quarter)],
+                out_ref.at[:, pl.ds(j * quarter, quarter)],
+                sems.at[j],
+            )
+            for j in range(2)
+        ]
         for copy in copies:
             copy.start()
         for copy in copies:
             copy.wait()
 
-    anywhere = pl.BlockSpec(memory_space=pl.ANY)
-    inside = pl.BlockSpec(memory_space=pltpu.VMEM)
-    out = jax.ShapeDtypeStruct((depth, width // 2), weight.dtype)
     return pl.pallas_call(
         kernel,
-        out_shape=(out, out),
-        in_specs=[pl.BlockSpec(memory_space=pltpu.SMEM), anywhere],
-        out_specs=(inside, inside),
-        scratch_shapes=[pltpu.SemaphoreType.DMA((4,))],
+        out_shape=jax.ShapeDtypeStruct((depth, width // 2), weight.dtype),
+        in_specs=[pl.BlockSpec(memory_space=pltpu.SMEM), pl.BlockSpec(memory_space=pl.ANY)],
+        out_specs=pl.BlockSpec(memory_space=pltpu.VMEM),
+        scratch_shapes=[pltpu.SemaphoreType.DMA((2,))],
         cost_estimate=pl.CostEstimate(
-            flops=0, bytes_accessed=4 * depth * width, transcendentals=0
+            flops=0, bytes_accessed=2 * depth * width, transcendentals=0
         ),
     )(half, weight)
 
@@ -417,26 +411,26 @@
     def kernel(scalar_ref, table_ref, mine_ref, other_ref, spans_ref, out_ref, total_ref, sems):
         present = spans_ref[:, :HEAD].astype(jnp.float32)
         present = jnp.where(present > 0.5 * ABSENT, 0.0, 1.0)
-        row = lax.broadcasted_iota(jnp.int32, (slots, slots), 0)
-        column = lax.broadcasted_iota(jnp.int32, (slots, slots), 1)
-        before = (column // SPAN < row // SPAN) & (column % SPAN == 0)
-        before = jnp.where(before, 1.0, 0.0).astype(jnp.bfloat16)
-        earlier = jnp.dot(before, present.astype(jnp.bfloat16), preferred_element_type=jnp.float32)
-        rank = earlier[:, :1].astype(jnp.int32) + scalar_ref[1]
-        target = lax.broadcasted_iota(jnp.int32, (slots, rows), 1)
-        sender = lax.broadcasted_iota(jnp.int32, (slots, rows), 0)
+        row = lax.broadcasted_iota(jnp.int32, (slots, 2 * slots), 0)
+        column = lax.broadcasted_iota(jnp.int32, (slots, 2 * slots), 1)
+        before = (row // SPAN < column // SPAN) & (row % SPAN == 0)
+        counts = ((column < slots) & before) | (row == column - slots)
+        counts = lax.dot_general(
+            present.astype(jnp.bfloat16),
+            jnp.where(counts, 1.0, 0.0).astype(jnp.bfloat16),
+            (((0,), (0,)), ((), ())),
+            preferred_element_type=jnp.float32,
+        )
+        rank = counts[:1, :slots].astype(jnp.int32) + scalar_ref[1]
+        target = lax.broadcasted_iota(jnp.int32, (rows, slots), 0)
+        sender = lax.broadcasted_iota(jnp.int32, (rows, slots), 1)
         hit = (target // SPAN == rank) & (target % SPAN == sender % SPAN)
-        hit = jnp.where(hit & (present[:, :1] > 0.5), 1.0, 0.0).astype(jnp.bfloat16)
+        hit = jnp.where(hit & (counts[:1, slots:] > 0.5), 1.0, 0.0).astype(jnp.bfloat16)
         keep = table_ref[:, KEEP : KEEP + 1] > 0.5
         copies = []
         for i in range(4):
             lanes = slice(i * part, (i + 1) * part)
-            came = lax.dot_general(
-                hit,
-                spans_ref[:, lanes],
-                (((0,), (0,)), ((), ())),
-                preferred_element_type=jnp.float32,
-            )
+            came = jnp.dot(hit, spans_ref[:, lanes], preferred_element_type=jnp.float32)
             home = (mine_ref, other_ref)[i // 2][:, (i % 2) * part : (i % 2 + 1) * part]
             total_ref[i] = jnp.where(keep, home.astype(jnp.float32), came).astype(jnp.bfloat16)
             which = scalar_ref[0] if i < 2 else 1 - scalar_ref[0]
@@ -518,7 +512,8 @@
     plan = (table, mask, scalars)
 
     links = Links(replicas, lax.axis_size("group"))
-    mine_weight, other_weight = halves(kv_weight, half)
+    mine_weight = head_pair(kv_weight, half, False)
+    other_weight = head_pair(kv_weight, half, True)
     peer_columns = core_columns(states, 1 - core, depth)
     peer_states = core_swap(peer_columns, replicas)
 
@@ -560,7 +555,7 @@
                 middle.append((moving, block(-j, False)))
             moving = links.send(moving, "back", sums)
             late.append((moving, block(fore - ring, False)))
-            late.append((links.send(other_weight, "y", sums), block(0, True)))
+            late.append((links.send(other_weight, "y"), block(0, True)))
             late.append((links.send(crossed, "x", sums), block(k, True)))
             middle = [(crossed, block(k, True))] + middle
             mine_peer, mine_own, other_peer, other_own, left_peer, left_own, pick = accumulate(

time: 93.8 us -> 92.7 us (0.988)
  local copies, waits for them, and re-layouts: 3.97 us -> 1.97 us
  Pallas kernels: 28.4 us -> 29.9 us
    unnamed x18 -> x28, local copies, waits for them, and re-layouts: 2.14 us -> 0.06 us
    pallas_call x1 -> x2, Pallas kernels: 2.23 us -> 3.7 us  [head_pair(): pl.pallas_call(kernel, out_shape=jax.ShapeDtypeStruct((depth, width // 2)...]
    ppermute x14, starting transfers between devices: 19.8 us -> 18.9 us  [send(): sent.append(lax.ppermute(after(value, *before), axis, pairs))]
  transfers between devices with their start and end apart: 18 -> 18, of which waited for: 11 -> 10; matrix products, arithmetic and copies ran while one was open for 7% -> 7% of each run, Pallas kernels for 25% -> 28%
where the time goes in v6:
time: 92.7 us; the launch traced here: 92.3 us
  Pallas kernels  29.9 us (32%)
  waiting for transfers between devices  26.1 us (28%)
  starting transfers between devices  23.9 us (26%)
  between operations  5.56 us (6%)
  other arithmetic  4.87 us (5%)
  local copies, waits for them, and re-layouts  1.97 us (2%)
    ppermute x14, waiting for transfers between devices, send(): sent.append(lax.ppermute(after(value, *before), axis, pairs))  22 us
    ppermute x14, starting transfers between devices, send(): sent.append(lax.ppermute(after(value, *before), axis, pairs))  18.9 us
    pallas_call x2, Pallas kernels, accumulate(): pl.pallas_call(kernel, out_shape=out_shape, in_specs=[pl.BlockSpec(memory...  12.2 us
    pallas_call x2, Pallas kernels, attend(): pl.pallas_call(kernel, out_shape=jax.ShapeDtypeStruct(queries.shape, jnp....  6.91 us
    all_to_all x1, starting transfers between devices, per_device(): spans = lax.all_to_all(spans, 'dp', split_axis=0, concat_axis=0, tiled=True)  4.82 us
    pallas_call x2, Pallas kernels, head_pair(): pl.pallas_call(kernel, out_shape=jax.ShapeDtypeStruct((depth, width // 2)...  3.7 us
    all_to_all x1, waiting for transfers between devices, per_device(): spans = lax.all_to_all(spans, 'dp', split_axis=0, concat_axis=0, tiled=True)  3.12 us
    pallas_call x1, Pallas kernels, core_columns(): pl.pallas_call(kernel, out_shape=jax.ShapeDtypeStruct((tokens, width // 2...  2.96 us
  transfers between devices with their start and end apart: 18, of which 10 were waited for; matrix products, arithmetic and copies ran while one was open for 7% of the time, Pallas kernels for 28%

profile of v6, /device:TPU:0, one launch (start us, length us, event | category | flops | bytes accessed | tf_op | source)
XLA Modules:
  0.0 92.3 jit_solution(5805510994173376498)
XLA Ops:
  0.6 1.8 %shard_map.87.refs_2_ = bf16[512,512]{1,0:T(8,128)(2,1)} custom-call(s32[1]{0:T(128)} %bitcast.half_ref, bf16[512,1024]{1,0:T(8,128)(2,1)} %weight_ref.3), custom_call_target="tpu_custom_call" | custom-call | bytes 1048576 | tf_op jit(solution)/shard_map/pallas_call | solution.py:81
  2.5 4.1 %collective-permute-start.1 = (bf16[512,512]{1,0:T(8,128)(2,1)}, bf16[512,512]{1,0:T(8,128)(2,1)S(1)}, u32[]{:S(2)}, u32[]{:S(2)}) collective-permute-start(bf16[512,512]{1,0:T(8,128)(2,1)} %shard_map.87.refs_2_), channel_id=1, source_target_pairs={{0,8},{1,9},{2,10},{3,11},{4,0},{5,1},{6,2},{7,3},{8,12},{9,13},{1... | collective-permute-start | bytes 1572872 | tf_op jit(solution)/shard_map/ppermute | solution.py:54
  6.6 1.5 %collective-permute-start.6 = (bf16[512,512]{1,0:T(8,128)(2,1)}, bf16[512,512]{1,0:T(8,128)(2,1)S(1)}, u32[]{:S(2)}, u32[]{:S(2)}) collective-permute-start(bf16[512,512]{1,0:T(8,128)(2,1)} %shard_map.87.refs_2_), channel_id=1, source_target_pairs={{0,2},{1,3},{2,0},{3,1},{4,6},{5,7},{6,4},{7,5},{8,10},{9,11},{10,... | collective-permute-start | bytes 1572872 | tf_op jit(solution)/shard_map/ppermute | solution.py:54
  8.1 3.0 %shard_map.86 = bf16[256,4096]{1,0:T(8,128)(2,1)} custom-call(s32[1]{0:T(128)S(6)} %sub.93.core_ref, bf16[256,8192]{1,0:T(8,128)(2,1)} %refs_1_.3), custom_call_target="tpu_custom_call" | custom-call | bytes 4194304 | tf_op jit(solution)/shard_map/pallas_call | solution.py:114
  20.8 1.5 %collective-permute-start.8 = (bf16[512,512]{1,0:T(8,128)(2,1)S(1)}, bf16[512,512]{1,0:T(8,128)(2,1)S(1)}, u32[]{:S(2)}, u32[]{:S(2)}) collective-permute-start(bf16[512,512]{1,0:T(8,128)(2,1)S(1)} %collective-permute-done.1.refs_4_), channel_id=1, source_target_pairs={{0,16},{16,0},{1,17},{17,1},{2,18},{18,2},{3,19},{19,3},{4,20},{20... | collective-permute-start | bytes 1572872 | tf_op jit(solution)/shard_map/ppermute | solution.py:54
  25.2 5.8 %collective-permute-done.2.refs_6_ = bf16[512,512]{1,0:T(8,128)(2,1)S(1)} collective-permute-done((bf16[512,512]{1,0:T(8,128)(2,1)S(1)}, bf16[512,512]{1,0:T(8,128)(2,1)S(1)}, u32[]{:S(2)}, u32[]{:S(2)}) %collective-permute-start.2) | collective-permute-done | bytes 524320 | tf_op jit(solution)/shard_map/ppermute | solution.py:54
  31.6 1.5 %collective-permute-start.7 = (bf16[512,512]{1,0:T(8,128)(2,1)S(1)}, bf16[512,512]{1,0:T(8,128)(2,1)}, u32[]{:S(2)}, u32[]{:S(2)}) collective-permute-start(bf16[512,512]{1,0:T(8,128)(2,1)S(1)} %collective-permute-done.2.refs_6_), channel_id=1, source_target_pairs={{0,2},{1,3},{2,0},{3,1},{4,6},{5,7},{6,4},{7,5},{8,10},{9,11},{10,... | collective-permute-start | bytes 1572872 | tf_op jit(solution)/shard_map/ppermute | solution.py:54
  34.1 1.5 %collective-permute-start.9 = (bf16[512,512]{1,0:T(8,128)(2,1)S(1)}, bf16[512,512]{1,0:T(8,128)(2,1)S(1)}, u32[]{:S(2)}, u32[]{:S(2)}) collective-permute-start(bf16[512,512]{1,0:T(8,128)(2,1)S(1)} %collective-permute-done.4.refs_5_), channel_id=1, source_target_pairs={{0,16},{16,0},{1,17},{17,1},{2,18},{18,2},{3,19},{19,3},{4,20},{20... | collective-permute-start | bytes 1572872 | tf_op jit(solution)/shard_map/ppermute | solution.py:54
  35.6 1.9 %shard_map.88.refs_9_ = bf16[512,512]{1,0:T(8,128)(2,1)} custom-call(s32[1]{0:T(128)} %bitcast.half_ref, bf16[512,1024]{1,0:T(8,128)(2,1)} %weight_ref.3), custom_call_target="tpu_custom_call" | custom-call | bytes 1048576 | tf_op jit(solution)/shard_map/pallas_call | solution.py:81
  37.5 7.5 %collective-permute-done.3.refs_8_ = bf16[512,512]{1,0:T(8,128)(2,1)} collective-permute-done((bf16[512,512]{1,0:T(8,128)(2,1)S(1)}, bf16[512,512]{1,0:T(8,128)(2,1)}, u32[]{:S(2)}, u32[]{:S(2)}) %collective-permute-start.3) | collective-permute-done | bytes 524320 | tf_op jit(solution)/shard_map/ppermute | solution.py:54
  46.3 1.5 %collective-permute-start.5 = (bf16[512,512]{1,0:T(8,128)(2,1)}, bf16[512,512]{1,0:T(8,128)(2,1)S(1)}, u32[]{:S(2)}, u32[]{:S(2)}) collective-permute-start(bf16[512,512]{1,0:T(8,128)(2,1)} %collective-permute-done.3.refs_8_), channel_id=1, source_target_pairs={{0,2},{1,3},{2,0},{3,1},{4,6},{5,7},{6,4},{7,5},{8,10},{9,11},{10,... | collective-permute-start | bytes 1572872 | tf_op jit(solution)/shard_map/ppermute | solution.py:54
  47.9 1.6 %collective-permute-start.10 = (bf16[512,512]{1,0:T(8,128)(2,1)}, bf16[512,512]{1,0:T(8,128)(2,1)S(1)}, u32[]{:S(2)}, u32[]{:S(2)}) collective-permute-start(bf16[512,512]{1,0:T(8,128)(2,1)} %collective-permute-done.7.refs_7_), channel_id=1, source_target_pairs={{0,16},{16,0},{1,17},{17,1},{2,18},{18,2},{3,19},{19,3},{4,20},{20... | collective-permute-start | bytes 1572872 | tf_op jit(solution)/shard_map/ppermute | solution.py:54
  50.5 7.3 %shard_map.89 = (f32[256,512]{1,0:T(8,128)}, f32[256,512]{1,0:T(8,128)}, f32[256,512]{1,0:T(8,128)}, f32[256,512]{1,0:T(8,128)}) custom-call(s32[12]{0:T(128)S(1)} %stack.58.scalar_ref, bf16[256,4096]{1,0:T(8,128)(2,1)} %collective-permute-done.refs_0_, bf16[256,8192]{1,0:T(8,128)(2,1)} %refs_1_.3, bf16[512,512]{1,0:T(8,128)(2,1)} %shard_map.87.refs_2_, ...), custom_call_target="tpu_custom_call" | custom-call | flops 2684354560 | bytes 10485760 | tf_op jit(solution)/shard_map/pallas_call | solution.py:229
  57.8 1.4 %collective-permute-done.11.refs_4_ = bf16[512,512]{1,0:T(8,128)(2,1)S(1)} collective-permute-done((bf16[512,512]{1,0:T(8,128)(2,1)}, bf16[512,512]{1,0:T(8,128)(2,1)S(1)}, u32[]{:S(2)}, u32[]{:S(2)}) %collective-permute-start.11) | collective-permute-done | bytes 524320 | tf_op jit(solution)/shard_map/ppermute | solution.py:54
  59.2 2.2 %collective-permute-done.5.refs_2_ = bf16[512,512]{1,0:T(8,128)(2,1)S(1)} collective-permute-done((bf16[512,512]{1,0:T(8,128)(2,1)}, bf16[512,512]{1,0:T(8,128)(2,1)S(1)}, u32[]{:S(2)}, u32[]{:S(2)}) %collective-permute-start.5) | collective-permute-done | bytes 524320 | tf_op jit(solution)/shard_map/ppermute | solution.py:54
  61.4 1.6 %collective-permute-start.14 = (bf16[512,512]{1,0:T(8,128)(2,1)S(1)}, bf16[512,512]{1,0:T(8,128)(2,1)S(1)}, u32[]{:S(2)}, u32[]{:S(2)}) collective-permute-start(bf16[512,512]{1,0:T(8,128)(2,1)S(1)} %collective-permute-done.5.refs_2_), channel_id=1, source_target_pairs={{0,16},{16,0},{1,17},{17,1},{2,18},{18,2},{3,19},{19,3},{4,20},{20... | collective-permute-start | bytes 1572872 | tf_op jit(solution)/shard_map/ppermute | solution.py:54
  63.0 4.9 %shard_map.90 = (f32[256,512]{1,0:T(8,128)S(1)}, f32[256,512]{1,0:T(8,128)S(1)}, f32[256,512]{1,0:T(8,128)S(1)}, f32[256,512]{1,0:T(8,128)S(1)}, bf16[256,1536]{...) custom-call(s32[8]{0:T(128)S(1)} %stack.51.scalar_ref, ...), custom_call_target="tpu_custom_call" | custom-call | flops 805306368 | bytes 3145728 | tf_op jit(solution)/shard_map/pallas_call | solution.py:229
  68.0 2.1 %collective-permute-done.13.refs_1_ = bf16[512,512]{1,0:T(8,128)(2,1)S(1)} collective-permute-done((bf16[512,512]{1,0:T(8,128)(2,1)}, bf16[512,512]{1,0:T(8,128)(2,1)S(1)}, u32[]{:S(2)}, u32[]{:S(2)}) %collective-permute-start.13) | collective-permute-done | bytes 524320 | tf_op jit(solution)/shard_map/ppermute | solution.py:54
  70.2 2.0 %collective-permute-done.12.refs_0_ = bf16[512,512]{1,0:T(8,128)(2,1)S(1)} collective-permute-done((bf16[512,512]{1,0:T(8,128)(2,1)S(1)}, bf16[512,512]{1,0:T(8,128)(2,1)S(1)}, u32[]{:S(2)}, u32[]{:S(2)}) %collective-permute-start.12) | collective-permute-done | bytes 524320 | tf_op jit(solution)/shard_map/ppermute | solution.py:54
  75.8 4.8 %all-to-all-start = ((bf16[16,8,1024]{2,1,0:T(8,128)(2,1)}), bf16[16,8,1024]{2,1,0:T(8,128)(2,1)S(1)}, u32[]{:S(2)}, u32[]{:S(2)}) async-start(bf16[16,8,1024]{2,1,0:T(8,128)(2,1)} %bitcast.21), calls=%async_computation | async-start | bytes 524288 | tf_op jit(solution)/shard_map/all_to_all | solution.py:584
  80.6 3.5 %shard_map.95.refs_0_ = bf16[256,4096]{1,0:T(8,128)(2,1)} custom-call(s32[1]{0:T(128)} %bitcast.half_ref, f32[256,256]{1,0:T(8,128)S(1)} %fusion.3.mask_ref, f32[256,256]{1,0:T(8,128)S(1)} %copy-done.1, bf16[256,4096]{1,0:T(8,128)(2,1)S(1)} %copy-done, bf16[256,512]{1,0:T(8,128)(2,1)S(1)} %get-tuple-element.52.key_ref.value_ref.mine_ref, ...), custom_call_target="tpu_custom_call" | custom-call | flops 536870912 | bytes 2097152 | tf_op jit(solution)/shard_map/pallas_call | solution.py:387
  84.1 3.4 %shard_map.96 = bf16[256,4096]{1,0:T(8,128)(2,1)} custom-call(s32[1]{0:T(128)} %bitcast.half_ref, f32[256,256]{1,0:T(8,128)S(1)} %fusion.3.mask_ref, f32[256,256]{1,0:T(8,128)S(1)} %copy-done.1, bf16[256,4096]{1,0:T(8,128)(2,1)S(1)} %copy-done, bf16[256,512]{1,0:T(8,128)(2,1)S(1)} %get-tuple-element.51.key_ref.value_ref.other_ref, ...), custom_call_target="tpu_custom_call", output_to_operand_aliasing={{}: (6, {})} | custom-call | flops 536870912 | bytes 2097152 | tf_op jit(solution)/shard_map/pallas_call | solution.py:387
  87.5 3.1 %all-to-all-done = bf16[16,8,1024]{2,1,0:T(8,128)(2,1)S(1)} async-done(((bf16[16,8,1024]{2,1,0:T(8,128)(2,1)}), bf16[16,8,1024]{2,1,0:T(8,128)(2,1)S(1)}, u32[]{:S(2)}, u32[]{:S(2)}) %all-to-all-start) | async-done | bytes 262176 | tf_op jit(solution)/shard_map/all_to_all | solution.py:584
  90.6 1.7 %shard_map.97 = bf16[192,1024]{1,0:T(8,128)(2,1)} custom-call(s32[2]{0:T(128)S(1)} %pad_add_fusion.scalar_ref, f32[256,256]{1,0:T(8,128)S(1)} %copy-done.1, bf16[256,512]{1,0:T(8,128)(2,1)S(1)} %get-tuple-element.52.key_ref.value_ref.mine_ref, bf16[256,512]{1,0:T(8,128)(2,1)S(1)} %get-tuple-element.51.key_ref.value_ref.other_ref, bf16[128,1024]{1,0:T(8,128)(2,1)S(1)} %bitcast.20), custom_call_target="tpu_custom_call" | custom-call | flops 50331648 | bytes 786432 | tf_op jit(solution)/shard_map/pallas_call | solution.py:446
  (70 shorter events, 15.5 us)
Async XLA Ops:
  2.5 17.1 %collective-permute-start.1 = (bf16[512,512]{1,0:T(8,128)(2,1)}, bf16[512,512]{1,0:T(8,128)(2,1)S(1)}, u32[]{:S(2)}, u32[]{:S(2)}) collective-permute-start(bf16[512,512]{1,0:T(8,128)(2,1)} %shard_map.87.refs_2_), channel_id=1, source_target_pairs={{0,8},{1,9},{2,10},{3,11},{4,0},{5,1},{6,2},{7,3},{8,12},{9,13},{1... | collective-permute-start | bytes 1572872 | tf_op jit(solution)/shard_map/ppermute | solution.py:54
  6.6 25.0 %collective-permute-start.6 = (bf16[512,512]{1,0:T(8,128)(2,1)}, bf16[512,512]{1,0:T(8,128)(2,1)S(1)}, u32[]{:S(2)}, u32[]{:S(2)}) collective-permute-start(bf16[512,512]{1,0:T(8,128)(2,1)} %shard_map.87.refs_2_), channel_id=1, source_target_pairs={{0,2},{1,3},{2,0},{3,1},{4,6},{5,7},{6,4},{7,5},{8,10},{9,11},{10,... | collective-permute-start | bytes 1572872 | tf_op jit(solution)/shard_map/ppermute | solution.py:54
  11.1 39.4 %collective-permute-start = (bf16[256,4096]{1,0:T(8,128)(2,1)}, bf16[256,4096]{1,0:T(8,128)(2,1)}, u32[]{:S(2)}, u32[]{:S(2)}) collective-permute-start(bf16[256,4096]{1,0:T(8,128)(2,1)} %shard_map.86), channel_id=1, source_target_pairs={{0,1},{1,0},{2,3},{3,2},{4,5},{5,4},{6,7},{7,6},{8,9},{9,8},{10,11... | collective-permute-start | bytes 6291464 | tf_op jit(solution)/shard_map/ppermute | solution.py:59
  11.2 19.8 %collective-permute-start.2 = (bf16[512,512]{1,0:T(8,128)(2,1)S(1)}, bf16[512,512]{1,0:T(8,128)(2,1)S(1)}, u32[]{:S(2)}, u32[]{:S(2)}) collective-permute-start(bf16[512,512]{1,0:T(8,128)(2,1)S(1)} %copy-done.2), channel_id=1, source_target_pairs={{8,0},{9,1},{10,2},{11,3},{0,4},{1,5},{2,6},{3,7},{12,8},{13,9},{1... | collective-permute-start | bytes 1572872 | tf_op jit(solution)/shard_map/ppermute | solution.py:54
  19.6 30.8 %copy-start.6 = (bf16[512,512]{1,0:T(8,128)(2,1)}, bf16[512,512]{1,0:T(8,128)(2,1)S(1)}, u32[]{:S(2)}) copy-start(bf16[512,512]{1,0:T(8,128)(2,1)S(1)} %collective-permute-done.1.refs_4_) | copy-start | bytes 1572868
  19.6 14.3 %collective-permute-start.4 = (bf16[512,512]{1,0:T(8,128)(2,1)S(1)}, bf16[512,512]{1,0:T(8,128)(2,1)S(1)}, u32[]{:S(2)}, u32[]{:S(2)}) collective-permute-start(bf16[512,512]{1,0:T(8,128)(2,1)S(1)} %collective-permute-done.1.refs_4_), channel_id=1, source_target_pairs={{0,2},{1,3},{2,0},{3,1},{4,6},{5,7},{6,4},{7,5},{8,10},{9,11},{10,... | collective-permute-start | bytes 1572872 | tf_op jit(solution)/shard_map/ppermute | solution.py:54
  20.8 13.3 %collective-permute-start.8 = (bf16[512,512]{1,0:T(8,128)(2,1)S(1)}, bf16[512,512]{1,0:T(8,128)(2,1)S(1)}, u32[]{:S(2)}, u32[]{:S(2)}) collective-permute-start(bf16[512,512]{1,0:T(8,128)(2,1)S(1)} %collective-permute-done.1.refs_4_), channel_id=1, source_target_pairs={{0,16},{16,0},{1,17},{17,1},{2,18},{18,2},{3,19},{19,3},{4,20},{20... | collective-permute-start | bytes 1572872 | tf_op jit(solution)/shard_map/ppermute | solution.py:54
  31.0 16.8 %copy-start.8 = (bf16[512,512]{1,0:T(8,128)(2,1)}, bf16[512,512]{1,0:T(8,128)(2,1)S(1)}, u32[]{:S(2)}) copy-start(bf16[512,512]{1,0:T(8,128)(2,1)S(1)} %collective-permute-done.2.refs_6_) | copy-start | bytes 1572868
  31.0 14.0 %collective-permute-start.3 = (bf16[512,512]{1,0:T(8,128)(2,1)S(1)}, bf16[512,512]{1,0:T(8,128)(2,1)}, u32[]{:S(2)}, u32[]{:S(2)}) collective-permute-start(bf16[512,512]{1,0:T(8,128)(2,1)S(1)} %collective-permute-done.1.refs_4_), channel_id=1, source_target_pairs={{0,8},{1,9},{2,10},{3,11},{4,0},{5,1},{6,2},{7,3},{8,12},{9,13},{1... | collective-permute-start | bytes 1572872 | tf_op jit(solution)/shard_map/ppermute | solution.py:54
  31.6 16.2 %collective-permute-start.7 = (bf16[512,512]{1,0:T(8,128)(2,1)S(1)}, bf16[512,512]{1,0:T(8,128)(2,1)}, u32[]{:S(2)}, u32[]{:S(2)}) collective-permute-start(bf16[512,512]{1,0:T(8,128)(2,1)S(1)} %collective-permute-done.2.refs_6_), channel_id=1, source_target_pairs={{0,2},{1,3},{2,0},{3,1},{4,6},{5,7},{6,4},{7,5},{8,10},{9,11},{10,... | collective-permute-start | bytes 1572872 | tf_op jit(solution)/shard_map/ppermute | solution.py:54
  33.9 15.5 %copy-start.9 = (bf16[512,512]{1,0:T(8,128)(2,1)}, bf16[512,512]{1,0:T(8,128)(2,1)S(1)}, u32[]{:S(2)}) copy-start(bf16[512,512]{1,0:T(8,128)(2,1)S(1)} %collective-permute-done.4.refs_5_) | copy-start | bytes 1572868
  34.1 10.9 %copy-start.10 = (bf16[512,512]{1,0:T(8,128)(2,1)}, bf16[512,512]{1,0:T(8,128)(2,1)S(1)}, u32[]{:S(2)}) copy-start(bf16[512,512]{1,0:T(8,128)(2,1)S(1)} %collective-permute-done.8.refs_10_) | copy-start | bytes 1572868
  34.1 13.7 %collective-permute-start.9 = (bf16[512,512]{1,0:T(8,128)(2,1)S(1)}, bf16[512,512]{1,0:T(8,128)(2,1)S(1)}, u32[]{:S(2)}, u32[]{:S(2)}) collective-permute-start(bf16[512,512]{1,0:T(8,128)(2,1)S(1)} %collective-permute-done.4.refs_5_), channel_id=1, source_target_pairs={{0,16},{16,0},{1,17},{17,1},{2,18},{18,2},{3,19},{19,3},{4,20},{20... | collective-permute-start | bytes 1572872 | tf_op jit(solution)/shard_map/ppermute | solution.py:54
  45.0 14.2 %collective-permute-start.11 = (bf16[512,512]{1,0:T(8,128)(2,1)}, bf16[512,512]{1,0:T(8,128)(2,1)S(1)}, u32[]{:S(2)}, u32[]{:S(2)}) collective-permute-start(bf16[512,512]{1,0:T(8,128)(2,1)} %shard_map.88.refs_9_), channel_id=1, source_target_pairs={{8,0},{9,1},{10,2},{11,3},{0,4},{1,5},{2,6},{3,7},{12,8},{13,9},{1... | collective-permute-start | bytes 1572872 | tf_op jit(solution)/shard_map/ppermute | solution.py:54
  46.3 15.1 %collective-permute-start.5 = (bf16[512,512]{1,0:T(8,128)(2,1)}, bf16[512,512]{1,0:T(8,128)(2,1)S(1)}, u32[]{:S(2)}, u32[]{:S(2)}) collective-permute-start(bf16[512,512]{1,0:T(8,128)(2,1)} %collective-permute-done.3.refs_8_), channel_id=1, source_target_pairs={{0,2},{1,3},{2,0},{3,1},{4,6},{5,7},{6,4},{7,5},{8,10},{9,11},{10,... | collective-permute-start | bytes 1572872 | tf_op jit(solution)/shard_map/ppermute | solution.py:54
  47.9 13.5 %collective-permute-start.10 = (bf16[512,512]{1,0:T(8,128)(2,1)}, bf16[512,512]{1,0:T(8,128)(2,1)S(1)}, u32[]{:S(2)}, u32[]{:S(2)}) collective-permute-start(bf16[512,512]{1,0:T(8,128)(2,1)} %collective-permute-done.7.refs_7_), channel_id=1, source_target_pairs={{0,16},{16,0},{1,17},{17,1},{2,18},{18,2},{3,19},{19,3},{4,20},{20... | collective-permute-start | bytes 1572872 | tf_op jit(solution)/shard_map/ppermute | solution.py:54
  49.5 20.7 %collective-permute-start.13 = (bf16[512,512]{1,0:T(8,128)(2,1)}, bf16[512,512]{1,0:T(8,128)(2,1)S(1)}, u32[]{:S(2)}, u32[]{:S(2)}) collective-permute-start(bf16[512,512]{1,0:T(8,128)(2,1)} %shard_map.88.refs_9_), channel_id=1, source_target_pairs={{0,2},{1,3},{2,0},{3,1},{4,6},{5,7},{6,4},{7,5},{8,10},{9,11},{10,... | collective-permute-start | bytes 1572872 | tf_op jit(solution)/shard_map/ppermute | solution.py:54
  59.2 13.0 %collective-permute-start.12 = (bf16[512,512]{1,0:T(8,128)(2,1)S(1)}, bf16[512,512]{1,0:T(8,128)(2,1)S(1)}, u32[]{:S(2)}, u32[]{:S(2)}) collective-permute-start(bf16[512,512]{1,0:T(8,128)(2,1)S(1)} %collective-permute-done.11.refs_4_), channel_id=1, source_target_pairs={{8,0},{9,1},{10,2},{11,3},{0,4},{1,5},{2,6},{3,7},{12,8},{13,9},{1... | collective-permute-start | bytes 1572872 | tf_op jit(solution)/shard_map/ppermute | solution.py:54
  61.4 10.8 %collective-permute-start.14 = (bf16[512,512]{1,0:T(8,128)(2,1)S(1)}, bf16[512,512]{1,0:T(8,128)(2,1)S(1)}, u32[]{:S(2)}, u32[]{:S(2)}) collective-permute-start(bf16[512,512]{1,0:T(8,128)(2,1)S(1)} %collective-permute-done.5.refs_2_), channel_id=1, source_target_pairs={{0,16},{16,0},{1,17},{17,1},{2,18},{18,2},{3,19},{19,3},{4,20},{20... | collective-permute-start | bytes 1572872 | tf_op jit(solution)/shard_map/ppermute | solution.py:54
  67.9 5.5 %collective-permute-start.16 = (f32[256,512]{1,0:T(8,128)S(1)}, f32[256,512]{1,0:T(8,128)S(1)}, u32[]{:S(2)}, u32[]{:S(2)}) collective-permute-start(f32[256,512]{1,0:T(8,128)S(1)} %get-tuple-element.49), channel_id=1, source_target_pairs={{0,1},{1,0},{2,3},{3,2},{4,5},{5,4},{6,7},{7,6},{8,9},{9,8},{10,11... | collective-permute-start | bytes 1572872 | tf_op jit(solution)/shard_map/ppermute | solution.py:59
  72.8 2.0 %collective-permute-start.15 = (f32[256,512]{1,0:T(8,128)S(1)}, f32[256,512]{1,0:T(8,128)S(1)}, u32[]{:S(2)}, u32[]{:S(2)}) collective-permute-start(f32[256,512]{1,0:T(8,128)S(1)} %shard_map.92), channel_id=1, source_target_pairs={{0,1},{1,0},{2,3},{3,2},{4,5},{5,4},{6,7},{7,6},{8,9},{9,8},{10,11... | collective-permute-start | bytes 1572872 | tf_op jit(solution)/shard_map/ppermute | solution.py:59
  73.5 7.1 %copy-start = (bf16[256,4096]{1,0:T(8,128)(2,1)S(1)}, bf16[256,4096]{1,0:T(8,128)(2,1)}, u32[]{:S(2)}) copy-start(bf16[256,4096]{1,0:T(8,128)(2,1)} %query_ref.3) | copy-start | bytes 6291460
  73.5 7.1 %copy-start.1 = (f32[256,256]{1,0:T(8,128)S(1)}, f32[256,256]{1,0:T(8,128)}, u32[]{:S(2)}) copy-start(f32[256,256]{1,0:T(8,128)} %concatenate.3.refs_9_.table_ref) | copy-start | bytes 786436
  75.8 14.9 %all-to-all-start = ((bf16[16,8,1024]{2,1,0:T(8,128)(2,1)}), bf16[16,8,1024]{2,1,0:T(8,128)(2,1)S(1)}, u32[]{:S(2)}, u32[]{:S(2)}) async-start(bf16[16,8,1024]{2,1,0:T(8,128)(2,1)} %bitcast.21), calls=%async_computation | async-start | bytes 524288 | tf_op jit(solution)/shard_map/all_to_all | solution.py:584
  (8 other events, 27.1 us)

commit v7 on v6

--- a/solution.py
+++ b/solution.py
@@ -512,7 +512,14 @@
     plan = (table, mask, scalars)
 
     links = Links(replicas, lax.axis_size("group"))
-    mine_weight = head_pair(kv_weight, half, False)
+    quarter = width // 4
+    mine_weight = jnp.concatenate(
+        [
+            lax.dynamic_slice_in_dim(kv_weight, (2 * j + half[0]) * quarter, quarter, 1)
+            for j in range(2)
+        ],
+        axis=1,
+    )
     other_weight = head_pair(kv_weight, half, True)
     peer_columns = core_columns(states, 1 - core, depth)
     peer_states = core_swap(peer_columns, replicas)

time: 92.7 us -> 91.8 us (level)
  Pallas kernels: 29.9 us -> 28 us
  local copies, waits for them, and re-layouts: 1.97 us -> 2.98 us
    pallas_call x2 -> x1, Pallas kernels: 3.7 us -> 1.85 us  [head_pair(): pl.pallas_call(kernel, out_shape=jax.ShapeDtypeStruct((depth, width // 2)...]
    dynamic_slice x0 -> x1, local copies, waits for them, and re-layouts: none -> 1.07 us  [per_device(): lax.dynamic_slice_in_dim(kv_weight, (2 * j + half[0]) * quarter, quarter, 1)]
where the time goes in v7:
time: 91.8 us; the launch traced here: 91.4 us
  Pallas kernels  28 us (31%)
  waiting for transfers between devices  26.5 us (29%)
  starting transfers between devices  23.9 us (26%)
  between operations  5.45 us (6%)
  other arithmetic  4.57 us (5%)
  local copies, waits for them, and re-layouts  2.98 us (3%)
    ppermute x14, waiting for transfers between devices, send(): sent.append(lax.ppermute(after(value, *before), axis, pairs))  22.4 us
    ppermute x14, starting transfers between devices, send(): sent.append(lax.ppermute(after(value, *before), axis, pairs))  18.8 us
    pallas_call x2, Pallas kernels, accumulate(): pl.pallas_call(kernel, out_shape=out_shape, in_specs=[pl.BlockSpec(memory...  12.2 us
    pallas_call x2, Pallas kernels, attend(): pl.pallas_call(kernel, out_shape=jax.ShapeDtypeStruct(queries.shape, jnp....  6.9 us
    all_to_all x1, starting transfers between devices, per_device(): spans = lax.all_to_all(spans, 'dp', split_axis=0, concat_axis=0, tiled=True)  4.82 us
    all_to_all x1, waiting for transfers between devices, per_device(): spans = lax.all_to_all(spans, 'dp', split_axis=0, concat_axis=0, tiled=True)  3.12 us
    pallas_call x1, Pallas kernels, core_columns(): pl.pallas_call(kernel, out_shape=jax.ShapeDtypeStruct((tokens, width // 2...  2.93 us
    pallas_call x1, Pallas kernels, head_pair(): pl.pallas_call(kernel, out_shape=jax.ShapeDtypeStruct((depth, width // 2)...  1.85 us
  transfers between devices with their start and end apart: 18, of which 10 were waited for; matrix products, arithmetic and copies ran while one was open for 7% of the time, Pallas kernels for 28%

profile of v7, /device:TPU:0, one launch (start us, length us, event | category | flops | bytes accessed | tf_op | source)
XLA Modules:
  0.0 91.4 jit_solution(8992054006956433424)
XLA Ops:
  1.8 4.1 %collective-permute-start.1 = (bf16[512,512]{1,0:T(8,128)(2,1)S(1)}, bf16[512,512]{1,0:T(8,128)(2,1)S(1)}, u32[]{:S(2)}, u32[]{:S(2)}) collective-permute-start(bf16[512,512]{1,0:T(8,128)(2,1)S(1)} %pad_maximum_fusion.refs_2_), channel_id=1, source_target_pairs={{0,8},{1,9},{2,10},{3,11},{4,0},{5,1},{6,2},{7,3},{8,12},{9,13},{1... | collective-permute-start | bytes 1572872 | tf_op jit(solution)/shard_map/ppermute | solution.py:54
  5.9 1.5 %collective-permute-start.6 = (bf16[512,512]{1,0:T(8,128)(2,1)S(1)}, bf16[512,512]{1,0:T(8,128)(2,1)S(1)}, u32[]{:S(2)}, u32[]{:S(2)}) collective-permute-start(bf16[512,512]{1,0:T(8,128)(2,1)S(1)} %pad_maximum_fusion.refs_2_), channel_id=1, source_target_pairs={{0,2},{1,3},{2,0},{3,1},{4,6},{5,7},{6,4},{7,5},{8,10},{9,11},{10,... | collective-permute-start | bytes 1572872 | tf_op jit(solution)/shard_map/ppermute | solution.py:54
  7.4 2.9 %shard_map.86 = bf16[256,4096]{1,0:T(8,128)(2,1)} custom-call(s32[1]{0:T(128)S(6)} %sub.93.core_ref, bf16[256,8192]{1,0:T(8,128)(2,1)} %refs_1_.3), custom_call_target="tpu_custom_call" | custom-call | bytes 4194304 | tf_op jit(solution)/shard_map/pallas_call | solution.py:114
  19.8 1.5 %collective-permute-start.8 = (bf16[512,512]{1,0:T(8,128)(2,1)S(1)}, bf16[512,512]{1,0:T(8,128)(2,1)S(1)}, u32[]{:S(2)}, u32[]{:S(2)}) collective-permute-start(bf16[512,512]{1,0:T(8,128)(2,1)S(1)} %collective-permute-done.1.refs_4_), channel_id=1, source_target_pairs={{0,16},{16,0},{1,17},{17,1},{2,18},{18,2},{3,19},{19,3},{4,20},{20... | collective-permute-start | bytes 1572872 | tf_op jit(solution)/shard_map/ppermute | solution.py:54
  24.0 6.1 %collective-permute-done.2.refs_6_ = bf16[512,512]{1,0:T(8,128)(2,1)S(1)} collective-permute-done((bf16[512,512]{1,0:T(8,128)(2,1)S(1)}, bf16[512,512]{1,0:T(8,128)(2,1)S(1)}, u32[]{:S(2)}, u32[]{:S(2)}) %collective-permute-start.2) | collective-permute-done | bytes 524320 | tf_op jit(solution)/shard_map/ppermute | solution.py:54
  30.7 1.5 %collective-permute-start.7 = (bf16[512,512]{1,0:T(8,128)(2,1)S(1)}, bf16[512,512]{1,0:T(8,128)(2,1)}, u32[]{:S(2)}, u32[]{:S(2)}) collective-permute-start(bf16[512,512]{1,0:T(8,128)(2,1)S(1)} %collective-permute-done.2.refs_6_), channel_id=1, source_target_pairs={{0,2},{1,3},{2,0},{3,1},{4,6},{5,7},{6,4},{7,5},{8,10},{9,11},{10,... | collective-permute-start | bytes 1572872 | tf_op jit(solution)/shard_map/ppermute | solution.py:54
  33.1 1.5 %collective-permute-start.9 = (bf16[512,512]{1,0:T(8,128)(2,1)S(1)}, bf16[512,512]{1,0:T(8,128)(2,1)S(1)}, u32[]{:S(2)}, u32[]{:S(2)}) collective-permute-start(bf16[512,512]{1,0:T(8,128)(2,1)S(1)} %collective-permute-done.4.refs_5_), channel_id=1, source_target_pairs={{0,16},{16,0},{1,17},{17,1},{2,18},{18,2},{3,19},{19,3},{4,20},{20... | collective-permute-start | bytes 1572872 | tf_op jit(solution)/shard_map/ppermute | solution.py:54
  34.6 1.9 %shard_map.87.refs_9_ = bf16[512,512]{1,0:T(8,128)(2,1)} custom-call(s32[1]{0:T(128)} %bitcast.half_ref, bf16[512,1024]{1,0:T(8,128)(2,1)} %weight_ref.1), custom_call_target="tpu_custom_call" | custom-call | bytes 1048576 | tf_op jit(solution)/shard_map/pallas_call | solution.py:81
  36.4 7.7 %collective-permute-done.3.refs_8_ = bf16[512,512]{1,0:T(8,128)(2,1)} collective-permute-done((bf16[512,512]{1,0:T(8,128)(2,1)S(1)}, bf16[512,512]{1,0:T(8,128)(2,1)}, u32[]{:S(2)}, u32[]{:S(2)}) %collective-permute-start.3) | collective-permute-done | bytes 524320 | tf_op jit(solution)/shard_map/ppermute | solution.py:54
  44.1 1.3 %collective-permute-start.11 = (bf16[512,512]{1,0:T(8,128)(2,1)}, bf16[512,512]{1,0:T(8,128)(2,1)S(1)}, u32[]{:S(2)}, u32[]{:S(2)}) collective-permute-start(bf16[512,512]{1,0:T(8,128)(2,1)} %shard_map.87.refs_9_), channel_id=1, source_target_pairs={{8,0},{9,1},{10,2},{11,3},{0,4},{1,5},{2,6},{3,7},{12,8},{13,9},{1... | collective-permute-start | bytes 1572872 | tf_op jit(solution)/shard_map/ppermute | solution.py:54
  45.4 1.5 %collective-permute-start.5 = (bf16[512,512]{1,0:T(8,128)(2,1)}, bf16[512,512]{1,0:T(8,128)(2,1)S(1)}, u32[]{:S(2)}, u32[]{:S(2)}) collective-permute-start(bf16[512,512]{1,0:T(8,128)(2,1)} %collective-permute-done.3.refs_8_), channel_id=1, source_target_pairs={{0,2},{1,3},{2,0},{3,1},{4,6},{5,7},{6,4},{7,5},{8,10},{9,11},{10,... | collective-permute-start | bytes 1572872 | tf_op jit(solution)/shard_map/ppermute | solution.py:54
  46.9 1.6 %collective-permute-start.10 = (bf16[512,512]{1,0:T(8,128)(2,1)}, bf16[512,512]{1,0:T(8,128)(2,1)S(1)}, u32[]{:S(2)}, u32[]{:S(2)}) collective-permute-start(bf16[512,512]{1,0:T(8,128)(2,1)} %collective-permute-done.7.refs_7_), channel_id=1, source_target_pairs={{0,16},{16,0},{1,17},{17,1},{2,18},{18,2},{3,19},{19,3},{4,20},{20... | collective-permute-start | bytes 1572872 | tf_op jit(solution)/shard_map/ppermute | solution.py:54
  49.4 7.3 %shard_map.88 = (f32[256,512]{1,0:T(8,128)}, f32[256,512]{1,0:T(8,128)}, f32[256,512]{1,0:T(8,128)}, f32[256,512]{1,0:T(8,128)}) custom-call(s32[12]{0:T(128)S(1)} %stack.58.scalar_ref, bf16[256,4096]{1,0:T(8,128)(2,1)} %collective-permute-done.refs_0_, bf16[256,8192]{1,0:T(8,128)(2,1)} %refs_1_.3, bf16[512,512]{1,0:T(8,128)(2,1)} %copy-done.2, ...), custom_call_target="tpu_custom_call" | custom-call | flops 2684354560 | bytes 10485760 | tf_op jit(solution)/shard_map/pallas_call | solution.py:229
  56.8 1.5 %collective-permute-done.11.refs_4_ = bf16[512,512]{1,0:T(8,128)(2,1)S(1)} collective-permute-done((bf16[512,512]{1,0:T(8,128)(2,1)}, bf16[512,512]{1,0:T(8,128)(2,1)S(1)}, u32[]{:S(2)}, u32[]{:S(2)}) %collective-permute-start.11) | collective-permute-done | bytes 524320 | tf_op jit(solution)/shard_map/ppermute | solution.py:54
  58.4 2.1 %collective-permute-done.5.refs_2_ = bf16[512,512]{1,0:T(8,128)(2,1)S(1)} collective-permute-done((bf16[512,512]{1,0:T(8,128)(2,1)}, bf16[512,512]{1,0:T(8,128)(2,1)S(1)}, u32[]{:S(2)}, u32[]{:S(2)}) %collective-permute-start.5) | collective-permute-done | bytes 524320 | tf_op jit(solution)/shard_map/ppermute | solution.py:54
  60.5 1.6 %collective-permute-start.14 = (bf16[512,512]{1,0:T(8,128)(2,1)S(1)}, bf16[512,512]{1,0:T(8,128)(2,1)S(1)}, u32[]{:S(2)}, u32[]{:S(2)}) collective-permute-start(bf16[512,512]{1,0:T(8,128)(2,1)S(1)} %collective-permute-done.5.refs_2_), channel_id=1, source_target_pairs={{0,16},{16,0},{1,17},{17,1},{2,18},{18,2},{3,19},{19,3},{4,20},{20... | collective-permute-start | bytes 1572872 | tf_op jit(solution)/shard_map/ppermute | solution.py:54
  62.1 4.9 %shard_map.89 = (f32[256,512]{1,0:T(8,128)S(1)}, f32[256,512]{1,0:T(8,128)S(1)}, f32[256,512]{1,0:T(8,128)S(1)}, f32[256,512]{1,0:T(8,128)S(1)}, bf16[256,1536]{...) custom-call(s32[8]{0:T(128)S(1)} %stack.51.scalar_ref, ...), custom_call_target="tpu_custom_call" | custom-call | flops 805306368 | bytes 3145728 | tf_op jit(solution)/shard_map/pallas_call | solution.py:229
  67.1 2.1 %collective-permute-done.13.refs_1_ = bf16[512,512]{1,0:T(8,128)(2,1)S(1)} collective-permute-done((bf16[512,512]{1,0:T(8,128)(2,1)}, bf16[512,512]{1,0:T(8,128)(2,1)S(1)}, u32[]{:S(2)}, u32[]{:S(2)}) %collective-permute-start.13) | collective-permute-done | bytes 524320 | tf_op jit(solution)/shard_map/ppermute | solution.py:54
  69.2 2.0 %collective-permute-done.12.refs_0_ = bf16[512,512]{1,0:T(8,128)(2,1)S(1)} collective-permute-done((bf16[512,512]{1,0:T(8,128)(2,1)S(1)}, bf16[512,512]{1,0:T(8,128)(2,1)S(1)}, u32[]{:S(2)}, u32[]{:S(2)}) %collective-permute-start.12) | collective-permute-done | bytes 524320 | tf_op jit(solution)/shard_map/ppermute | solution.py:54
  74.8 4.8 %all-to-all-start = ((bf16[16,8,1024]{2,1,0:T(8,128)(2,1)}), bf16[16,8,1024]{2,1,0:T(8,128)(2,1)S(1)}, u32[]{:S(2)}, u32[]{:S(2)}) async-start(bf16[16,8,1024]{2,1,0:T(8,128)(2,1)} %bitcast.21), calls=%async_computation | async-start | bytes 524288 | tf_op jit(solution)/shard_map/all_to_all | solution.py:591
  79.7 3.5 %shard_map.94.refs_0_ = bf16[256,4096]{1,0:T(8,128)(2,1)} custom-call(s32[1]{0:T(128)} %bitcast.half_ref, f32[256,256]{1,0:T(8,128)S(1)} %fusion.3.mask_ref, f32[256,256]{1,0:T(8,128)S(1)} %copy-done.1, bf16[256,4096]{1,0:T(8,128)(2,1)S(1)} %copy-done, bf16[256,512]{1,0:T(8,128)(2,1)S(1)} %get-tuple-element.52.key_ref.value_ref.mine_ref, ...), custom_call_target="tpu_custom_call" | custom-call | flops 536870912 | bytes 2097152 | tf_op jit(solution)/shard_map/pallas_call | solution.py:387
  83.1 3.4 %shard_map.95 = bf16[256,4096]{1,0:T(8,128)(2,1)} custom-call(s32[1]{0:T(128)} %bitcast.half_ref, f32[256,256]{1,0:T(8,128)S(1)} %fusion.3.mask_ref, f32[256,256]{1,0:T(8,128)S(1)} %copy-done.1, bf16[256,4096]{1,0:T(8,128)(2,1)S(1)} %copy-done, bf16[256,512]{1,0:T(8,128)(2,1)S(1)} %get-tuple-element.51.key_ref.value_ref.other_ref, ...), custom_call_target="tpu_custom_call", output_to_operand_aliasing={{}: (6, {})} | custom-call | flops 536870912 | bytes 2097152 | tf_op jit(solution)/shard_map/pallas_call | solution.py:387
  86.6 3.1 %all-to-all-done = bf16[16,8,1024]{2,1,0:T(8,128)(2,1)S(1)} async-done(((bf16[16,8,1024]{2,1,0:T(8,128)(2,1)}), bf16[16,8,1024]{2,1,0:T(8,128)(2,1)S(1)}, u32[]{:S(2)}, u32[]{:S(2)}) %all-to-all-start) | async-done | bytes 262176 | tf_op jit(solution)/shard_map/all_to_all | solution.py:591
  89.7 1.7 %shard_map.96 = bf16[192,1024]{1,0:T(8,128)(2,1)} custom-call(s32[2]{0:T(128)S(1)} %pad_add_fusion.scalar_ref, f32[256,256]{1,0:T(8,128)S(1)} %copy-done.1, bf16[256,512]{1,0:T(8,128)(2,1)S(1)} %get-tuple-element.52.key_ref.value_ref.mine_ref, bf16[256,512]{1,0:T(8,128)(2,1)S(1)} %get-tuple-element.51.key_ref.value_ref.other_ref, bf16[128,1024]{1,0:T(8,128)(2,1)S(1)} %bitcast.20), custom_call_target="tpu_custom_call" | custom-call | flops 50331648 | bytes 786432 | tf_op jit(solution)/shard_map/pallas_call | solution.py:446
  (71 shorter events, 14.8 us)
Async XLA Ops:
  1.8 8.6 %copy-start.2 = (bf16[512,512]{1,0:T(8,128)(2,1)}, bf16[512,512]{1,0:T(8,128)(2,1)S(1)}, u32[]{:S(2)}) copy-start(bf16[512,512]{1,0:T(8,128)(2,1)S(1)} %pad_maximum_fusion.refs_2_) | copy-start | bytes 1572868
  1.8 16.8 %collective-permute-start.1 = (bf16[512,512]{1,0:T(8,128)(2,1)S(1)}, bf16[512,512]{1,0:T(8,128)(2,1)S(1)}, u32[]{:S(2)}, u32[]{:S(2)}) collective-permute-start(bf16[512,512]{1,0:T(8,128)(2,1)S(1)} %pad_maximum_fusion.refs_2_), channel_id=1, source_target_pairs={{0,8},{1,9},{2,10},{3,11},{4,0},{5,1},{6,2},{7,3},{8,12},{9,13},{1... | collective-permute-start | bytes 1572872 | tf_op jit(solution)/shard_map/ppermute | solution.py:54
  5.9 24.8 %collective-permute-start.6 = (bf16[512,512]{1,0:T(8,128)(2,1)S(1)}, bf16[512,512]{1,0:T(8,128)(2,1)S(1)}, u32[]{:S(2)}, u32[]{:S(2)}) collective-permute-start(bf16[512,512]{1,0:T(8,128)(2,1)S(1)} %pad_maximum_fusion.refs_2_), channel_id=1, source_target_pairs={{0,2},{1,3},{2,0},{3,1},{4,6},{5,7},{6,4},{7,5},{8,10},{9,11},{10,... | collective-permute-start | bytes 1572872 | tf_op jit(solution)/shard_map/ppermute | solution.py:54
  10.3 39.1 %collective-permute-start = (bf16[256,4096]{1,0:T(8,128)(2,1)}, bf16[256,4096]{1,0:T(8,128)(2,1)}, u32[]{:S(2)}, u32[]{:S(2)}) collective-permute-start(bf16[256,4096]{1,0:T(8,128)(2,1)} %shard_map.86), channel_id=1, source_target_pairs={{0,1},{1,0},{2,3},{3,2},{4,5},{5,4},{6,7},{7,6},{8,9},{9,8},{10,11... | collective-permute-start | bytes 6291464 | tf_op jit(solution)/shard_map/ppermute | solution.py:59
  10.4 19.7 %collective-permute-start.2 = (bf16[512,512]{1,0:T(8,128)(2,1)S(1)}, bf16[512,512]{1,0:T(8,128)(2,1)S(1)}, u32[]{:S(2)}, u32[]{:S(2)}) collective-permute-start(bf16[512,512]{1,0:T(8,128)(2,1)S(1)} %pad_maximum_fusion.refs_2_), channel_id=1, source_target_pairs={{8,0},{9,1},{10,2},{11,3},{0,4},{1,5},{2,6},{3,7},{12,8},{13,9},{1... | collective-permute-start | bytes 1572872 | tf_op jit(solution)/shard_map/ppermute | solution.py:54
  18.6 30.8 %copy-start.6 = (bf16[512,512]{1,0:T(8,128)(2,1)}, bf16[512,512]{1,0:T(8,128)(2,1)S(1)}, u32[]{:S(2)}) copy-start(bf16[512,512]{1,0:T(8,128)(2,1)S(1)} %collective-permute-done.1.refs_4_) | copy-start | bytes 1572868
  18.6 14.3 %collective-permute-start.4 = (bf16[512,512]{1,0:T(8,128)(2,1)S(1)}, bf16[512,512]{1,0:T(8,128)(2,1)S(1)}, u32[]{:S(2)}, u32[]{:S(2)}) collective-permute-start(bf16[512,512]{1,0:T(8,128)(2,1)S(1)} %collective-permute-done.1.refs_4_), channel_id=1, source_target_pairs={{0,2},{1,3},{2,0},{3,1},{4,6},{5,7},{6,4},{7,5},{8,10},{9,11},{10,... | collective-permute-start | bytes 1572872 | tf_op jit(solution)/shard_map/ppermute | solution.py:54
  19.8 13.3 %collective-permute-start.8 = (bf16[512,512]{1,0:T(8,128)(2,1)S(1)}, bf16[512,512]{1,0:T(8,128)(2,1)S(1)}, u32[]{:S(2)}, u32[]{:S(2)}) collective-permute-start(bf16[512,512]{1,0:T(8,128)(2,1)S(1)} %collective-permute-done.1.refs_4_), channel_id=1, source_target_pairs={{0,16},{16,0},{1,17},{17,1},{2,18},{18,2},{3,19},{19,3},{4,20},{20... | collective-permute-start | bytes 1572872 | tf_op jit(solution)/shard_map/ppermute | solution.py:54
  30.1 16.8 %copy-start.8 = (bf16[512,512]{1,0:T(8,128)(2,1)}, bf16[512,512]{1,0:T(8,128)(2,1)S(1)}, u32[]{:S(2)}) copy-start(bf16[512,512]{1,0:T(8,128)(2,1)S(1)} %collective-permute-done.2.refs_6_) | copy-start | bytes 1572868
  30.1 14.0 %collective-permute-start.3 = (bf16[512,512]{1,0:T(8,128)(2,1)S(1)}, bf16[512,512]{1,0:T(8,128)(2,1)}, u32[]{:S(2)}, u32[]{:S(2)}) collective-permute-start(bf16[512,512]{1,0:T(8,128)(2,1)S(1)} %collective-permute-done.1.refs_4_), channel_id=1, source_target_pairs={{0,8},{1,9},{2,10},{3,11},{4,0},{5,1},{6,2},{7,3},{8,12},{9,13},{1... | collective-permute-start | bytes 1572872 | tf_op jit(solution)/shard_map/ppermute | solution.py:54
  30.7 16.2 %collective-permute-start.7 = (bf16[512,512]{1,0:T(8,128)(2,1)S(1)}, bf16[512,512]{1,0:T(8,128)(2,1)}, u32[]{:S(2)}, u32[]{:S(2)}) collective-permute-start(bf16[512,512]{1,0:T(8,128)(2,1)S(1)} %collective-permute-done.2.refs_6_), channel_id=1, source_target_pairs={{0,2},{1,3},{2,0},{3,1},{4,6},{5,7},{6,4},{7,5},{8,10},{9,11},{10,... | collective-permute-start | bytes 1572872 | tf_op jit(solution)/shard_map/ppermute | solution.py:54
  32.9 15.6 %copy-start.9 = (bf16[512,512]{1,0:T(8,128)(2,1)}, bf16[512,512]{1,0:T(8,128)(2,1)S(1)}, u32[]{:S(2)}) copy-start(bf16[512,512]{1,0:T(8,128)(2,1)S(1)} %collective-permute-done.4.refs_5_) | copy-start | bytes 1572868
  33.1 11.0 %copy-start.10 = (bf16[512,512]{1,0:T(8,128)(2,1)}, bf16[512,512]{1,0:T(8,128)(2,1)S(1)}, u32[]{:S(2)}) copy-start(bf16[512,512]{1,0:T(8,128)(2,1)S(1)} %collective-permute-done.8.refs_10_) | copy-start | bytes 1572868
  33.1 13.8 %collective-permute-start.9 = (bf16[512,512]{1,0:T(8,128)(2,1)S(1)}, bf16[512,512]{1,0:T(8,128)(2,1)S(1)}, u32[]{:S(2)}, u32[]{:S(2)}) collective-permute-start(bf16[512,512]{1,0:T(8,128)(2,1)S(1)} %collective-permute-done.4.refs_5_), channel_id=1, source_target_pairs={{0,16},{16,0},{1,17},{17,1},{2,18},{18,2},{3,19},{19,3},{4,20},{20... | collective-permute-start | bytes 1572872 | tf_op jit(solution)/shard_map/ppermute | solution.py:54
  44.1 14.2 %collective-permute-start.11 = (bf16[512,512]{1,0:T(8,128)(2,1)}, bf16[512,512]{1,0:T(8,128)(2,1)S(1)}, u32[]{:S(2)}, u32[]{:S(2)}) collective-permute-start(bf16[512,512]{1,0:T(8,128)(2,1)} %shard_map.87.refs_9_), channel_id=1, source_target_pairs={{8,0},{9,1},{10,2},{11,3},{0,4},{1,5},{2,6},{3,7},{12,8},{13,9},{1... | collective-permute-start | bytes 1572872 | tf_op jit(solution)/shard_map/ppermute | solution.py:54
  45.4 15.1 %collective-permute-start.5 = (bf16[512,512]{1,0:T(8,128)(2,1)}, bf16[512,512]{1,0:T(8,128)(2,1)S(1)}, u32[]{:S(2)}, u32[]{:S(2)}) collective-permute-start(bf16[512,512]{1,0:T(8,128)(2,1)} %collective-permute-done.3.refs_8_), channel_id=1, source_target_pairs={{0,2},{1,3},{2,0},{3,1},{4,6},{5,7},{6,4},{7,5},{8,10},{9,11},{10,... | collective-permute-start | bytes 1572872 | tf_op jit(solution)/shard_map/ppermute | solution.py:54
  46.9 13.5 %collective-permute-start.10 = (bf16[512,512]{1,0:T(8,128)(2,1)}, bf16[512,512]{1,0:T(8,128)(2,1)S(1)}, u32[]{:S(2)}, u32[]{:S(2)}) collective-permute-start(bf16[512,512]{1,0:T(8,128)(2,1)} %collective-permute-done.7.refs_7_), channel_id=1, source_target_pairs={{0,16},{16,0},{1,17},{17,1},{2,18},{18,2},{3,19},{19,3},{4,20},{20... | collective-permute-start | bytes 1572872 | tf_op jit(solution)/shard_map/ppermute | solution.py:54
  48.6 20.7 %collective-permute-start.13 = (bf16[512,512]{1,0:T(8,128)(2,1)}, bf16[512,512]{1,0:T(8,128)(2,1)S(1)}, u32[]{:S(2)}, u32[]{:S(2)}) collective-permute-start(bf16[512,512]{1,0:T(8,128)(2,1)} %shard_map.87.refs_9_), channel_id=1, source_target_pairs={{0,2},{1,3},{2,0},{3,1},{4,6},{5,7},{6,4},{7,5},{8,10},{9,11},{10,... | collective-permute-start | bytes 1572872 | tf_op jit(solution)/shard_map/ppermute | solution.py:54
  58.3 13.0 %collective-permute-start.12 = (bf16[512,512]{1,0:T(8,128)(2,1)S(1)}, bf16[512,512]{1,0:T(8,128)(2,1)S(1)}, u32[]{:S(2)}, u32[]{:S(2)}) collective-permute-start(bf16[512,512]{1,0:T(8,128)(2,1)S(1)} %collective-permute-done.11.refs_4_), channel_id=1, source_target_pairs={{8,0},{9,1},{10,2},{11,3},{0,4},{1,5},{2,6},{3,7},{12,8},{13,9},{1... | collective-permute-start | bytes 1572872 | tf_op jit(solution)/shard_map/ppermute | solution.py:54
  60.5 10.8 %collective-permute-start.14 = (bf16[512,512]{1,0:T(8,128)(2,1)S(1)}, bf16[512,512]{1,0:T(8,128)(2,1)S(1)}, u32[]{:S(2)}, u32[]{:S(2)}) collective-permute-start(bf16[512,512]{1,0:T(8,128)(2,1)S(1)} %collective-permute-done.5.refs_2_), channel_id=1, source_target_pairs={{0,16},{16,0},{1,17},{17,1},{2,18},{18,2},{3,19},{19,3},{4,20},{20... | collective-permute-start | bytes 1572872 | tf_op jit(solution)/shard_map/ppermute | solution.py:54
  67.0 5.5 %collective-permute-start.16 = (f32[256,512]{1,0:T(8,128)S(1)}, f32[256,512]{1,0:T(8,128)S(1)}, u32[]{:S(2)}, u32[]{:S(2)}) collective-permute-start(f32[256,512]{1,0:T(8,128)S(1)} %get-tuple-element.49), channel_id=1, source_target_pairs={{0,1},{1,0},{2,3},{3,2},{4,5},{5,4},{6,7},{7,6},{8,9},{9,8},{10,11... | collective-permute-start | bytes 1572872 | tf_op jit(solution)/shard_map/ppermute | solution.py:59
  71.9 2.0 %collective-permute-start.15 = (f32[256,512]{1,0:T(8,128)S(1)}, f32[256,512]{1,0:T(8,128)S(1)}, u32[]{:S(2)}, u32[]{:S(2)}) collective-permute-start(f32[256,512]{1,0:T(8,128)S(1)} %shard_map.91), channel_id=1, source_target_pairs={{0,1},{1,0},{2,3},{3,2},{4,5},{5,4},{6,7},{7,6},{8,9},{9,8},{10,11... | collective-permute-start | bytes 1572872 | tf_op jit(solution)/shard_map/ppermute | solution.py:59
  72.5 7.1 %copy-start = (bf16[256,4096]{1,0:T(8,128)(2,1)S(1)}, bf16[256,4096]{1,0:T(8,128)(2,1)}, u32[]{:S(2)}) copy-start(bf16[256,4096]{1,0:T(8,128)(2,1)} %query_ref.3) | copy-start | bytes 6291460
  74.8 14.9 %all-to-all-start = ((bf16[16,8,1024]{2,1,0:T(8,128)(2,1)}), bf16[16,8,1024]{2,1,0:T(8,128)(2,1)S(1)}, u32[]{:S(2)}, u32[]{:S(2)}) async-start(bf16[16,8,1024]{2,1,0:T(8,128)(2,1)} %bitcast.21), calls=%async_computation | async-start | bytes 524288 | tf_op jit(solution)/shard_map/all_to_all | solution.py:591
  (8 other events, 30.9 us)

commit v8 on v7

--- a/solution.py
+++ b/solution.py
@@ -547,7 +547,8 @@
         mine.append((held[k], block(k, False)))
         crossed = links.send(held[k], "y")
         if 1 <= k < fore:
-            other.append((links.send(held[k], "x"), block(k, False)))
+            swapped = links.send(held[k], "x")
+            other.append((swapped, block(k, False)))
         if final:
             early = mine + other
             sums = accumulate(
@@ -557,13 +558,13 @@
                 [0] * len(mine) + [1] * len(other),
                 bias=kv_bias[None, :],
             )
+            swapped = links.send(swapped, "fore")
+            middle.append((swapped, block(fore, False)))
             for j in range(1, ring - fore):
-                moving = links.send(moving, "back")
-                middle.append((moving, block(-j, False)))
-            moving = links.send(moving, "back", sums)
-            late.append((moving, block(fore - ring, False)))
+                moving = links.send(moving, "back", sums)
+                (late if j == ring - fore - 1 else middle).append((moving, block(-j, False)))
             late.append((links.send(other_weight, "y"), block(0, True)))
-            late.append((links.send(crossed, "x", sums), block(k, True)))
+            late.append((links.send(crossed, "x"), block(k, True)))
             middle = [(crossed, block(k, True))] + middle
             mine_peer, mine_own, other_peer, other_own, left_peer, left_own, pick = accumulate(
                 both,

time: 91.8 us -> 91.5 us (level)
    ppermute x14, starting transfers between devices: 18.8 us -> 19.8 us  [send(): sent.append(lax.ppermute(after(value, *before), axis, pairs))]
  transfers between devices with their start and end apart: 18 -> 18, of which waited for: 10 -> 9; matrix products, arithmetic and copies ran while one was open for 7% -> 7% of each run, Pallas kernels for 28% -> 28%
where the time goes in v8:
time: 91.5 us; the launch traced here: 91.1 us
  Pallas kernels  28 us (31%)
  waiting for transfers between devices  25.6 us (28%)
  starting transfers between devices  24.5 us (27%)
  between operations  5.47 us (6%)
  other arithmetic  4.53 us (5%)
  local copies, waits for them, and re-layouts  2.97 us (3%)
    ppermute x14, waiting for transfers between devices, send(): sent.append(lax.ppermute(after(value, *before), axis, pairs))  21.5 us
    ppermute x14, starting transfers between devices, send(): sent.append(lax.ppermute(after(value, *before), axis, pairs))  19.8 us
    pallas_call x2, Pallas kernels, accumulate(): pl.pallas_call(kernel, out_shape=out_shape, in_specs=[pl.BlockSpec(memory...  12.2 us
    pallas_call x2, Pallas kernels, attend(): pl.pallas_call(kernel, out_shape=jax.ShapeDtypeStruct(queries.shape, jnp....  6.92 us
    all_to_all x1, starting transfers between devices, per_device(): spans = lax.all_to_all(spans, 'dp', split_axis=0, concat_axis=0, tiled=True)  4.46 us
    all_to_all x1, waiting for transfers between devices, per_device(): spans = lax.all_to_all(spans, 'dp', split_axis=0, concat_axis=0, tiled=True)  3.1 us
    pallas_call x1, Pallas kernels, core_columns(): pl.pallas_call(kernel, out_shape=jax.ShapeDtypeStruct((tokens, width // 2...  2.93 us
    pallas_call x1, Pallas kernels, head_pair(): pl.pallas_call(kernel, out_shape=jax.ShapeDtypeStruct((depth, width // 2)...  1.86 us
  transfers between devices with their start and end apart: 18, of which 9 were waited for; matrix products, arithmetic and copies ran while one was open for 7% of the time, Pallas kernels for 28%

profile of v8, /device:TPU:0, one launch (start us, length us, event | category | flops | bytes accessed | tf_op | source)
XLA Modules:
  0.0 91.1 jit_solution(17053309925856834726)
XLA Ops:
  1.8 4.1 %collective-permute-start.1 = (bf16[512,512]{1,0:T(8,128)(2,1)S(1)}, bf16[512,512]{1,0:T(8,128)(2,1)S(1)}, u32[]{:S(2)}, u32[]{:S(2)}) collective-permute-start(bf16[512,512]{1,0:T(8,128)(2,1)S(1)} %pad_maximum_fusion.refs_2_), channel_id=1, source_target_pairs={{0,8},{1,9},{2,10},{3,11},{4,0},{5,1},{6,2},{7,3},{8,12},{9,13},{1... | collective-permute-start | bytes 1572872 | tf_op jit(solution)/shard_map/ppermute | solution.py:54
  5.9 1.5 %collective-permute-start.6 = (bf16[512,512]{1,0:T(8,128)(2,1)S(1)}, bf16[512,512]{1,0:T(8,128)(2,1)S(1)}, u32[]{:S(2)}, u32[]{:S(2)}) collective-permute-start(bf16[512,512]{1,0:T(8,128)(2,1)S(1)} %pad_maximum_fusion.refs_2_), channel_id=1, source_target_pairs={{0,2},{1,3},{2,0},{3,1},{4,6},{5,7},{6,4},{7,5},{8,10},{9,11},{10,... | collective-permute-start | bytes 1572872 | tf_op jit(solution)/shard_map/ppermute | solution.py:54
  7.4 2.9 %shard_map.86 = bf16[256,4096]{1,0:T(8,128)(2,1)} custom-call(s32[1]{0:T(128)S(6)} %sub.90.core_ref, bf16[256,8192]{1,0:T(8,128)(2,1)} %refs_1_.3), custom_call_target="tpu_custom_call" | custom-call | bytes 4194304 | tf_op jit(solution)/shard_map/pallas_call | solution.py:114
  18.6 1.2 %collective-permute-start.4 = (bf16[512,512]{1,0:T(8,128)(2,1)S(1)}, bf16[512,512]{1,0:T(8,128)(2,1)S(1)}, u32[]{:S(2)}, u32[]{:S(2)}) collective-permute-start(bf16[512,512]{1,0:T(8,128)(2,1)S(1)} %collective-permute-done.1.refs_4_), channel_id=1, source_target_pairs={{0,2},{1,3},{2,0},{3,1},{4,6},{5,7},{6,4},{7,5},{8,10},{9,11},{10,... | collective-permute-start | bytes 1572872 | tf_op jit(solution)/shard_map/ppermute | solution.py:54
  19.8 1.5 %collective-permute-start.8 = (bf16[512,512]{1,0:T(8,128)(2,1)S(1)}, bf16[512,512]{1,0:T(8,128)(2,1)}, u32[]{:S(2)}, u32[]{:S(2)}) collective-permute-start(bf16[512,512]{1,0:T(8,128)(2,1)S(1)} %collective-permute-done.1.refs_4_), channel_id=1, source_target_pairs={{0,16},{16,0},{1,17},{17,1},{2,18},{18,2},{3,19},{19,3},{4,20},{20... | collective-permute-start | bytes 1572872 | tf_op jit(solution)/shard_map/ppermute | solution.py:54
  21.3 1.2 %fusion.8 = s32[256]{0:T(256)S(1)} fusion(s32[]{:T(128)} %bitcast.3, s32[]{:T(128)} %bitcast.2), kind=kLoop, calls=%fused_computation.18 | loop fusion | flops 1280 | bytes 1032 | tf_op jit(solution)/shard_map/add | solution.py:497
  22.6 1.2 %iota_compare_fusion.4 = (pred[256]{0:T(512)(128)(4,1)S(1)}, pred[256]{0:T(512)(128)(4,1)S(1)}) fusion(s32[]{:T(128)} %bitcast.1, s32[]{:T(128)} %bitcast.3, s32[]{:T(128)} %bitcast.2), kind=kLoop, calls=%fused_computation.21 | loop fusion | flops 1792 | bytes 524 | tf_op jit(solution)/shard_map/lt | solution.py:490
  23.9 6.3 %collective-permute-done.2.refs_6_ = bf16[512,512]{1,0:T(8,128)(2,1)} collective-permute-done((bf16[512,512]{1,0:T(8,128)(2,1)S(1)}, bf16[512,512]{1,0:T(8,128)(2,1)}, u32[]{:S(2)}, u32[]{:S(2)}) %collective-permute-start.2) | collective-permute-done | bytes 524320 | tf_op jit(solution)/shard_map/ppermute | solution.py:54
  30.8 1.5 %collective-permute-start.7 = (bf16[512,512]{1,0:T(8,128)(2,1)}, bf16[512,512]{1,0:T(8,128)(2,1)}, u32[]{:S(2)}, u32[]{:S(2)}) collective-permute-start(bf16[512,512]{1,0:T(8,128)(2,1)} %collective-permute-done.2.refs_6_), channel_id=1, source_target_pairs={{0,2},{1,3},{2,0},{3,1},{4,6},{5,7},{6,4},{7,5},{8,10},{9,11},{10,... | collective-permute-start | bytes 1572872 | tf_op jit(solution)/shard_map/ppermute | solution.py:54
  33.1 1.5 %collective-permute-start.9 = (bf16[512,512]{1,0:T(8,128)(2,1)S(1)}, bf16[512,512]{1,0:T(8,128)(2,1)S(1)}, u32[]{:S(2)}, u32[]{:S(2)}) collective-permute-start(bf16[512,512]{1,0:T(8,128)(2,1)S(1)} %collective-permute-done.4.refs_5_), channel_id=1, source_target_pairs={{0,16},{16,0},{1,17},{17,1},{2,18},{18,2},{3,19},{19,3},{4,20},{20... | collective-permute-start | bytes 1572872 | tf_op jit(solution)/shard_map/ppermute | solution.py:54
  34.6 9.6 %collective-permute-done.3.refs_8_ = bf16[512,512]{1,0:T(8,128)(2,1)} collective-permute-done((bf16[512,512]{1,0:T(8,128)(2,1)S(1)}, bf16[512,512]{1,0:T(8,128)(2,1)}, u32[]{:S(2)}, u32[]{:S(2)}) %collective-permute-start.3) | collective-permute-done | bytes 524320 | tf_op jit(solution)/shard_map/ppermute | solution.py:54
  45.4 1.5 %collective-permute-start.5 = (bf16[512,512]{1,0:T(8,128)(2,1)}, bf16[512,512]{1,0:T(8,128)(2,1)S(1)}, u32[]{:S(2)}, u32[]{:S(2)}) collective-permute-start(bf16[512,512]{1,0:T(8,128)(2,1)} %collective-permute-done.3.refs_8_), channel_id=1, source_target_pairs={{0,2},{1,3},{2,0},{3,1},{4,6},{5,7},{6,4},{7,5},{8,10},{9,11},{10,... | collective-permute-start | bytes 1572872 | tf_op jit(solution)/shard_map/ppermute | solution.py:54
  46.9 1.6 %collective-permute-start.10 = (bf16[512,512]{1,0:T(8,128)(2,1)}, bf16[512,512]{1,0:T(8,128)(2,1)}, u32[]{:S(2)}, u32[]{:S(2)}) collective-permute-start(bf16[512,512]{1,0:T(8,128)(2,1)} %collective-permute-done.7.refs_7_), channel_id=1, source_target_pairs={{0,16},{16,0},{1,17},{17,1},{2,18},{18,2},{3,19},{19,3},{4,20},{20... | collective-permute-start | bytes 1572872 | tf_op jit(solution)/shard_map/ppermute | solution.py:54
  48.5 1.9 %shard_map.87.refs_9_ = bf16[512,512]{1,0:T(8,128)(2,1)} custom-call(s32[1]{0:T(128)} %bitcast.half_ref, bf16[512,1024]{1,0:T(8,128)(2,1)} %weight_ref.1), custom_call_target="tpu_custom_call" | custom-call | bytes 1048576 | tf_op jit(solution)/shard_map/pallas_call | solution.py:81
  51.4 7.3 %shard_map.88 = (f32[256,512]{1,0:T(8,128)}, f32[256,512]{1,0:T(8,128)}, f32[256,512]{1,0:T(8,128)}, f32[256,512]{1,0:T(8,128)}) custom-call(s32[12]{0:T(128)S(1)} %stack.55.scalar_ref, bf16[256,4096]{1,0:T(8,128)(2,1)} %collective-permute-done.refs_0_, bf16[256,8192]{1,0:T(8,128)(2,1)} %refs_1_.3, bf16[512,512]{1,0:T(8,128)(2,1)} %copy-done.2, ...), custom_call_target="tpu_custom_call" | custom-call | flops 2684354560 | bytes 10485760 | tf_op jit(solution)/shard_map/pallas_call | solution.py:229
  60.5 1.5 %collective-permute-start.14 = (bf16[512,512]{1,0:T(8,128)(2,1)S(1)}, bf16[512,512]{1,0:T(8,128)(2,1)S(1)}, u32[]{:S(2)}, u32[]{:S(2)}) collective-permute-start(bf16[512,512]{1,0:T(8,128)(2,1)S(1)} %collective-permute-done.5.refs_2_), channel_id=1, source_target_pairs={{0,16},{16,0},{1,17},{17,1},{2,18},{18,2},{3,19},{19,3},{4,20},{20... | collective-permute-start | bytes 1572872 | tf_op jit(solution)/shard_map/ppermute | solution.py:54
  62.0 4.9 %shard_map.89 = (f32[256,512]{1,0:T(8,128)S(1)}, f32[256,512]{1,0:T(8,128)S(1)}, f32[256,512]{1,0:T(8,128)S(1)}, f32[256,512]{1,0:T(8,128)S(1)}, bf16[256,1536]{...) custom-call(s32[8]{0:T(128)S(1)} %stack.49.scalar_ref, ...), custom_call_target="tpu_custom_call" | custom-call | flops 805306368 | bytes 3145728 | tf_op jit(solution)/shard_map/pallas_call | solution.py:229
  67.0 2.2 %collective-permute-done.13.refs_1_ = bf16[512,512]{1,0:T(8,128)(2,1)S(1)} collective-permute-done((bf16[512,512]{1,0:T(8,128)(2,1)}, bf16[512,512]{1,0:T(8,128)(2,1)S(1)}, u32[]{:S(2)}, u32[]{:S(2)}) %collective-permute-start.13) | collective-permute-done | bytes 524320 | tf_op jit(solution)/shard_map/ppermute | solution.py:54
  69.2 2.1 %collective-permute-done.12.refs_0_ = bf16[512,512]{1,0:T(8,128)(2,1)S(1)} collective-permute-done((bf16[512,512]{1,0:T(8,128)(2,1)S(1)}, bf16[512,512]{1,0:T(8,128)(2,1)S(1)}, u32[]{:S(2)}, u32[]{:S(2)}) %collective-permute-start.12) | collective-permute-done | bytes 524320 | tf_op jit(solution)/shard_map/ppermute | solution.py:54
  74.9 4.5 %all-to-all-start = ((bf16[16,8,1024]{2,1,0:T(8,128)(2,1)}), bf16[16,8,1024]{2,1,0:T(8,128)(2,1)S(1)}, u32[]{:S(2)}, u32[]{:S(2)}) async-start(bf16[16,8,1024]{2,1,0:T(8,128)(2,1)} %bitcast.20), calls=%async_computation | async-start | bytes 524288 | tf_op jit(solution)/shard_map/all_to_all | solution.py:592
  79.4 3.5 %shard_map.94.refs_0_ = bf16[256,4096]{1,0:T(8,128)(2,1)} custom-call(s32[1]{0:T(128)} %bitcast.half_ref, f32[256,256]{1,0:T(8,128)S(1)} %fusion.3.mask_ref, f32[256,256]{1,0:T(8,128)S(1)} %copy-done.1, bf16[256,4096]{1,0:T(8,128)(2,1)S(1)} %copy-done, bf16[256,512]{1,0:T(8,128)(2,1)S(1)} %get-tuple-element.52.key_ref.value_ref.mine_ref, ...), custom_call_target="tpu_custom_call" | custom-call | flops 536870912 | bytes 2097152 | tf_op jit(solution)/shard_map/pallas_call | solution.py:387
  82.9 3.4 %shard_map.95 = bf16[256,4096]{1,0:T(8,128)(2,1)} custom-call(s32[1]{0:T(128)} %bitcast.half_ref, f32[256,256]{1,0:T(8,128)S(1)} %fusion.3.mask_ref, f32[256,256]{1,0:T(8,128)S(1)} %copy-done.1, bf16[256,4096]{1,0:T(8,128)(2,1)S(1)} %copy-done, bf16[256,512]{1,0:T(8,128)(2,1)S(1)} %get-tuple-element.51.key_ref.value_ref.other_ref, ...), custom_call_target="tpu_custom_call", output_to_operand_aliasing={{}: (6, {})} | custom-call | flops 536870912 | bytes 2097152 | tf_op jit(solution)/shard_map/pallas_call | solution.py:387
  86.3 3.1 %all-to-all-done = bf16[16,8,1024]{2,1,0:T(8,128)(2,1)S(1)} async-done(((bf16[16,8,1024]{2,1,0:T(8,128)(2,1)}), bf16[16,8,1024]{2,1,0:T(8,128)(2,1)S(1)}, u32[]{:S(2)}, u32[]{:S(2)}) %all-to-all-start) | async-done | bytes 262176 | tf_op jit(solution)/shard_map/all_to_all | solution.py:592
  89.4 1.7 %shard_map.96 = bf16[192,1024]{1,0:T(8,128)(2,1)} custom-call(s32[2]{0:T(128)S(1)} %pad_add_fusion.scalar_ref, f32[256,256]{1,0:T(8,128)S(1)} %copy-done.1, bf16[256,512]{1,0:T(8,128)(2,1)S(1)} %get-tuple-element.52.key_ref.value_ref.mine_ref, bf16[256,512]{1,0:T(8,128)(2,1)S(1)} %get-tuple-element.51.key_ref.value_ref.other_ref, bf16[128,1024]{1,0:T(8,128)(2,1)S(1)} %bitcast.19), custom_call_target="tpu_custom_call" | custom-call | flops 50331648 | bytes 786432 | tf_op jit(solution)/shard_map/pallas_call | solution.py:446
  (67 shorter events, 14.0 us)
Async XLA Ops:
  1.8 8.6 %copy-start.2 = (bf16[512,512]{1,0:T(8,128)(2,1)}, bf16[512,512]{1,0:T(8,128)(2,1)S(1)}, u32[]{:S(2)}) copy-start(bf16[512,512]{1,0:T(8,128)(2,1)S(1)} %pad_maximum_fusion.refs_2_) | copy-start | bytes 1572868
  1.8 16.8 %collective-permute-start.1 = (bf16[512,512]{1,0:T(8,128)(2,1)S(1)}, bf16[512,512]{1,0:T(8,128)(2,1)S(1)}, u32[]{:S(2)}, u32[]{:S(2)}) collective-permute-start(bf16[512,512]{1,0:T(8,128)(2,1)S(1)} %pad_maximum_fusion.refs_2_), channel_id=1, source_target_pairs={{0,8},{1,9},{2,10},{3,11},{4,0},{5,1},{6,2},{7,3},{8,12},{9,13},{1... | collective-permute-start | bytes 1572872 | tf_op jit(solution)/shard_map/ppermute | solution.py:54
  5.9 24.9 %collective-permute-start.6 = (bf16[512,512]{1,0:T(8,128)(2,1)S(1)}, bf16[512,512]{1,0:T(8,128)(2,1)S(1)}, u32[]{:S(2)}, u32[]{:S(2)}) collective-permute-start(bf16[512,512]{1,0:T(8,128)(2,1)S(1)} %pad_maximum_fusion.refs_2_), channel_id=1, source_target_pairs={{0,2},{1,3},{2,0},{3,1},{4,6},{5,7},{6,4},{7,5},{8,10},{9,11},{10,... | collective-permute-start | bytes 1572872 | tf_op jit(solution)/shard_map/ppermute | solution.py:54
  10.3 41.0 %collective-permute-start = (bf16[256,4096]{1,0:T(8,128)(2,1)}, bf16[256,4096]{1,0:T(8,128)(2,1)}, u32[]{:S(2)}, u32[]{:S(2)}) collective-permute-start(bf16[256,4096]{1,0:T(8,128)(2,1)} %shard_map.86), channel_id=1, source_target_pairs={{0,1},{1,0},{2,3},{3,2},{4,5},{5,4},{6,7},{7,6},{8,9},{9,8},{10,11... | collective-permute-start | bytes 6291464 | tf_op jit(solution)/shard_map/ppermute | solution.py:59
  10.4 19.8 %collective-permute-start.2 = (bf16[512,512]{1,0:T(8,128)(2,1)S(1)}, bf16[512,512]{1,0:T(8,128)(2,1)}, u32[]{:S(2)}, u32[]{:S(2)}) collective-permute-start(bf16[512,512]{1,0:T(8,128)(2,1)S(1)} %pad_maximum_fusion.refs_2_), channel_id=1, source_target_pairs={{8,0},{9,1},{10,2},{11,3},{0,4},{1,5},{2,6},{3,7},{12,8},{13,9},{1... | collective-permute-start | bytes 1572872 | tf_op jit(solution)/shard_map/ppermute | solution.py:54
  18.6 32.8 %copy-start.6 = (bf16[512,512]{1,0:T(8,128)(2,1)}, bf16[512,512]{1,0:T(8,128)(2,1)S(1)}, u32[]{:S(2)}) copy-start(bf16[512,512]{1,0:T(8,128)(2,1)S(1)} %collective-permute-done.1.refs_4_) | copy-start | bytes 1572868
  18.6 14.3 %collective-permute-start.4 = (bf16[512,512]{1,0:T(8,128)(2,1)S(1)}, bf16[512,512]{1,0:T(8,128)(2,1)S(1)}, u32[]{:S(2)}, u32[]{:S(2)}) collective-permute-start(bf16[512,512]{1,0:T(8,128)(2,1)S(1)} %collective-permute-done.1.refs_4_), channel_id=1, source_target_pairs={{0,2},{1,3},{2,0},{3,1},{4,6},{5,7},{6,4},{7,5},{8,10},{9,11},{10,... | collective-permute-start | bytes 1572872 | tf_op jit(solution)/shard_map/ppermute | solution.py:54
  19.8 13.4 %collective-permute-start.8 = (bf16[512,512]{1,0:T(8,128)(2,1)S(1)}, bf16[512,512]{1,0:T(8,128)(2,1)}, u32[]{:S(2)}, u32[]{:S(2)}) collective-permute-start(bf16[512,512]{1,0:T(8,128)(2,1)S(1)} %collective-permute-done.1.refs_4_), channel_id=1, source_target_pairs={{0,16},{16,0},{1,17},{17,1},{2,18},{18,2},{3,19},{19,3},{4,20},{20... | collective-permute-start | bytes 1572872 | tf_op jit(solution)/shard_map/ppermute | solution.py:54
  30.2 14.0 %collective-permute-start.3 = (bf16[512,512]{1,0:T(8,128)(2,1)S(1)}, bf16[512,512]{1,0:T(8,128)(2,1)}, u32[]{:S(2)}, u32[]{:S(2)}) collective-permute-start(bf16[512,512]{1,0:T(8,128)(2,1)S(1)} %collective-permute-done.1.refs_4_), channel_id=1, source_target_pairs={{0,8},{1,9},{2,10},{3,11},{4,0},{5,1},{6,2},{7,3},{8,12},{9,13},{1... | collective-permute-start | bytes 1572872 | tf_op jit(solution)/shard_map/ppermute | solution.py:54
  30.8 20.6 %copy-start.7 = (bf16[512,512]{1,0:T(8,128)(2,1)}, bf16[512,512]{1,0:T(8,128)(2,1)S(1)}, u32[]{:S(2)}) copy-start(bf16[512,512]{1,0:T(8,128)(2,1)S(1)} %collective-permute-done.6.refs_3_) | copy-start | bytes 1572868
  30.8 16.1 %collective-permute-start.7 = (bf16[512,512]{1,0:T(8,128)(2,1)}, bf16[512,512]{1,0:T(8,128)(2,1)}, u32[]{:S(2)}, u32[]{:S(2)}) collective-permute-start(bf16[512,512]{1,0:T(8,128)(2,1)} %collective-permute-done.2.refs_6_), channel_id=1, source_target_pairs={{0,2},{1,3},{2,0},{3,1},{4,6},{5,7},{6,4},{7,5},{8,10},{9,11},{10,... | collective-permute-start | bytes 1572872 | tf_op jit(solution)/shard_map/ppermute | solution.py:54
  32.8 11.4 %copy-start.8 = (bf16[512,512]{1,0:T(8,128)(2,1)}, bf16[512,512]{1,0:T(8,128)(2,1)S(1)}, u32[]{:S(2)}) copy-start(bf16[512,512]{1,0:T(8,128)(2,1)S(1)} %collective-permute-done.4.refs_5_) | copy-start | bytes 1572868
  33.1 13.8 %collective-permute-start.9 = (bf16[512,512]{1,0:T(8,128)(2,1)S(1)}, bf16[512,512]{1,0:T(8,128)(2,1)S(1)}, u32[]{:S(2)}, u32[]{:S(2)}) collective-permute-start(bf16[512,512]{1,0:T(8,128)(2,1)S(1)} %collective-permute-done.4.refs_5_), channel_id=1, source_target_pairs={{0,16},{16,0},{1,17},{17,1},{2,18},{18,2},{3,19},{19,3},{4,20},{20... | collective-permute-start | bytes 1572872 | tf_op jit(solution)/shard_map/ppermute | solution.py:54
  44.2 14.5 %collective-permute-start.11 = (bf16[512,512]{1,0:T(8,128)(2,1)}, bf16[512,512]{1,0:T(8,128)(2,1)S(1)}, u32[]{:S(2)}, u32[]{:S(2)}) collective-permute-start(bf16[512,512]{1,0:T(8,128)(2,1)} %collective-permute-done.8.refs_10_), channel_id=1, source_target_pairs={{0,8},{1,9},{2,10},{3,11},{4,0},{5,1},{6,2},{7,3},{8,12},{9,13},{1... | collective-permute-start | bytes 1572872 | tf_op jit(solution)/shard_map/ppermute | solution.py:54
  45.4 15.1 %collective-permute-start.5 = (bf16[512,512]{1,0:T(8,128)(2,1)}, bf16[512,512]{1,0:T(8,128)(2,1)S(1)}, u32[]{:S(2)}, u32[]{:S(2)}) collective-permute-start(bf16[512,512]{1,0:T(8,128)(2,1)} %collective-permute-done.3.refs_8_), channel_id=1, source_target_pairs={{0,2},{1,3},{2,0},{3,1},{4,6},{5,7},{6,4},{7,5},{8,10},{9,11},{10,... | collective-permute-start | bytes 1572872 | tf_op jit(solution)/shard_map/ppermute | solution.py:54
  46.9 13.5 %collective-permute-start.10 = (bf16[512,512]{1,0:T(8,128)(2,1)}, bf16[512,512]{1,0:T(8,128)(2,1)}, u32[]{:S(2)}, u32[]{:S(2)}) collective-permute-start(bf16[512,512]{1,0:T(8,128)(2,1)} %collective-permute-done.7.refs_7_), channel_id=1, source_target_pairs={{0,16},{16,0},{1,17},{17,1},{2,18},{18,2},{3,19},{19,3},{4,20},{20... | collective-permute-start | bytes 1572872 | tf_op jit(solution)/shard_map/ppermute | solution.py:54
  50.4 18.8 %collective-permute-start.13 = (bf16[512,512]{1,0:T(8,128)(2,1)}, bf16[512,512]{1,0:T(8,128)(2,1)S(1)}, u32[]{:S(2)}, u32[]{:S(2)}) collective-permute-start(bf16[512,512]{1,0:T(8,128)(2,1)} %shard_map.87.refs_9_), channel_id=1, source_target_pairs={{0,2},{1,3},{2,0},{3,1},{4,6},{5,7},{6,4},{7,5},{8,10},{9,11},{10,... | collective-permute-start | bytes 1572872 | tf_op jit(solution)/shard_map/ppermute | solution.py:54
  51.4 7.4 %copy-start.3 = (bf16[512,512]{1,0:T(8,128)(2,1)S(1)}, bf16[512,512]{1,0:T(8,128)(2,1)}, u32[]{:S(2)}) copy-start(bf16[512,512]{1,0:T(8,128)(2,1)} %shard_map.87.refs_9_) | copy-start | bytes 1572868
  58.7 12.6 %collective-permute-start.12 = (bf16[512,512]{1,0:T(8,128)(2,1)S(1)}, bf16[512,512]{1,0:T(8,128)(2,1)S(1)}, u32[]{:S(2)}, u32[]{:S(2)}) collective-permute-start(bf16[512,512]{1,0:T(8,128)(2,1)S(1)} %copy-done.3), channel_id=1, source_target_pairs={{8,0},{9,1},{10,2},{11,3},{0,4},{1,5},{2,6},{3,7},{12,8},{13,9},{1... | collective-permute-start | bytes 1572872 | tf_op jit(solution)/shard_map/ppermute | solution.py:54
  60.5 10.9 %collective-permute-start.14 = (bf16[512,512]{1,0:T(8,128)(2,1)S(1)}, bf16[512,512]{1,0:T(8,128)(2,1)S(1)}, u32[]{:S(2)}, u32[]{:S(2)}) collective-permute-start(bf16[512,512]{1,0:T(8,128)(2,1)S(1)} %collective-permute-done.5.refs_2_), channel_id=1, source_target_pairs={{0,16},{16,0},{1,17},{17,1},{2,18},{18,2},{3,19},{19,3},{4,20},{20... | collective-permute-start | bytes 1572872 | tf_op jit(solution)/shard_map/ppermute | solution.py:54
  66.9 5.7 %collective-permute-start.16 = (f32[256,512]{1,0:T(8,128)S(1)}, f32[256,512]{1,0:T(8,128)S(1)}, u32[]{:S(2)}, u32[]{:S(2)}) collective-permute-start(f32[256,512]{1,0:T(8,128)S(1)} %get-tuple-element.49), channel_id=1, source_target_pairs={{0,1},{1,0},{2,3},{3,2},{4,5},{5,4},{6,7},{7,6},{8,9},{9,8},{10,11... | collective-permute-start | bytes 1572872 | tf_op jit(solution)/shard_map/ppermute | solution.py:59
  72.0 2.0 %collective-permute-start.15 = (f32[256,512]{1,0:T(8,128)S(1)}, f32[256,512]{1,0:T(8,128)S(1)}, u32[]{:S(2)}, u32[]{:S(2)}) collective-permute-start(f32[256,512]{1,0:T(8,128)S(1)} %shard_map.91), channel_id=1, source_target_pairs={{0,1},{1,0},{2,3},{3,2},{4,5},{5,4},{6,7},{7,6},{8,9},{9,8},{10,11... | collective-permute-start | bytes 1572872 | tf_op jit(solution)/shard_map/ppermute | solution.py:59
  72.6 6.8 %copy-start = (bf16[256,4096]{1,0:T(8,128)(2,1)S(1)}, bf16[256,4096]{1,0:T(8,128)(2,1)}, u32[]{:S(2)}) copy-start(bf16[256,4096]{1,0:T(8,128)(2,1)} %query_ref.3) | copy-start | bytes 6291460
  74.9 14.5 %all-to-all-start = ((bf16[16,8,1024]{2,1,0:T(8,128)(2,1)}), bf16[16,8,1024]{2,1,0:T(8,128)(2,1)S(1)}, u32[]{:S(2)}, u32[]{:S(2)}) async-start(bf16[16,8,1024]{2,1,0:T(8,128)(2,1)} %bitcast.20), calls=%async_computation | async-start | bytes 524288 | tf_op jit(solution)/shard_map/all_to_all | solution.py:592
  (6 other events, 24.5 us)

commit v9 on v8

--- a/solution.py
+++ b/solution.py
@@ -426,11 +426,12 @@
         sender = lax.broadcasted_iota(jnp.int32, (rows, slots), 1)
         hit = (target // SPAN == rank) & (target % SPAN == sender % SPAN)
         hit = jnp.where(hit & (counts[:1, slots:] > 0.5), 1.0, 0.0).astype(jnp.bfloat16)
-        keep = table_ref[:, KEEP : KEEP + 1] > 0.5
+        keep = table_ref[:, KEEP - HEAD : KEEP - HEAD + 1] > 0.5
+        arrived = jnp.dot(hit, spans_ref[...], preferred_element_type=jnp.float32)
         copies = []
         for i in range(4):
             lanes = slice(i * part, (i + 1) * part)
-            came = jnp.dot(hit, spans_ref[:, lanes], preferred_element_type=jnp.float32)
+            came = arrived[:, lanes]
             home = (mine_ref, other_ref)[i // 2][:, (i % 2) * part : (i % 2 + 1) * part]
             total_ref[i] = jnp.where(keep, home.astype(jnp.float32), came).astype(jnp.bfloat16)
             which = scalar_ref[0] if i < 2 else 1 - scalar_ref[0]
@@ -450,7 +451,7 @@
             num_scalar_prefetch=1,
             grid=(1,),
             in_specs=[
-                pl.BlockSpec((rows, table.shape[1]), lambda i, s: (0, 0)),
+                pl.BlockSpec((rows, HEAD), lambda i, s: (0, 1)),
                 home,
                 home,
                 pl.BlockSpec((slots, width), lambda i, s: (0, 0)),

time: 91.5 us -> 91.5 us (level)
  no operation moved by 1% of the time
where the time goes in v9:
time: 91.5 us; the launch traced here: 91.1 us
  Pallas kernels  28 us (31%)
  waiting for transfers between devices  25.6 us (28%)
  starting transfers between devices  24.5 us (27%)
  between operations  5.47 us (6%)
  other arithmetic  4.53 us (5%)
  local copies, waits for them, and re-layouts  2.97 us (3%)
    ppermute x14, waiting for transfers between devices, send(): sent.append(lax.ppermute(after(value, *before), axis, pairs))  21.5 us
    ppermute x14, starting transfers between devices, send(): sent.append(lax.ppermute(after(value, *before), axis, pairs))  19.8 us
    pallas_call x2, Pallas kernels, accumulate(): pl.pallas_call(kernel, out_shape=out_shape, in_specs=[pl.BlockSpec(memory...  12.2 us
    pallas_call x2, Pallas kernels, attend(): pl.pallas_call(kernel, out_shape=jax.ShapeDtypeStruct(queries.shape, jnp....  6.92 us
    all_to_all x1, starting transfers between devices, per_device(): spans = lax.all_to_all(spans, 'dp', split_axis=0, concat_axis=0, tiled=True)  4.46 us
    all_to_all x1, waiting for transfers between devices, per_device(): spans = lax.all_to_all(spans, 'dp', split_axis=0, concat_axis=0, tiled=True)  3.1 us
    pallas_call x1, Pallas kernels, core_columns(): pl.pallas_call(kernel, out_shape=jax.ShapeDtypeStruct((tokens, width // 2...  2.93 us
    pallas_call x1, Pallas kernels, head_pair(): pl.pallas_call(kernel, out_shape=jax.ShapeDtypeStruct((depth, width // 2)...  1.86 us
  transfers between devices with their start and end apart: 18, of which 9 were waited for; matrix products, arithmetic and copies ran while one was open for 7% of the time, Pallas kernels for 28%

profile of v9, /device:TPU:0, one launch (start us, length us, event | category | flops | bytes accessed | tf_op | source)
XLA Modules:
  0.0 91.1 jit_solution(13014120119401844793)
XLA Ops:
  1.8 4.1 %collective-permute-start.1 = (bf16[512,512]{1,0:T(8,128)(2,1)S(1)}, bf16[512,512]{1,0:T(8,128)(2,1)S(1)}, u32[]{:S(2)}, u32[]{:S(2)}) collective-permute-start(bf16[512,512]{1,0:T(8,128)(2,1)S(1)} %pad_maximum_fusion.refs_2_), channel_id=1, source_target_pairs={{0,8},{1,9},{2,10},{3,11},{4,0},{5,1},{6,2},{7,3},{8,12},{9,13},{1... | collective-permute-start | bytes 1572872 | tf_op jit(solution)/shard_map/ppermute | solution.py:54
  5.9 1.5 %collective-permute-start.6 = (bf16[512,512]{1,0:T(8,128)(2,1)S(1)}, bf16[512,512]{1,0:T(8,128)(2,1)S(1)}, u32[]{:S(2)}, u32[]{:S(2)}) collective-permute-start(bf16[512,512]{1,0:T(8,128)(2,1)S(1)} %pad_maximum_fusion.refs_2_), channel_id=1, source_target_pairs={{0,2},{1,3},{2,0},{3,1},{4,6},{5,7},{6,4},{7,5},{8,10},{9,11},{10,... | collective-permute-start | bytes 1572872 | tf_op jit(solution)/shard_map/ppermute | solution.py:54
  7.4 2.9 %shard_map.86 = bf16[256,4096]{1,0:T(8,128)(2,1)} custom-call(s32[1]{0:T(128)S(6)} %sub.90.core_ref, bf16[256,8192]{1,0:T(8,128)(2,1)} %refs_1_.3), custom_call_target="tpu_custom_call" | custom-call | bytes 4194304 | tf_op jit(solution)/shard_map/pallas_call | solution.py:114
  18.6 1.2 %collective-permute-start.4 = (bf16[512,512]{1,0:T(8,128)(2,1)S(1)}, bf16[512,512]{1,0:T(8,128)(2,1)S(1)}, u32[]{:S(2)}, u32[]{:S(2)}) collective-permute-start(bf16[512,512]{1,0:T(8,128)(2,1)S(1)} %collective-permute-done.1.refs_4_), channel_id=1, source_target_pairs={{0,2},{1,3},{2,0},{3,1},{4,6},{5,7},{6,4},{7,5},{8,10},{9,11},{10,... | collective-permute-start | bytes 1572872 | tf_op jit(solution)/shard_map/ppermute | solution.py:54
  19.8 1.5 %collective-permute-start.8 = (bf16[512,512]{1,0:T(8,128)(2,1)S(1)}, bf16[512,512]{1,0:T(8,128)(2,1)}, u32[]{:S(2)}, u32[]{:S(2)}) collective-permute-start(bf16[512,512]{1,0:T(8,128)(2,1)S(1)} %collective-permute-done.1.refs_4_), channel_id=1, source_target_pairs={{0,16},{16,0},{1,17},{17,1},{2,18},{18,2},{3,19},{19,3},{4,20},{20... | collective-permute-start | bytes 1572872 | tf_op jit(solution)/shard_map/ppermute | solution.py:54
  21.3 1.2 %fusion.8 = s32[256]{0:T(256)S(1)} fusion(s32[]{:T(128)} %bitcast.3, s32[]{:T(128)} %bitcast.2), kind=kLoop, calls=%fused_computation.18 | loop fusion | flops 1280 | bytes 1032 | tf_op jit(solution)/shard_map/add | solution.py:498
  22.6 1.2 %iota_compare_fusion.4 = (pred[256]{0:T(512)(128)(4,1)S(1)}, pred[256]{0:T(512)(128)(4,1)S(1)}) fusion(s32[]{:T(128)} %bitcast.1, s32[]{:T(128)} %bitcast.3, s32[]{:T(128)} %bitcast.2), kind=kLoop, calls=%fused_computation.21 | loop fusion | flops 1792 | bytes 524 | tf_op jit(solution)/shard_map/lt | solution.py:491
  23.9 6.3 %collective-permute-done.2.refs_6_ = bf16[512,512]{1,0:T(8,128)(2,1)} collective-permute-done((bf16[512,512]{1,0:T(8,128)(2,1)S(1)}, bf16[512,512]{1,0:T(8,128)(2,1)}, u32[]{:S(2)}, u32[]{:S(2)}) %collective-permute-start.2) | collective-permute-done | bytes 524320 | tf_op jit(solution)/shard_map/ppermute | solution.py:54
  30.8 1.5 %collective-permute-start.7 = (bf16[512,512]{1,0:T(8,128)(2,1)}, bf16[512,512]{1,0:T(8,128)(2,1)}, u32[]{:S(2)}, u32[]{:S(2)}) collective-permute-start(bf16[512,512]{1,0:T(8,128)(2,1)} %collective-permute-done.2.refs_6_), channel_id=1, source_target_pairs={{0,2},{1,3},{2,0},{3,1},{4,6},{5,7},{6,4},{7,5},{8,10},{9,11},{10,... | collective-permute-start | bytes 1572872 | tf_op jit(solution)/shard_map/ppermute | solution.py:54
  33.1 1.5 %collective-permute-start.9 = (bf16[512,512]{1,0:T(8,128)(2,1)S(1)}, bf16[512,512]{1,0:T(8,128)(2,1)S(1)}, u32[]{:S(2)}, u32[]{:S(2)}) collective-permute-start(bf16[512,512]{1,0:T(8,128)(2,1)S(1)} %collective-permute-done.4.refs_5_), channel_id=1, source_target_pairs={{0,16},{16,0},{1,17},{17,1},{2,18},{18,2},{3,19},{19,3},{4,20},{20... | collective-permute-start | bytes 1572872 | tf_op jit(solution)/shard_map/ppermute | solution.py:54
  34.6 9.6 %collective-permute-done.3.refs_8_ = bf16[512,512]{1,0:T(8,128)(2,1)} collective-permute-done((bf16[512,512]{1,0:T(8,128)(2,1)S(1)}, bf16[512,512]{1,0:T(8,128)(2,1)}, u32[]{:S(2)}, u32[]{:S(2)}) %collective-permute-start.3) | collective-permute-done | bytes 524320 | tf_op jit(solution)/shard_map/ppermute | solution.py:54
  45.4 1.5 %collective-permute-start.5 = (bf16[512,512]{1,0:T(8,128)(2,1)}, bf16[512,512]{1,0:T(8,128)(2,1)S(1)}, u32[]{:S(2)}, u32[]{:S(2)}) collective-permute-start(bf16[512,512]{1,0:T(8,128)(2,1)} %collective-permute-done.3.refs_8_), channel_id=1, source_target_pairs={{0,2},{1,3},{2,0},{3,1},{4,6},{5,7},{6,4},{7,5},{8,10},{9,11},{10,... | collective-permute-start | bytes 1572872 | tf_op jit(solution)/shard_map/ppermute | solution.py:54
  46.9 1.6 %collective-permute-start.10 = (bf16[512,512]{1,0:T(8,128)(2,1)}, bf16[512,512]{1,0:T(8,128)(2,1)}, u32[]{:S(2)}, u32[]{:S(2)}) collective-permute-start(bf16[512,512]{1,0:T(8,128)(2,1)} %collective-permute-done.7.refs_7_), channel_id=1, source_target_pairs={{0,16},{16,0},{1,17},{17,1},{2,18},{18,2},{3,19},{19,3},{4,20},{20... | collective-permute-start | bytes 1572872 | tf_op jit(solution)/shard_map/ppermute | solution.py:54
  48.5 1.9 %shard_map.87.refs_9_ = bf16[512,512]{1,0:T(8,128)(2,1)} custom-call(s32[1]{0:T(128)} %bitcast.half_ref, bf16[512,1024]{1,0:T(8,128)(2,1)} %weight_ref.1), custom_call_target="tpu_custom_call" | custom-call | bytes 1048576 | tf_op jit(solution)/shard_map/pallas_call | solution.py:81
  51.4 7.3 %shard_map.88 = (f32[256,512]{1,0:T(8,128)}, f32[256,512]{1,0:T(8,128)}, f32[256,512]{1,0:T(8,128)}, f32[256,512]{1,0:T(8,128)}) custom-call(s32[12]{0:T(128)S(1)} %stack.55.scalar_ref, bf16[256,4096]{1,0:T(8,128)(2,1)} %collective-permute-done.refs_0_, bf16[256,8192]{1,0:T(8,128)(2,1)} %refs_1_.3, bf16[512,512]{1,0:T(8,128)(2,1)} %copy-done.2, ...), custom_call_target="tpu_custom_call" | custom-call | flops 2684354560 | bytes 10485760 | tf_op jit(solution)/shard_map/pallas_call | solution.py:229
  60.5 1.5 %collective-permute-start.14 = (bf16[512,512]{1,0:T(8,128)(2,1)S(1)}, bf16[512,512]{1,0:T(8,128)(2,1)S(1)}, u32[]{:S(2)}, u32[]{:S(2)}) collective-permute-start(bf16[512,512]{1,0:T(8,128)(2,1)S(1)} %collective-permute-done.5.refs_2_), channel_id=1, source_target_pairs={{0,16},{16,0},{1,17},{17,1},{2,18},{18,2},{3,19},{19,3},{4,20},{20... | collective-permute-start | bytes 1572872 | tf_op jit(solution)/shard_map/ppermute | solution.py:54
  62.0 4.9 %shard_map.89 = (f32[256,512]{1,0:T(8,128)S(1)}, f32[256,512]{1,0:T(8,128)S(1)}, f32[256,512]{1,0:T(8,128)S(1)}, f32[256,512]{1,0:T(8,128)S(1)}, bf16[256,1536]{...) custom-call(s32[8]{0:T(128)S(1)} %stack.49.scalar_ref, ...), custom_call_target="tpu_custom_call" | custom-call | flops 805306368 | bytes 3145728 | tf_op jit(solution)/shard_map/pallas_call | solution.py:229
  67.0 2.2 %collective-permute-done.13.refs_1_ = bf16[512,512]{1,0:T(8,128)(2,1)S(1)} collective-permute-done((bf16[512,512]{1,0:T(8,128)(2,1)}, bf16[512,512]{1,0:T(8,128)(2,1)S(1)}, u32[]{:S(2)}, u32[]{:S(2)}) %collective-permute-start.13) | collective-permute-done | bytes 524320 | tf_op jit(solution)/shard_map/ppermute | solution.py:54
  69.2 2.1 %collective-permute-done.12.refs_0_ = bf16[512,512]{1,0:T(8,128)(2,1)S(1)} collective-permute-done((bf16[512,512]{1,0:T(8,128)(2,1)S(1)}, bf16[512,512]{1,0:T(8,128)(2,1)S(1)}, u32[]{:S(2)}, u32[]{:S(2)}) %collective-permute-start.12) | collective-permute-done | bytes 524320 | tf_op jit(solution)/shard_map/ppermute | solution.py:54
  74.9 4.5 %all-to-all-start = ((bf16[16,8,1024]{2,1,0:T(8,128)(2,1)}), bf16[16,8,1024]{2,1,0:T(8,128)(2,1)S(1)}, u32[]{:S(2)}, u32[]{:S(2)}) async-start(bf16[16,8,1024]{2,1,0:T(8,128)(2,1)} %bitcast.20), calls=%async_computation | async-start | bytes 524288 | tf_op jit(solution)/shard_map/all_to_all | solution.py:593
  79.4 3.5 %shard_map.94.refs_0_ = bf16[256,4096]{1,0:T(8,128)(2,1)} custom-call(s32[1]{0:T(128)} %bitcast.half_ref, f32[256,256]{1,0:T(8,128)S(1)} %fusion.3.mask_ref, f32[256,256]{1,0:T(8,128)S(1)} %copy-done.1, bf16[256,4096]{1,0:T(8,128)(2,1)S(1)} %copy-done, bf16[256,512]{1,0:T(8,128)(2,1)S(1)} %get-tuple-element.52.key_ref.value_ref.mine_ref, ...), custom_call_target="tpu_custom_call" | custom-call | flops 536870912 | bytes 2097152 | tf_op jit(solution)/shard_map/pallas_call | solution.py:387
  82.9 3.4 %shard_map.95 = bf16[256,4096]{1,0:T(8,128)(2,1)} custom-call(s32[1]{0:T(128)} %bitcast.half_ref, f32[256,256]{1,0:T(8,128)S(1)} %fusion.3.mask_ref, f32[256,256]{1,0:T(8,128)S(1)} %copy-done.1, bf16[256,4096]{1,0:T(8,128)(2,1)S(1)} %copy-done, bf16[256,512]{1,0:T(8,128)(2,1)S(1)} %get-tuple-element.51.key_ref.value_ref.other_ref, ...), custom_call_target="tpu_custom_call", output_to_operand_aliasing={{}: (6, {})} | custom-call | flops 536870912 | bytes 2097152 | tf_op jit(solution)/shard_map/pallas_call | solution.py:387
  86.3 3.1 %all-to-all-done = bf16[16,8,1024]{2,1,0:T(8,128)(2,1)S(1)} async-done(((bf16[16,8,1024]{2,1,0:T(8,128)(2,1)}), bf16[16,8,1024]{2,1,0:T(8,128)(2,1)S(1)}, u32[]{:S(2)}, u32[]{:S(2)}) %all-to-all-start) | async-done | bytes 262176 | tf_op jit(solution)/shard_map/all_to_all | solution.py:593
  89.4 1.7 %shard_map.96 = bf16[192,1024]{1,0:T(8,128)(2,1)} custom-call(s32[2]{0:T(128)S(1)} %pad_add_fusion.scalar_ref, f32[256,256]{1,0:T(8,128)S(1)} %copy-done.1, bf16[256,512]{1,0:T(8,128)(2,1)S(1)} %get-tuple-element.52.key_ref.value_ref.mine_ref, bf16[256,512]{1,0:T(8,128)(2,1)S(1)} %get-tuple-element.51.key_ref.value_ref.other_ref, bf16[128,1024]{1,0:T(8,128)(2,1)S(1)} %bitcast.19), custom_call_target="tpu_custom_call" | custom-call | flops 50331648 | bytes 786432 | tf_op jit(solution)/shard_map/pallas_call | solution.py:447
  (67 shorter events, 14.0 us)
Async XLA Ops:
  1.8 8.6 %copy-start.2 = (bf16[512,512]{1,0:T(8,128)(2,1)}, bf16[512,512]{1,0:T(8,128)(2,1)S(1)}, u32[]{:S(2)}) copy-start(bf16[512,512]{1,0:T(8,128)(2,1)S(1)} %pad_maximum_fusion.refs_2_) | copy-start | bytes 1572868
  1.8 16.8 %collective-permute-start.1 = (bf16[512,512]{1,0:T(8,128)(2,1)S(1)}, bf16[512,512]{1,0:T(8,128)(2,1)S(1)}, u32[]{:S(2)}, u32[]{:S(2)}) collective-permute-start(bf16[512,512]{1,0:T(8,128)(2,1)S(1)} %pad_maximum_fusion.refs_2_), channel_id=1, source_target_pairs={{0,8},{1,9},{2,10},{3,11},{4,0},{5,1},{6,2},{7,3},{8,12},{9,13},{1... | collective-permute-start | bytes 1572872 | tf_op jit(solution)/shard_map/ppermute | solution.py:54
  5.9 24.9 %collective-permute-start.6 = (bf16[512,512]{1,0:T(8,128)(2,1)S(1)}, bf16[512,512]{1,0:T(8,128)(2,1)S(1)}, u32[]{:S(2)}, u32[]{:S(2)}) collective-permute-start(bf16[512,512]{1,0:T(8,128)(2,1)S(1)} %pad_maximum_fusion.refs_2_), channel_id=1, source_target_pairs={{0,2},{1,3},{2,0},{3,1},{4,6},{5,7},{6,4},{7,5},{8,10},{9,11},{10,... | collective-permute-start | bytes 1572872 | tf_op jit(solution)/shard_map/ppermute | solution.py:54
  10.3 41.0 %collective-permute-start = (bf16[256,4096]{1,0:T(8,128)(2,1)}, bf16[256,4096]{1,0:T(8,128)(2,1)}, u32[]{:S(2)}, u32[]{:S(2)}) collective-permute-start(bf16[256,4096]{1,0:T(8,128)(2,1)} %shard_map.86), channel_id=1, source_target_pairs={{0,1},{1,0},{2,3},{3,2},{4,5},{5,4},{6,7},{7,6},{8,9},{9,8},{10,11... | collective-permute-start | bytes 6291464 | tf_op jit(solution)/shard_map/ppermute | solution.py:59
  10.4 19.8 %collective-permute-start.2 = (bf16[512,512]{1,0:T(8,128)(2,1)S(1)}, bf16[512,512]{1,0:T(8,128)(2,1)}, u32[]{:S(2)}, u32[]{:S(2)}) collective-permute-start(bf16[512,512]{1,0:T(8,128)(2,1)S(1)} %pad_maximum_fusion.refs_2_), channel_id=1, source_target_pairs={{8,0},{9,1},{10,2},{11,3},{0,4},{1,5},{2,6},{3,7},{12,8},{13,9},{1... | collective-permute-start | bytes 1572872 | tf_op jit(solution)/shard_map/ppermute | solution.py:54
  18.6 32.8 %copy-start.6 = (bf16[512,512]{1,0:T(8,128)(2,1)}, bf16[512,512]{1,0:T(8,128)(2,1)S(1)}, u32[]{:S(2)}) copy-start(bf16[512,512]{1,0:T(8,128)(2,1)S(1)} %collective-permute-done.1.refs_4_) | copy-start | bytes 1572868
  18.6 14.3 %collective-permute-start.4 = (bf16[512,512]{1,0:T(8,128)(2,1)S(1)}, bf16[512,512]{1,0:T(8,128)(2,1)S(1)}, u32[]{:S(2)}, u32[]{:S(2)}) collective-permute-start(bf16[512,512]{1,0:T(8,128)(2,1)S(1)} %collective-permute-done.1.refs_4_), channel_id=1, source_target_pairs={{0,2},{1,3},{2,0},{3,1},{4,6},{5,7},{6,4},{7,5},{8,10},{9,11},{10,... | collective-permute-start | bytes 1572872 | tf_op jit(solution)/shard_map/ppermute | solution.py:54
  19.8 13.4 %collective-permute-start.8 = (bf16[512,512]{1,0:T(8,128)(2,1)S(1)}, bf16[512,512]{1,0:T(8,128)(2,1)}, u32[]{:S(2)}, u32[]{:S(2)}) collective-permute-start(bf16[512,512]{1,0:T(8,128)(2,1)S(1)} %collective-permute-done.1.refs_4_), channel_id=1, source_target_pairs={{0,16},{16,0},{1,17},{17,1},{2,18},{18,2},{3,19},{19,3},{4,20},{20... | collective-permute-start | bytes 1572872 | tf_op jit(solution)/shard_map/ppermute | solution.py:54
  30.2 14.0 %collective-permute-start.3 = (bf16[512,512]{1,0:T(8,128)(2,1)S(1)}, bf16[512,512]{1,0:T(8,128)(2,1)}, u32[]{:S(2)}, u32[]{:S(2)}) collective-permute-start(bf16[512,512]{1,0:T(8,128)(2,1)S(1)} %collective-permute-done.1.refs_4_), channel_id=1, source_target_pairs={{0,8},{1,9},{2,10},{3,11},{4,0},{5,1},{6,2},{7,3},{8,12},{9,13},{1... | collective-permute-start | bytes 1572872 | tf_op jit(solution)/shard_map/ppermute | solution.py:54
  30.8 20.6 %copy-start.7 = (bf16[512,512]{1,0:T(8,128)(2,1)}, bf16[512,512]{1,0:T(8,128)(2,1)S(1)}, u32[]{:S(2)}) copy-start(bf16[512,512]{1,0:T(8,128)(2,1)S(1)} %collective-permute-done.6.refs_3_) | copy-start | bytes 1572868
  30.8 16.1 %collective-permute-start.7 = (bf16[512,512]{1,0:T(8,128)(2,1)}, bf16[512,512]{1,0:T(8,128)(2,1)}, u32[]{:S(2)}, u32[]{:S(2)}) collective-permute-start(bf16[512,512]{1,0:T(8,128)(2,1)} %collective-permute-done.2.refs_6_), channel_id=1, source_target_pairs={{0,2},{1,3},{2,0},{3,1},{4,6},{5,7},{6,4},{7,5},{8,10},{9,11},{10,... | collective-permute-start | bytes 1572872 | tf_op jit(solution)/shard_map/ppermute | solution.py:54
  32.8 11.4 %copy-start.8 = (bf16[512,512]{1,0:T(8,128)(2,1)}, bf16[512,512]{1,0:T(8,128)(2,1)S(1)}, u32[]{:S(2)}) copy-start(bf16[512,512]{1,0:T(8,128)(2,1)S(1)} %collective-permute-done.4.refs_5_) | copy-start | bytes 1572868
  33.1 13.8 %collective-permute-start.9 = (bf16[512,512]{1,0:T(8,128)(2,1)S(1)}, bf16[512,512]{1,0:T(8,128)(2,1)S(1)}, u32[]{:S(2)}, u32[]{:S(2)}) collective-permute-start(bf16[512,512]{1,0:T(8,128)(2,1)S(1)} %collective-permute-done.4.refs_5_), channel_id=1, source_target_pairs={{0,16},{16,0},{1,17},{17,1},{2,18},{18,2},{3,19},{19,3},{4,20},{20... | collective-permute-start | bytes 1572872 | tf_op jit(solution)/shard_map/ppermute | solution.py:54
  44.2 14.5 %collective-permute-start.11 = (bf16[512,512]{1,0:T(8,128)(2,1)}, bf16[512,512]{1,0:T(8,128)(2,1)S(1)}, u32[]{:S(2)}, u32[]{:S(2)}) collective-permute-start(bf16[512,512]{1,0:T(8,128)(2,1)} %collective-permute-done.8.refs_10_), channel_id=1, source_target_pairs={{0,8},{1,9},{2,10},{3,11},{4,0},{5,1},{6,2},{7,3},{8,12},{9,13},{1... | collective-permute-start | bytes 1572872 | tf_op jit(solution)/shard_map/ppermute | solution.py:54
  45.4 15.1 %collective-permute-start.5 = (bf16[512,512]{1,0:T(8,128)(2,1)}, bf16[512,512]{1,0:T(8,128)(2,1)S(1)}, u32[]{:S(2)}, u32[]{:S(2)}) collective-permute-start(bf16[512,512]{1,0:T(8,128)(2,1)} %collective-permute-done.3.refs_8_), channel_id=1, source_target_pairs={{0,2},{1,3},{2,0},{3,1},{4,6},{5,7},{6,4},{7,5},{8,10},{9,11},{10,... | collective-permute-start | bytes 1572872 | tf_op jit(solution)/shard_map/ppermute | solution.py:54
  46.9 13.5 %collective-permute-start.10 = (bf16[512,512]{1,0:T(8,128)(2,1)}, bf16[512,512]{1,0:T(8,128)(2,1)}, u32[]{:S(2)}, u32[]{:S(2)}) collective-permute-start(bf16[512,512]{1,0:T(8,128)(2,1)} %collective-permute-done.7.refs_7_), channel_id=1, source_target_pairs={{0,16},{16,0},{1,17},{17,1},{2,18},{18,2},{3,19},{19,3},{4,20},{20... | collective-permute-start | bytes 1572872 | tf_op jit(solution)/shard_map/ppermute | solution.py:54
  50.4 18.8 %collective-permute-start.13 = (bf16[512,512]{1,0:T(8,128)(2,1)}, bf16[512,512]{1,0:T(8,128)(2,1)S(1)}, u32[]{:S(2)}, u32[]{:S(2)}) collective-permute-start(bf16[512,512]{1,0:T(8,128)(2,1)} %shard_map.87.refs_9_), channel_id=1, source_target_pairs={{0,2},{1,3},{2,0},{3,1},{4,6},{5,7},{6,4},{7,5},{8,10},{9,11},{10,... | collective-permute-start | bytes 1572872 | tf_op jit(solution)/shard_map/ppermute | solution.py:54
  51.4 7.4 %copy-start.3 = (bf16[512,512]{1,0:T(8,128)(2,1)S(1)}, bf16[512,512]{1,0:T(8,128)(2,1)}, u32[]{:S(2)}) copy-start(bf16[512,512]{1,0:T(8,128)(2,1)} %shard_map.87.refs_9_) | copy-start | bytes 1572868
  58.7 12.6 %collective-permute-start.12 = (bf16[512,512]{1,0:T(8,128)(2,1)S(1)}, bf16[512,512]{1,0:T(8,128)(2,1)S(1)}, u32[]{:S(2)}, u32[]{:S(2)}) collective-permute-start(bf16[512,512]{1,0:T(8,128)(2,1)S(1)} %copy-done.3), channel_id=1, source_target_pairs={{8,0},{9,1},{10,2},{11,3},{0,4},{1,5},{2,6},{3,7},{12,8},{13,9},{1... | collective-permute-start | bytes 1572872 | tf_op jit(solution)/shard_map/ppermute | solution.py:54
  60.5 10.9 %collective-permute-start.14 = (bf16[512,512]{1,0:T(8,128)(2,1)S(1)}, bf16[512,512]{1,0:T(8,128)(2,1)S(1)}, u32[]{:S(2)}, u32[]{:S(2)}) collective-permute-start(bf16[512,512]{1,0:T(8,128)(2,1)S(1)} %collective-permute-done.5.refs_2_), channel_id=1, source_target_pairs={{0,16},{16,0},{1,17},{17,1},{2,18},{18,2},{3,19},{19,3},{4,20},{20... | collective-permute-start | bytes 1572872 | tf_op jit(solution)/shard_map/ppermute | solution.py:54
  66.9 5.7 %collective-permute-start.16 = (f32[256,512]{1,0:T(8,128)S(1)}, f32[256,512]{1,0:T(8,128)S(1)}, u32[]{:S(2)}, u32[]{:S(2)}) collective-permute-start(f32[256,512]{1,0:T(8,128)S(1)} %get-tuple-element.49), channel_id=1, source_target_pairs={{0,1},{1,0},{2,3},{3,2},{4,5},{5,4},{6,7},{7,6},{8,9},{9,8},{10,11... | collective-permute-start | bytes 1572872 | tf_op jit(solution)/shard_map/ppermute | solution.py:59
  72.0 2.0 %collective-permute-start.15 = (f32[256,512]{1,0:T(8,128)S(1)}, f32[256,512]{1,0:T(8,128)S(1)}, u32[]{:S(2)}, u32[]{:S(2)}) collective-permute-start(f32[256,512]{1,0:T(8,128)S(1)} %shard_map.91), channel_id=1, source_target_pairs={{0,1},{1,0},{2,3},{3,2},{4,5},{5,4},{6,7},{7,6},{8,9},{9,8},{10,11... | collective-permute-start | bytes 1572872 | tf_op jit(solution)/shard_map/ppermute | solution.py:59
  72.6 6.8 %copy-start = (bf16[256,4096]{1,0:T(8,128)(2,1)S(1)}, bf16[256,4096]{1,0:T(8,128)(2,1)}, u32[]{:S(2)}) copy-start(bf16[256,4096]{1,0:T(8,128)(2,1)} %query_ref.3) | copy-start | bytes 6291460
  74.9 14.5 %all-to-all-start = ((bf16[16,8,1024]{2,1,0:T(8,128)(2,1)}), bf16[16,8,1024]{2,1,0:T(8,128)(2,1)S(1)}, u32[]{:S(2)}, u32[]{:S(2)}) async-start(bf16[16,8,1024]{2,1,0:T(8,128)(2,1)} %bitcast.20), calls=%async_computation | async-start | bytes 524288 | tf_op jit(solution)/shard_map/all_to_all | solution.py:593
  (6 other events, 24.5 us)
